TPU v7x, 256 devices: a whole 4x4x8 slice. The times are simulated.
256 devices in a mesh: blk: 64 (over x, z, core), smp: 4 (over y).
Axes of the slice: x: 4, y: 4, z: 8, core: 2. Of those that a mesh axis runs over, the one named last changes fastest.
Arguments:
- encodings: bfloat16 [1024, 57344], P('smp', 'blk'), may hold values from -1 to 1
- hidden_pre: bfloat16 [1024, 8192], P('smp', 'blk'), may hold values from -6 to 6
- cotangent: bfloat16 [1024, 688128], P('smp', 'blk'), may hold values from -0.75 to 0.75
- out_weights: bfloat16 [10752, 128, 128], P('blk'), may hold values from -0.0390625 to 0.0390625
- out_contacts: int32 [5376, 2], P('blk'), may hold values from 0 to 63, all different within a row
- in_contacts: int32 [448, 4], P('blk'), may hold values from 0 to 63, all different within a row
Outputs:
- out_weight_grad: bfloat16 [10752, 128, 128], P(('blk', 'smp'))
- in_weight_grad: bfloat16 [1792, 128, 128], P(('blk', 'smp'))
Inputs may be any that keep to these rules, and one draw needn't show every extreme that they name: `out_contacts`: each row names 2 different hidden blocks, and every hidden block is named by some row. `in_contacts`: each row names 4 different hidden blocks, and every hidden block is named by some row.
All inputs are finite; a program needn't handle non-finite values.
Results may differ from a plain program's by a relative error of at most 0.0051.
Values may be sent and summed in bfloat16 or wider, within the bound.
No kernel may reach another device: no remote copies, remote signals or barrier semaphores. Data moves between devices by JAX's collectives and lax.ppermute only.
A program may use at most 128 MiB of HBM per device.

v0:
```python
import jax
import jax.numpy as jnp
from jax import lax
from jax.sharding import PartitionSpec as P


def silu_slope(values):
    sigma = jax.nn.sigmoid(values)
    return sigma * (1.0 + values * (1.0 - sigma))


def per_device(encodings, hidden_pre, cotangent, out_weights, out_contacts, in_contacts):
    sample_rows = cotangent.shape[0]
    block_size = out_weights.shape[1]
    out_local, per_out = out_contacts.shape
    in_local, per_in = in_contacts.shape
    pre_whole = lax.all_gather(hidden_pre, "blk", axis=1, tiled=True)
    hid_count = pre_whole.shape[1] // block_size
    pre_blocks = pre_whole.reshape(sample_rows, hid_count, block_size)
    activation = jax.nn.silu(pre_blocks.astype(jnp.float32)).astype(jnp.bfloat16)
    out_index = out_contacts.reshape(-1)
    in_index = in_contacts.reshape(-1)
    activ_taken = jnp.take(activation, out_index, axis=1).reshape(
        sample_rows, out_local, per_out, block_size
    )
    cot_blocks = cotangent.reshape(sample_rows, out_local, block_size)
    out_terms = jnp.einsum(
        "sokb,soc->okbc", activ_taken, cot_blocks, preferred_element_type=jnp.float32
    )
    out_terms = out_terms.reshape(out_local * per_out, block_size, block_size)
    out_grad = lax.psum_scatter(out_terms, "smp", scatter_dimension=0, tiled=True).astype(
        jnp.bfloat16
    )
    weight_view = out_weights.reshape(out_local, per_out, block_size, block_size)
    partial_terms = jnp.einsum(
        "soc,okbc->oksb", cot_blocks, weight_view, preferred_element_type=jnp.float32
    )
    partial_terms = partial_terms.reshape(out_local * per_out, sample_rows, block_size)
    hidden_terms = jax.ops.segment_sum(partial_terms, out_index, num_segments=hid_count)
    summed = lax.psum(hidden_terms, "blk")
    summed_taken = jnp.swapaxes(jnp.take(summed, in_index, axis=0), 0, 1)
    pre_taken = jnp.take(pre_blocks, in_index, axis=1).astype(jnp.float32)
    grad_taken = (summed_taken * silu_slope(pre_taken)).astype(jnp.bfloat16)
    grad_view = grad_taken.reshape(sample_rows, in_local, per_in, block_size)
    enc_blocks = encodings.reshape(sample_rows, in_local, block_size)
    in_terms = jnp.einsum(
        "sib,sikc->ikbc", enc_blocks, grad_view, preferred_element_type=jnp.float32
    )
    in_terms = in_terms.reshape(in_local * per_in, block_size, block_size)
    in_grad = lax.psum_scatter(in_terms, "smp", scatter_dimension=0, tiled=True).astype(
        jnp.bfloat16
    )
    return (out_grad, in_grad)


def solution(mesh):
    in_specs = (
        P("smp", "blk"),
        P("smp", "blk"),
        P("smp", "blk"),
        P("blk", None, None),
        P("blk", None),
        P("blk", None),
    )
    out_specs = (P(("blk", "smp"), None, None), P(("blk", "smp"), None, None))
    return jax.shard_map(
        per_device, mesh=mesh, in_specs=in_specs, out_specs=out_specs, check_vma=False
    )
```

profile of v0, /device:TPU:1, one launch (start us, length us, event | category | flops | bytes accessed | tf_op | source)
XLA Modules:
  0.0 569.9 jit_solution(5942079644765487091)
XLA Ops:
  7.2 8.3 %copy.36 = bf16[256,10752]{0,1:T(8,128)(2,1)} copy(bf16[256,10752]{1,0:T(8,128)(2,1)} %param.8) | data formatting | bytes 11010048 | tf_op args[2]
  15.5 14.6 %fusion.17 = f32[84,2,128,256]{3,2,1,0:T(8,128)} fusion(bf16[84,2,128,128]{3,2,1,0:T(8,128)(2,1)} %bitcast.57, bf16[256,84,128,1]{0,2,3,1:T(8,128)(2,1)} %bitcast.55), kind=kOutput, calls=%fused_computation.33 | convolution fusion | flops 1409286144 | bytes 33030144 | tf_op jit(solution)/shard_map/soc,okbc->oksb/dot_general | solution.py:35
  30.1 21.6 %copy.41 = f32[168,256,128]{2,1,0:T(8,128)} copy(f32[168,256,128]{1,2,0:T(8,128)} %bitcast.53) | data formatting | bytes 44040192 | tf_op jit(solution)/shard_map/reshape | solution.py:38
  51.7 0.1 copy.34
  51.8 0.1 reshape.144
  52.0 4.4 broadcast_in_dim.36
  56.3 52.2 %scatter_fusion = f32[64,256,128]{2,1,0:T(8,128)} fusion(f32[64,256,128]{2,1,0:T(8,128)} %broadcast_in_dim.36, s32[168]{0:T(256)S(1)} %reshape.144, f32[168,256,128]{2,1,0:T(8,128)} %copy.41), kind=kCustom, calls=%fused_computation.3 | custom fusion | flops 5505024 | bytes 66060960 | tf_op jit(solution)/shard_map/scatter-add | solution.py:39
  108.6 0.8 copy-done.1
  109.3 0.7 copy.32
  110.1 0.0 reduce-scatter.5.cloned.1.call-start
  110.2 0.1 copy.38
  110.3 0.1 reshape.114
  110.3 0.1 reshape.111
  110.4 0.2 copy.44
  110.7 205.7 %all-reduce.2.cloned.1.call-done = f32[64,256,128]{2,1,0:T(8,128)} async-done(((f32[64,256,128]{2,1,0:T(8,128)}), f32[64,256,128]{2,1,0:T(8,128)}) %all-reduce.2.cloned.1.call-update) | async-done | bytes 8388624 | tf_op jit(solution)/shard_map/psum | solution.py:40
  316.4 5.9 %gather_fusion.1 = f32[28,256,128]{2,1,0:T(8,128)} fusion(f32[64,256,128]{2,1,0:T(8,128)} %all-reduce.2.cloned.1.call-done, s32[1024]{0:T(1024)S(1)} %pad_clamp_fusion), kind=kCustom, calls=%fused_computation.1 | custom fusion | bytes 7340144 | tf_op jit(solution)/shard_map/jit(_take)/gather | solution.py:41
  322.3 77.4 %all-gather.2.cloned.1.call-done = bf16[256,8192]{0,1:T(8,128)(2,1)} async-done(((bf16[256,128]{0,1:T(8,128)(2,1)}), bf16[256,8192]{0,1:T(8,128)(2,1)}) %all-gather.2.cloned.1.call-update) | async-done | bytes 4194320 | tf_op jit(solution)/shard_map/all_gather | solution.py:17
  399.7 6.4 %copy.33 = bf16[256,64,128]{2,0,1:T(8,128)(2,1)} copy(bf16[256,64,128]{0,2,1:T(8,128)(2,1)} %bitcast.61) | data formatting | bytes 8388608 | tf_op jit(solution)/shard_map/reshape | solution.py:19
  406.1 3.1 gather_fusion.2
  409.2 3.8 fusion.14
  413.0 0.8 fusion.18
  413.7 1.7 copy.47
  415.5 0.2 reduce-scatter.3.cloned.1.call-start
  415.7 0.1 reshape.108
  415.9 0.1 copy.31
  416.0 5.1 fusion.6
  421.1 10.0 %gather_fusion = bf16[168,256,128]{2,1,0:T(8,128)(2,1)} fusion(bf16[256,64,128]{2,0,1:T(8,128)(2,1)} %fusion.6, s32[1024]{0:T(1024)S(1)} %pad_clamp_fusion.1), kind=kCustom, calls=%fused_computation | custom fusion | bytes 22020768 | tf_op jit(solution)/shard_map/jit(_take)/gather | solution.py:23
  431.1 14.7 %copy.35 = bf16[256,84,2,128]{0,3,2,1:T(8,128)(2,1)} copy(bf16[256,84,2,128]{3,0,2,1:T(8,128)(2,1)} %bitcast.54) | data formatting | bytes 22020096 | tf_op jit(solution)/shard_map/jit(_take)/gather | solution.py:23
  445.8 13.0 %fusion = f32[84,2,128,128]{3,2,1,0:T(8,128)} fusion(bf16[256,84,128,1]{0,2,3,1:T(8,128)(2,1)} %bitcast.56, bf16[256,84,2,128]{0,3,2,1:T(8,128)(2,1)} %copy.35, pred[84,2]{1,0:T(8,128)(4,1)S(1)} %copy.31), kind=kOutput, calls=%fused_computation.4 | convolution fusion | flops 1414791168 | bytes 27525288 | tf_op jit(solution)/shard_map/sokb,soc->okbc/dot_general | solution.py:27
  458.9 1.7 convert_element_type.23
  460.6 99.6 %reduce-scatter.3.cloned.1.call-done = f32[42,128,128]{2,1,0:T(8,128)} async-done(((f32[168,128,128]{2,1,0:T(8,128)}), f32[42,128,128]{2,1,0:T(8,128)}) %reduce-scatter.3.cloned.1.call-update) | async-done | bytes 2752528 | tf_op jit(solution)/shard_map/reduce_scatter | solution.py:31
  560.2 3.1 convert_element_type.20
  (20 shorter events, 0.2 us)
Async XLA Ops:
  7.2 309.2 %all-reduce.2.cloned.1.call-start = ((), (), s32[]{:S(2)}) async-start(), calls=%async_computation.4 | async-start | bytes 16777216 | tf_op jit(solution)/shard_map/psum | solution.py:40
  30.1 21.7 %copy-start.3 = (s32[84,2]{0,1:T(2,128)S(1)}, s32[84,2]{0,1:T(2,128)}, u32[]{:S(2)}) copy-start(s32[84,2]{0,1:T(2,128)} %param.10) | copy-start | bytes 2020
  108.5 0.8 copy-start.1
  108.5 1.7 copy-start.2
  108.5 1.9 copy-start
  108.5 291.2 %all-gather.2.cloned.1.call-start = ((), (), s32[]{:S(2)}) async-start(), calls=%async_computation.2 | async-start | bytes 4259840 | tf_op jit(solution)/shard_map/all_gather | solution.py:17
  110.1 348.8 %reduce-scatter.5.cloned.1.call-start = ((), (), s32[]{:S(2)}) async-start(), calls=%async_computation.5 | async-start | bytes 2293760 | tf_op jit(solution)/shard_map/reduce_scatter | solution.py:50
  415.5 144.8 %reduce-scatter.3.cloned.1.call-start = ((), (), s32[]{:S(2)}) async-start(), calls=%async_computation.3 | async-start | bytes 13762560 | tf_op jit(solution)/shard_map/reduce_scatter | solution.py:31
Sparse Core Ops, SparseCore 0:
  108.7 207.6 all-reduce.1
  320.1 79.5 all-gather.1
  415.6 27.0 reduce-scatter.4
  459.0 101.2 reduce-scatter.2
where the time goes:
time: 571 us; the launch traced here: 570 us
  waiting for transfers between devices  383 us (67%)
  local copies, waits for them, and re-layouts  78.6 us (14%)
  other arithmetic  65.9 us (12%)
  matrix products  28.4 us (5%)
  between operations  13.9 us (2%)
    psum x1, waiting for transfers between devices, per_device(): summed = lax.psum(hidden_terms, 'blk')  206 us
    reduce_scatter x1, waiting for transfers between devices, per_device(): lax.psum_scatter(out_terms, 'smp', scatter_dimension=0, tiled=True)  99.6 us
    all_gather x1, waiting for transfers between devices, per_device(): pre_whole = lax.all_gather(hidden_pre, 'blk', axis=1, tiled=True)  77.4 us
    scatter-add x1, other arithmetic, per_device(): jax.ops.segment_sum(partial_terms, out_index, num_segments=hid_count)  52.2 us
    gather x2, local copies, waits for them, and re-layouts, per_device(): jnp.take(activation, out_index, axis=1)  24.7 us
    reshape x1, local copies, waits for them, and re-layouts, per_device(): partial_terms.reshape(out_local * per_out, sample_rows, block_size)  21.6 us
    dot_general x1, matrix products, per_device(): jnp.einsum('soc,okbc->oksb', cot_blocks, weight_view, preferred_element_t...  14.6 us
    dot_general x1, matrix products, per_device(): jnp.einsum('sokb,soc->okbc', activ_taken, cot_blocks, preferred_element_t...  13 us
  transfers between devices with their start and end apart: 4, of which 3 were waited for; matrix products, arithmetic and copies ran while one was open for 9% of the time, Pallas kernels for 0%

commit v1 on v0

v1 whole, which is shorter than its diff:
```python
import jax
import jax.numpy as jnp
from jax import lax
from jax.experimental import pallas as pl
from jax.experimental.pallas import tpu as pltpu
from jax.sharding import PartitionSpec as P

BF16 = jnp.bfloat16
F32 = jnp.float32
NX, NZ, NC, NY = 4, 8, 2, 4
BS = 128
STEP_BLOCKS = 7
VMEM = 56 * 2**20


def index_of(x, z, core):
    return ((x % NX) * NZ + z % NZ) * NC + core % NC


def moved(value, dx=0, dz=0, dc=0):
    pairs = [
        (index_of(x, z, c), index_of(x + dx, z + dz, c + dc))
        for x in range(NX)
        for z in range(NZ)
        for c in range(NC)
    ]
    return lax.ppermute(value, "blk", pairs)


def moved_smp(value, dy):
    return lax.ppermute(value, "smp", [(i, (i + dy) % NY) for i in range(NY)])


def params(**more):
    return pltpu.CompilerParams(vmem_limit_bytes=VMEM, **more)


def contract(lhs, rhs, over):
    return lax.dot_general(lhs, rhs, ((over[:1], over[1:]), ((), ())), preferred_element_type=F32)


def after(value, other):
    anywhere = pl.BlockSpec(memory_space=pl.ANY)
    return pl.pallas_call(
        lambda *refs: None,
        in_specs=[anywhere, anywhere],
        out_specs=anywhere,
        out_shape=jax.ShapeDtypeStruct(value.shape, value.dtype),
        input_output_aliases={0: 0},
        name="after",
    )(value, other)


def hidden_kernel(place, contacts, cot_ref, weight_ref, send_ref, keep_ref, total):
    step = pl.program_id(0)
    core = place[2]

    @pl.when(step == 0)
    def _():
        total[...] = jnp.zeros_like(total)

    for o in range(STEP_BLOCKS):
        cot = cot_ref[:, o * BS : (o + 1) * BS]
        weights = weight_ref[2 * o : 2 * o + 2].reshape(2 * BS, BS)
        terms = contract(cot, weights, (1, 1))
        for m in range(2):
            k = contacts[m, step * STEP_BLOCKS + o]
            total[k] += terms[:, m * BS : (m + 1) * BS]

    @pl.when(step == pl.num_programs(0) - 1)
    def _():
        def write(p, carry):
            send_ref[p] = total[2 * p + 1 - core].astype(BF16)
            keep_ref[p] = total[2 * p + core]
            return carry

        lax.fori_loop(0, NX * NZ, write, 0)


def hidden_sums(place, contacts, cotangent, weights):
    rows = cotangent.shape[0]
    count = NX * NZ
    steps = weights.shape[0] // (2 * STEP_BLOCKS)
    return pl.pallas_call(
        hidden_kernel,
        grid_spec=pltpu.PrefetchScalarGridSpec(
            num_scalar_prefetch=2,
            grid=(steps,),
            in_specs=[
                pl.BlockSpec((rows, STEP_BLOCKS * BS), lambda g, *_: (0, g)),
                pl.BlockSpec((2 * STEP_BLOCKS, BS, BS), lambda g, *_: (g, 0, 0)),
            ],
            out_specs=[
                pl.BlockSpec((count, rows, BS), lambda g, *_: (0, 0, 0)),
                pl.BlockSpec((count, rows, BS), lambda g, *_: (0, 0, 0)),
            ],
            scratch_shapes=[pltpu.VMEM((2 * count, rows, BS), F32)],
        ),
        out_shape=[
            jax.ShapeDtypeStruct((count, rows, BS), BF16),
            jax.ShapeDtypeStruct((count, rows, BS), F32),
        ],
        compiler_params=params(),
        cost_estimate=pl.CostEstimate(flops=3 * 10**9, bytes_accessed=2**24, transcendentals=0),
        name="hidden_sums",
    )(place, contacts, cotangent, weights)


def core_kernel(place, keep_ref, got_ref, *outs):
    x = place[0]
    for d in range(NX):
        at = (x + d) & (NX - 1)
        outs[d][0] = (keep_ref[at, 0] + got_ref[at, 0].astype(F32)).astype(outs[d].dtype)


def core_sums(place, keep, got):
    rows = keep.shape[1]
    spec = pl.BlockSpec((NX, 1, rows, BS), lambda g, *_: (0, g, 0, 0))
    return pl.pallas_call(
        core_kernel,
        grid_spec=pltpu.PrefetchScalarGridSpec(
            num_scalar_prefetch=1,
            grid=(NZ,),
            in_specs=[spec, spec],
            out_specs=[pl.BlockSpec((1, rows, BS), lambda g, *_: (g, 0, 0))] * NX,
        ),
        out_shape=[
            jax.ShapeDtypeStruct((NZ, rows, BS), BF16 if d else F32) for d in range(NX)
        ],
        compiler_params=params(),
        cost_estimate=pl.CostEstimate(flops=10**6, bytes_accessed=2**23, transcendentals=0),
        name="core_sums",
    )(place, keep.reshape(NX, NZ, rows, BS), got.reshape(NX, NZ, rows, BS))


def line_kernel(place, keep_ref, a_ref, b_ref, c_ref, *outs):
    z = place[1]
    for d in range(NZ):
        at = (z + d) & (NZ - 1)
        total = keep_ref[at] + a_ref[at].astype(F32) + b_ref[at].astype(F32) + c_ref[at].astype(F32)
        outs[d][...] = total.astype(outs[d].dtype)


def line_sums(place, keep, *got):
    rows = keep.shape[1]
    whole = pl.BlockSpec(memory_space=pltpu.VMEM)
    return pl.pallas_call(
        line_kernel,
        in_specs=[pl.BlockSpec(memory_space=pltpu.SMEM)] + [whole] * NX,
        out_specs=[whole] * NZ,
        out_shape=[jax.ShapeDtypeStruct((rows, BS), BF16 if d else F32) for d in range(NZ)],
        compiler_params=params(),
        cost_estimate=pl.CostEstimate(flops=10**6, bytes_accessed=2**22, transcendentals=0),
        name="line_sums",
    )(place, keep, *got)


def out_kernel(place, contacts, cot_ref, own_ref, other_ref, out_ref, held, sems):
    step = pl.program_id(0)
    x, core = place[0], place[2]

    @pl.when(step == 0)
    def _():
        copies = [
            pltpu.make_async_copy(own_ref, held.at[core], sems.at[0]),
            pltpu.make_async_copy(other_ref, held.at[1 - core], sems.at[1]),
        ]
        for copy in copies:
            copy.start()
        for copy in copies:
            copy.wait()

    for o in range(STEP_BLOCKS):
        cot = cot_ref[:, o * BS : (o + 1) * BS]
        for m in range(2):
            k = contacts[m, step * STEP_BLOCKS + o]
            slot = ((k >> 1) & (NZ - 1)) * NX + ((x - (k >> 4)) & (NX - 1))
            out_ref[2 * o + m] = contract(held[k & 1, slot], cot, (1, 0)).astype(BF16)


def out_terms(place, contacts, cotangent, own, other):
    rows = cotangent.shape[0]
    count = contacts.shape[1]
    return pl.pallas_call(
        out_kernel,
        grid_spec=pltpu.PrefetchScalarGridSpec(
            num_scalar_prefetch=2,
            grid=(count // STEP_BLOCKS,),
            in_specs=[
                pl.BlockSpec((rows, STEP_BLOCKS * BS), lambda g, *_: (0, g)),
                pl.BlockSpec(memory_space=pl.ANY),
                pl.BlockSpec(memory_space=pl.ANY),
            ],
            out_specs=pl.BlockSpec((2 * STEP_BLOCKS, BS, BS), lambda g, *_: (g, 0, 0)),
            scratch_shapes=[
                pltpu.VMEM((NC, NX * NZ, BS, rows), BF16),
                pltpu.SemaphoreType.DMA((2,)),
            ],
        ),
        out_shape=jax.ShapeDtypeStruct((2 * count, BS, BS), BF16),
        compiler_params=params(),
        cost_estimate=pl.CostEstimate(flops=3 * 10**9, bytes_accessed=2**24, transcendentals=0),
        name="out_terms",
    )(place, contacts, cotangent, own, other)


def in_kernel(place, contacts, enc_ref, *refs):
    parts, outs, (held, made, sems) = refs[: NC * NX], refs[NC * NX : NC * NX + NY], refs[NC * NX + NY :]
    x, z, core, y = place[0], place[1], place[2], place[3]
    copies = [
        pltpu.make_async_copy(part, held.at[n], sems.at[n]) for n, part in enumerate(parts)
    ]
    for copy in copies:
        copy.start()
    for copy in copies:
        copy.wait()
    per_in, count = contacts.shape
    for i in range(count):
        turned = enc_ref[:, i * BS : (i + 1) * BS].T
        for m in range(per_in):
            k = contacts[m, i]
            slot = ((k & 1) ^ core) * NX + ((x - (k >> 4)) & (NX - 1))
            value = held[slot, (z - (k >> 1)) & (NZ - 1)]
            made[i * per_in + m] = contract(turned, value, (1, 0))
    each = count * per_in // NY
    for d in range(NY):
        first = ((y + d) & (NY - 1)) * each
        for n in range(each):
            outs[d][n] = made[first + n].astype(outs[d].dtype)


def in_terms(place, contacts, encodings, parts):
    rows = encodings.shape[0]
    per_in, count = contacts.shape
    each = per_in * count // NY
    smem = pl.BlockSpec(memory_space=pltpu.SMEM)
    whole = pl.BlockSpec(memory_space=pltpu.VMEM)
    return pl.pallas_call(
        in_kernel,
        in_specs=[smem, smem, whole] + [pl.BlockSpec(memory_space=pl.ANY)] * (NC * NX),
        out_specs=[whole] * NY,
        scratch_shapes=[
            pltpu.VMEM((NC * NX, NZ, rows, BS), BF16),
            pltpu.VMEM((per_in * count, BS, BS), F32),
            pltpu.SemaphoreType.DMA((NC * NX,)),
        ],
        out_shape=[jax.ShapeDtypeStruct((each, BS, BS), BF16 if d else F32) for d in range(NY)],
        compiler_params=params(),
        cost_estimate=pl.CostEstimate(flops=5 * 10**8, bytes_accessed=2**23, transcendentals=0),
        name="in_terms",
    )(place, contacts, encodings, *parts)


def silu_slope(values):
    sigma = jax.nn.sigmoid(values)
    return sigma * (1.0 + values * (1.0 - sigma))


def per_device(encodings, hidden_pre, cotangent, out_weights, out_contacts, in_contacts):
    position = lax.axis_index("blk")
    place = jnp.stack(
        [position // (NZ * NC), position // NC % NZ, position % NC, lax.axis_index("smp")]
    ).astype(jnp.int32)
    out_index, in_index = out_contacts.T, in_contacts.T
    pre = hidden_pre.astype(F32)

    activation = jax.nn.silu(pre).astype(BF16).T
    along_x = jnp.stack([activation] + [moved(activation, dx=d) for d in range(1, NX)])
    lines = [[index_of(x, z, c) for z in range(NZ)] for x in range(NX) for c in range(NC)]
    act_own = lax.all_gather(along_x, "blk", axis_index_groups=lines)
    act_own = act_own.reshape(NZ * NX, BS, -1)

    send, keep = hidden_sums(place, out_index, cotangent, out_weights)

    by_x = core_sums(place, keep, moved(send, dc=1))
    by_z = line_sums(place, by_x[0], *[moved(by_x[d], dx=d) for d in range(1, NX)])
    act_own = after(act_own, by_z[0])
    got = [moved(by_z[d], dz=d) for d in range(1, NZ)]
    grad_act = sum((g.astype(F32) for g in got), by_z[0])
    grad_pre = (grad_act * silu_slope(pre)).astype(BF16)

    along_z = jnp.stack([grad_pre] + [moved(grad_pre, dz=d) for d in range(1, NZ)])
    own = [along_z] + [moved(along_z, dx=d) for d in range(1, NX)]
    parts = own + [moved(part, dc=1) for part in own]

    terms = out_terms(place, out_index, cotangent, act_own, moved(act_own, dc=1))
    out_grad = lax.psum_scatter(terms, "smp", scatter_dimension=0, tiled=True)

    mine, *away = in_terms(place, in_index, encodings, parts)
    in_grad = sum((moved_smp(a, d + 1).astype(F32) for d, a in enumerate(away)), mine)
    return (out_grad, in_grad.astype(BF16))


def solution(mesh):
    in_specs = (
        P("smp", "blk"),
        P("smp", "blk"),
        P("smp", "blk"),
        P("blk", None, None),
        P("blk", None),
        P("blk", None),
    )
    out_specs = (P(("blk", "smp"), None, None), P(("blk", "smp"), None, None))
    return jax.shard_map(
        per_device, mesh=mesh, in_specs=in_specs, out_specs=out_specs, check_vma=False
    )
```

time: 571 us -> 201 us (0.35)
  waiting for transfers between devices: 383 us -> 69.1 us
  local copies, waits for them, and re-layouts: 78.6 us -> 6.2 us
  other arithmetic: 65.9 us -> 3.5 us
  starting transfers between devices: 0.34 us -> 62.6 us
  Pallas kernels: 0 us -> 43.7 us
  matrix products: 28.4 us -> 0 us
    psum x1 -> x0, waiting for transfers between devices: 206 us -> none  [per_device(): summed = lax.psum(hidden_terms, 'blk')]
    reduce_scatter x2 -> x1, waiting for transfers between devices: 99.7 us -> 0.01 us  [per_device(): out_grad = lax.psum_scatter(terms, 'smp', scatter_dimension=0, tiled=True)]
    all_gather x1, waiting for transfers between devices: 77.4 us -> 0.01 us  [per_device(): act_own = lax.all_gather(along_x, 'blk', axis_index_groups=lines)]
    ppermute x0 -> x32, waiting for transfers between devices: none -> 69.1 us  [the longest x29 59.6 us: moved(): return lax.ppermute(value, 'blk', pairs)]
    ppermute x0 -> x32, starting transfers between devices: none -> 62.6 us  [the longest x29 57.5 us: moved(): return lax.ppermute(value, 'blk', pairs)]
    scatter-add x1 -> x0, other arithmetic: 52.2 us -> none  [per_device(): jax.ops.segment_sum(partial_terms, out_index, num_segments=hid_count)]
    pallas_call x0 -> x6, Pallas kernels: none -> 43.7 us  [the longest x1 15.1 us: hidden_sums(): pl.pallas_call(hidden_kernel, grid_spec=pltpu.PrefetchScalarGridSpec(num_...]
    gather x4 -> x0, local copies, waits for them, and re-layouts: 33.7 us -> none  [the longest x2 24.7 us: per_device(): jnp.take(activation, out_index, axis=1)]
  transfers between devices with their start and end apart: 4 -> 34, of which waited for: 3 -> 18; matrix products, arithmetic and copies ran while one was open for 9% -> 1% of each run, Pallas kernels for 0% -> 15%
where the time goes in v1:
time: 201 us; the launch traced here: 200 us
  waiting for transfers between devices  69.1 us (34%)
  starting transfers between devices  62.6 us (31%)
  Pallas kernels  43.7 us (22%)
  between operations  14.3 us (7%)
  local copies, waits for them, and re-layouts  6.2 us (3%)
  other arithmetic  3.5 us (2%)
    ppermute x29, waiting for transfers between devices, moved(): return lax.ppermute(value, 'blk', pairs)  59.6 us
    ppermute x29, starting transfers between devices, moved(): return lax.ppermute(value, 'blk', pairs)  57.5 us
    pallas_call x1, Pallas kernels, hidden_sums(): pl.pallas_call(hidden_kernel, grid_spec=pltpu.PrefetchScalarGridSpec(num_...  15.1 us
    pallas_call x1, Pallas kernels, out_terms(): pl.pallas_call(out_kernel, grid_spec=pltpu.PrefetchScalarGridSpec(num_sca...  13.9 us
    ppermute x3, waiting for transfers between devices, moved_smp(): return lax.ppermute(value, 'smp', [(i, (i + dy) % NY) for i in range(NY)])  9.5 us
    pallas_call x1, Pallas kernels, core_sums(): pl.pallas_call(core_kernel, grid_spec=pltpu.PrefetchScalarGridSpec(num_sc...  7.26 us
    unnamed x50, local copies, waits for them, and re-layouts  5.33 us
    ppermute x3, starting transfers between devices, moved_smp(): return lax.ppermute(value, 'smp', [(i, (i + dy) % NY) for i in range(NY)])  5.06 us
  transfers between devices with their start and end apart: 34, of which 18 were waited for; matrix products, arithmetic and copies ran while one was open for 1% of the time, Pallas kernels for 15%

profile of v1, /device:TPU:1, one launch (start us, length us, event | category | flops | bytes accessed | tf_op | source)
XLA Modules:
  0.0 199.6 jit_solution(7217295075558889001)
XLA Ops:
  8.1 2.1 %collective-permute-start = (bf16[128,256]{0,1:T(8,128)(2,1)S(1)}, bf16[128,256]{0,1:T(8,128)(2,1)S(1)}, u32[]{:S(2)}, u32[]{:S(2)}) collective-permute-start(bf16[128,256]{0,1:T(8,128)(2,1)S(1)} %get-tuple-element.41), channel_id=1, source_target_pairs={{0,64},{4,68},{8,72},{12,76},{16,80},{20,84},{24,88},{28,92},{32,9... | collective-permute-start | bytes 196616 | tf_op jit(solution)/shard_map/ppermute | solution.py:27
  10.2 2.5 %collective-permute-start.1 = (bf16[128,256]{0,1:T(8,128)(2,1)S(1)}, bf16[128,256]{0,1:T(8,128)(2,1)S(1)}, u32[]{:S(2)}, u32[]{:S(2)}) collective-permute-start(bf16[128,256]{0,1:T(8,128)(2,1)S(1)} %get-tuple-element.41), channel_id=1, source_target_pairs={{0,128},{4,132},{8,136},{12,140},{16,144},{20,148},{24,152},{28,15... | collective-permute-start | bytes 196616 | tf_op jit(solution)/shard_map/ppermute | solution.py:27
  17.7 15.1 %hidden_sums.1 = (bf16[32,256,128]{2,1,0:T(8,128)(2,1)}, f32[32,256,128]{2,1,0:T(8,128)}) custom-call(s32[4]{0:T(128)} %pad_add_fusion.place, s32[2,84]{1,0:T(2,128)} %bitcast.38, bf16[256,10752]{1,0:T(8,128)(2,1)} %cot_ref.3, bf16[168,128,128]{2,1,0:T(8,128)(2,1)} %weight_ref.1), custom_call_target="tpu_custom_call" | custom-call | flops 3000000000 | bytes 16777216 | tf_op jit(solution)/shard_map/hidden_sums/pallas_call | solution.py:84
  32.8 2.4 %collective-permute-start.3 = (bf16[32,256,128]{2,1,0:T(8,128)(2,1)}, bf16[32,256,128]{2,1,0:T(8,128)(2,1)S(1)}, u32[]{:S(2)}, u32[]{:S(2)}) collective-permute-start(bf16[32,256,128]{2,1,0:T(8,128)(2,1)} %get-tuple-element.21), channel_id=1, source_target_pairs={{0,4},{4,0},{8,12},{12,8},{16,20},{20,16},{24,28},{28,24},{32,36},... | collective-permute-start | bytes 6291464 | tf_op jit(solution)/shard_map/ppermute | solution.py:27
  35.2 4.0 %collective-permute-done.3 = bf16[32,256,128]{2,1,0:T(8,128)(2,1)S(1)} collective-permute-done((bf16[32,256,128]{2,1,0:T(8,128)(2,1)}, bf16[32,256,128]{2,1,0:T(8,128)(2,1)S(1)}, u32[]{:S(2)}, u32[]{:S(2)}) %collective-permute-start.3) | collective-permute-done | bytes 2097184 | tf_op jit(solution)/shard_map/ppermute | solution.py:27
  40.5 7.3 %core_sums.1 = (f32[8,256,128]{2,1,0:T(8,128)}, bf16[8,256,128]{2,1,0:T(8,128)(2,1)}, bf16[8,256,128]{2,1,0:T(8,128)(2,1)}, bf16[8,256,128]{2,1,0:T(8,128)(2,1)}) custom-call(s32[4]{0:T(128)} %pad_add_fusion.place, f32[4,8,256,128]{3,2,1,0:T(8,128)} %bitcast.32, bf16[4,8,256,128]{3,2,1,0:T(8,128)(2,1)} %bitcast.33), custom_call_target="tpu_custom_call" | custom-call | flops 1000000 | bytes 8388608 | tf_op jit(solution)/shard_map/core_sums/pallas_call | solution.py:119
  48.9 2.5 %collective-permute-start.5 = (bf16[8,256,128]{2,1,0:T(8,128)(2,1)}, bf16[8,256,128]{2,1,0:T(8,128)(2,1)S(1)}, u32[]{:S(2)}, u32[]{:S(2)}) collective-permute-start(bf16[8,256,128]{2,1,0:T(8,128)(2,1)} %get-tuple-element.24), channel_id=1, source_target_pairs={{0,128},{4,132},{8,136},{12,140},{16,144},{20,148},{24,152},{28,15... | collective-permute-start | bytes 1572872 | tf_op jit(solution)/shard_map/ppermute | solution.py:27
  51.4 11.0 %collective-permute-done.4.a_ref = bf16[8,256,128]{2,1,0:T(8,128)(2,1)S(1)} collective-permute-done((bf16[8,256,128]{2,1,0:T(8,128)(2,1)}, bf16[8,256,128]{2,1,0:T(8,128)(2,1)S(1)}, u32[]{:S(2)}, u32[]{:S(2)}) %collective-permute-start.4) | collective-permute-done | bytes 524320 | tf_op jit(solution)/shard_map/ppermute | solution.py:27
  62.4 12.1 %collective-permute-done.5.b_ref = bf16[8,256,128]{2,1,0:T(8,128)(2,1)S(1)} collective-permute-done((bf16[8,256,128]{2,1,0:T(8,128)(2,1)}, bf16[8,256,128]{2,1,0:T(8,128)(2,1)S(1)}, u32[]{:S(2)}, u32[]{:S(2)}) %collective-permute-start.5) | collective-permute-done | bytes 524320 | tf_op jit(solution)/shard_map/ppermute | solution.py:27
  75.5 2.5 %line_sums.1 = (f32[256,128]{1,0:T(8,128)}, bf16[256,128]{1,0:T(8,128)(2,1)}, bf16[256,128]{1,0:T(8,128)(2,1)}, bf16[256,128]{1,0:T(8,128)(2,1)}, bf16[256,128]{...) custom-call(s32[4]{0:T(128)} %pad_add_fusion.place, ...), custom_call_target="tpu_custom_call" | custom-call | flops 1000000 | bytes 4194304 | tf_op jit(solution)/shard_map/line_sums/pallas_call | solution.py:147
  79.3 4.0 %collective-permute-done.7.other_ref = bf16[32,128,256]{2,1,0:T(8,128)(2,1)S(1)} collective-permute-done((bf16[32,128,256]{2,1,0:T(8,128)(2,1)}, bf16[32,128,256]{2,1,0:T(8,128)(2,1)S(1)}, u32[]{:S(2)}, u32[]{:S(2)}) %collective-permute-start.7) | collective-permute-done | bytes 2097184 | tf_op jit(solution)/shard_map/ppermute | solution.py:27
  84.7 13.9 %out_terms.1 = bf16[168,128,128]{2,1,0:T(8,128)(2,1)} custom-call(s32[4]{0:T(128)} %pad_add_fusion.place, s32[2,84]{1,0:T(2,128)} %bitcast.39, bf16[256,10752]{1,0:T(8,128)(2,1)} %cot_ref.3, bf16[32,128,256]{2,1,0:T(8,128)(2,1)} %after.1.own_ref, bf16[32,128,256]{2,1,0:T(8,128)(2,1)} %copy-done.1), custom_call_target="tpu_custom_call" | custom-call | flops 3000000000 | bytes 16777216 | tf_op jit(solution)/shard_map/out_terms/pallas_call | solution.py:184
  99.4 4.0 %collective-permute-start.10 = (bf16[256,128]{1,0:T(8,128)(2,1)S(1)}, bf16[256,128]{1,0:T(8,128)(2,1)S(1)}, u32[]{:S(2)}, u32[]{:S(2)}) collective-permute-start(bf16[256,128]{1,0:T(8,128)(2,1)S(1)} %copy-done.21), channel_id=1, source_target_pairs={{0,24},{4,28},{8,32},{12,36},{16,40},{20,44},{24,48},{28,52},{32,5... | collective-permute-start | bytes 196616 | tf_op jit(solution)/shard_map/ppermute | solution.py:27
  103.4 4.3 %collective-permute-start.11 = (bf16[256,128]{1,0:T(8,128)(2,1)S(1)}, bf16[256,128]{1,0:T(8,128)(2,1)S(1)}, u32[]{:S(2)}, u32[]{:S(2)}) collective-permute-start(bf16[256,128]{1,0:T(8,128)(2,1)S(1)} %copy-done.20), channel_id=1, source_target_pairs={{0,32},{4,36},{8,40},{12,44},{16,48},{20,52},{24,56},{28,60},{32,0... | collective-permute-start | bytes 196616 | tf_op jit(solution)/shard_map/ppermute | solution.py:27
  107.7 2.7 %collective-permute-start.12 = (bf16[256,128]{1,0:T(8,128)(2,1)S(1)}, bf16[256,128]{1,0:T(8,128)(2,1)S(1)}, u32[]{:S(2)}, u32[]{:S(2)}) collective-permute-start(bf16[256,128]{1,0:T(8,128)(2,1)S(1)} %copy-done.19), channel_id=1, source_target_pairs={{0,40},{4,44},{8,48},{12,52},{16,56},{20,60},{24,0},{28,4},{32,8},... | collective-permute-start | bytes 196616 | tf_op jit(solution)/shard_map/ppermute | solution.py:27
  112.8 2.6 %collective-permute-start.9 = (bf16[256,128]{1,0:T(8,128)(2,1)S(1)}, bf16[256,128]{1,0:T(8,128)(2,1)S(1)}, u32[]{:S(2)}, u32[]{:S(2)}) collective-permute-start(bf16[256,128]{1,0:T(8,128)(2,1)S(1)} %copy-done.15), channel_id=1, source_target_pairs={{0,16},{4,20},{8,24},{12,28},{16,32},{20,36},{24,40},{28,44},{32,4... | collective-permute-start | bytes 196616 | tf_op jit(solution)/shard_map/ppermute | solution.py:27
  116.2 4.1 %collective-permute-done.13 = bf16[256,128]{1,0:T(8,128)(2,1)S(1)} collective-permute-done((bf16[256,128]{1,0:T(8,128)(2,1)S(1)}, bf16[256,128]{1,0:T(8,128)(2,1)S(1)}, u32[]{:S(2)}, u32[]{:S(2)}) %collective-permute-start.13) | collective-permute-done | bytes 65568 | tf_op jit(solution)/shard_map/ppermute | solution.py:27
  125.8 2.4 %collective-permute-start.18 = (bf16[256,128]{1,0:T(8,128)(2,1)S(1)}, bf16[256,128]{1,0:T(8,128)(2,1)S(1)}, u32[]{:S(2)}, u32[]{:S(2)}) collective-permute-start(bf16[256,128]{1,0:T(8,128)(2,1)S(1)} %get-tuple-element.39), channel_id=1, source_target_pairs={{0,32},{4,36},{8,40},{12,44},{16,48},{20,52},{24,56},{28,60},{32,0... | collective-permute-start | bytes 196616 | tf_op jit(solution)/shard_map/ppermute | solution.py:27
  128.2 2.1 %collective-permute-start.19 = (bf16[256,128]{1,0:T(8,128)(2,1)S(1)}, bf16[256,128]{1,0:T(8,128)(2,1)S(1)}, u32[]{:S(2)}, u32[]{:S(2)}) collective-permute-start(bf16[256,128]{1,0:T(8,128)(2,1)S(1)} %get-tuple-element.39), channel_id=1, source_target_pairs={{0,40},{4,44},{8,48},{12,52},{16,56},{20,60},{24,0},{28,4},{32,8},... | collective-permute-start | bytes 196616 | tf_op jit(solution)/shard_map/ppermute | solution.py:27
  130.3 3.5 %collective-permute-start.20 = (bf16[256,128]{1,0:T(8,128)(2,1)S(1)}, bf16[256,128]{1,0:T(8,128)(2,1)S(1)}, u32[]{:S(2)}, u32[]{:S(2)}) collective-permute-start(bf16[256,128]{1,0:T(8,128)(2,1)S(1)} %get-tuple-element.39), channel_id=1, source_target_pairs={{0,48},{4,52},{8,56},{12,60},{16,0},{20,4},{24,8},{28,12},{32,16},... | collective-permute-start | bytes 196616 | tf_op jit(solution)/shard_map/ppermute | solution.py:27
  133.9 2.7 %collective-permute-done.18 = bf16[256,128]{1,0:T(8,128)(2,1)S(1)} collective-permute-done((bf16[256,128]{1,0:T(8,128)(2,1)S(1)}, bf16[256,128]{1,0:T(8,128)(2,1)S(1)}, u32[]{:S(2)}, u32[]{:S(2)}) %collective-permute-start.18) | collective-permute-done | bytes 65568 | tf_op jit(solution)/shard_map/ppermute | solution.py:27
  136.6 3.2 %collective-permute-done.20 = bf16[256,128]{1,0:T(8,128)(2,1)S(1)} collective-permute-done((bf16[256,128]{1,0:T(8,128)(2,1)S(1)}, bf16[256,128]{1,0:T(8,128)(2,1)S(1)}, u32[]{:S(2)}, u32[]{:S(2)}) %collective-permute-start.20) | collective-permute-done | bytes 65568 | tf_op jit(solution)/shard_map/ppermute | solution.py:27
  141.0 3.1 %collective-permute-start.23 = (bf16[8,256,128]{2,1,0:T(8,128)(2,1)S(1)}, bf16[8,256,128]{2,1,0:T(8,128)(2,1)S(1)}, u32[]{:S(2)}, u32[]{:S(2)}) collective-permute-start(bf16[8,256,128]{2,1,0:T(8,128)(2,1)S(1)} %bitcast_dynamic-update-slice_fusion.refs_0_), channel_id=1, source_target_pairs={{0,128},{4,132},{8,136},{12,140},{16,144},{20,148},{24,152},{28,15... | collective-permute-start | bytes 1572872 | tf_op jit(solution)/shard_map/ppermute | solution.py:27
  144.1 3.1 %collective-permute-start.25 = (bf16[8,256,128]{2,1,0:T(8,128)(2,1)S(1)}, bf16[8,256,128]{2,1,0:T(8,128)(2,1)S(1)}, u32[]{:S(2)}, u32[]{:S(2)}) collective-permute-start(bf16[8,256,128]{2,1,0:T(8,128)(2,1)S(1)} %bitcast_dynamic-update-slice_fusion.refs_0_), channel_id=1, source_target_pairs={{0,4},{4,0},{8,12},{12,8},{16,20},{20,16},{24,28},{28,24},{32,36},... | collective-permute-start | bytes 1572872 | tf_op jit(solution)/shard_map/ppermute | solution.py:27
  147.2 6.0 %collective-permute-done.22.refs_1_ = bf16[8,256,128]{2,1,0:T(8,128)(2,1)S(1)} collective-permute-done((bf16[8,256,128]{2,1,0:T(8,128)(2,1)S(1)}, bf16[8,256,128]{2,1,0:T(8,128)(2,1)S(1)}, u32[]{:S(2)}, u32[]{:S(2)}) %collective-permute-start.22) | collective-permute-done | bytes 524320 | tf_op jit(solution)/shard_map/ppermute | solution.py:27
  153.2 6.0 %collective-permute-start.26 = (bf16[8,256,128]{2,1,0:T(8,128)(2,1)S(1)}, bf16[8,256,128]{2,1,0:T(8,128)(2,1)S(1)}, u32[]{:S(2)}, u32[]{:S(2)}) collective-permute-start(bf16[8,256,128]{2,1,0:T(8,128)(2,1)S(1)} %collective-permute-done.22.refs_1_), channel_id=1, source_target_pairs={{0,4},{4,0},{8,12},{12,8},{16,20},{20,16},{24,28},{28,24},{32,36},... | collective-permute-start | bytes 1572872 | tf_op jit(solution)/shard_map/ppermute | solution.py:27
  159.2 5.6 %collective-permute-done.23.refs_2_ = bf16[8,256,128]{2,1,0:T(8,128)(2,1)S(1)} collective-permute-done((bf16[8,256,128]{2,1,0:T(8,128)(2,1)S(1)}, bf16[8,256,128]{2,1,0:T(8,128)(2,1)S(1)}, u32[]{:S(2)}, u32[]{:S(2)}) %collective-permute-start.23) | collective-permute-done | bytes 524320 | tf_op jit(solution)/shard_map/ppermute | solution.py:27
  164.7 3.5 %collective-permute-start.27 = (bf16[8,256,128]{2,1,0:T(8,128)(2,1)S(1)}, bf16[8,256,128]{2,1,0:T(8,128)(2,1)S(1)}, u32[]{:S(2)}, u32[]{:S(2)}) collective-permute-start(bf16[8,256,128]{2,1,0:T(8,128)(2,1)S(1)} %collective-permute-done.23.refs_2_), channel_id=1, source_target_pairs={{0,4},{4,0},{8,12},{12,8},{16,20},{20,16},{24,28},{28,24},{32,36},... | collective-permute-start | bytes 1572872 | tf_op jit(solution)/shard_map/ppermute | solution.py:27
  171.3 5.0 %in_terms.1 = (f32[7,128,128]{2,1,0:T(8,128)}, bf16[7,128,128]{2,1,0:T(8,128)(2,1)}, bf16[7,128,128]{2,1,0:T(8,128)(2,1)}, bf16[7,128,128]{2,1,0:T(8,128)(2,1)}) custom-call(s32[4]{0:T(128)} %pad_add_fusion.place, s32[4,7]{1,0:T(4,128)} %bitcast.37, bf16[256,896]{1,0:T(8,128)(2,1)} %enc_ref.1, bf16[8,256,128]{2,1,0:T(8,128)(2,1)} %copy-done.2, ...), custom_call_target="tpu_custom_call" | custom-call | flops 500000000 | bytes 8388608 | tf_op jit(solution)/shard_map/in_terms/pallas_call | solution.py:238
  177.6 2.8 %collective-permute-start.30 = (bf16[7,128,128]{2,1,0:T(8,128)(2,1)}, bf16[7,128,128]{2,1,0:T(8,128)(2,1)S(1)}, u32[]{:S(2)}, u32[]{:S(2)}) collective-permute-start(bf16[7,128,128]{2,1,0:T(8,128)(2,1)} %get-tuple-element.36), channel_id=1, source_target_pairs={{0,2},{1,3},{2,0},{3,1},{4,6},{5,7},{6,4},{7,5},{8,10},{9,11},{10,... | collective-permute-start | bytes 688136 | tf_op jit(solution)/shard_map/ppermute | solution.py:31
  181.4 3.6 %collective-permute-done.29 = bf16[7,128,128]{2,1,0:T(8,128)(2,1)S(1)} collective-permute-done((bf16[7,128,128]{2,1,0:T(8,128)(2,1)}, bf16[7,128,128]{2,1,0:T(8,128)(2,1)S(1)}, u32[]{:S(2)}, u32[]{:S(2)}) %collective-permute-start.29) | collective-permute-done | bytes 229408 | tf_op jit(solution)/shard_map/ppermute | solution.py:31
  185.0 5.9 %collective-permute-done.30 = bf16[7,128,128]{2,1,0:T(8,128)(2,1)S(1)} collective-permute-done((bf16[7,128,128]{2,1,0:T(8,128)(2,1)}, bf16[7,128,128]{2,1,0:T(8,128)(2,1)S(1)}, u32[]{:S(2)}, u32[]{:S(2)}) %collective-permute-start.30) | collective-permute-done | bytes 229408 | tf_op jit(solution)/shard_map/ppermute | solution.py:31
  (101 shorter events, 29.8 us)
Async XLA Ops:
  7.2 70.9 %all-gather.3.cloned.1.call-start = ((), (), s32[]{:S(2)}) async-start(), calls=%async_computation.2 | async-start | bytes 2359296 | tf_op jit(solution)/shard_map/all_gather | solution.py:270
  8.1 5.7 %collective-permute-start = (bf16[128,256]{0,1:T(8,128)(2,1)S(1)}, bf16[128,256]{0,1:T(8,128)(2,1)S(1)}, u32[]{:S(2)}, u32[]{:S(2)}) collective-permute-start(bf16[128,256]{0,1:T(8,128)(2,1)S(1)} %get-tuple-element.41), channel_id=1, source_target_pairs={{0,64},{4,68},{8,72},{12,76},{16,80},{20,84},{24,88},{28,92},{32,9... | collective-permute-start | bytes 196616 | tf_op jit(solution)/shard_map/ppermute | solution.py:27
  10.2 5.1 %collective-permute-start.1 = (bf16[128,256]{0,1:T(8,128)(2,1)S(1)}, bf16[128,256]{0,1:T(8,128)(2,1)S(1)}, u32[]{:S(2)}, u32[]{:S(2)}) collective-permute-start(bf16[128,256]{0,1:T(8,128)(2,1)S(1)} %get-tuple-element.41), channel_id=1, source_target_pairs={{0,128},{4,132},{8,136},{12,140},{16,144},{20,148},{24,152},{28,15... | collective-permute-start | bytes 196616 | tf_op jit(solution)/shard_map/ppermute | solution.py:27
  17.0 175.7 %reduce-scatter.2.cloned.1.call-start = ((), (), s32[]{:S(2)}) async-start(), calls=%async_computation.1 | async-start | bytes 6881280 | tf_op jit(solution)/shard_map/reduce_scatter | solution.py:287
  32.8 6.4 %collective-permute-start.3 = (bf16[32,256,128]{2,1,0:T(8,128)(2,1)}, bf16[32,256,128]{2,1,0:T(8,128)(2,1)S(1)}, u32[]{:S(2)}, u32[]{:S(2)}) collective-permute-start(bf16[32,256,128]{2,1,0:T(8,128)(2,1)} %get-tuple-element.21), channel_id=1, source_target_pairs={{0,4},{4,0},{8,12},{12,8},{16,20},{20,16},{24,28},{28,24},{32,36},... | collective-permute-start | bytes 6291464 | tf_op jit(solution)/shard_map/ppermute | solution.py:27
  47.8 14.6 %collective-permute-start.4 = (bf16[8,256,128]{2,1,0:T(8,128)(2,1)}, bf16[8,256,128]{2,1,0:T(8,128)(2,1)S(1)}, u32[]{:S(2)}, u32[]{:S(2)}) collective-permute-start(bf16[8,256,128]{2,1,0:T(8,128)(2,1)} %get-tuple-element.23), channel_id=1, source_target_pairs={{0,64},{4,68},{8,72},{12,76},{16,80},{20,84},{24,88},{28,92},{32,9... | collective-permute-start | bytes 1572872 | tf_op jit(solution)/shard_map/ppermute | solution.py:27
  48.9 25.7 %collective-permute-start.5 = (bf16[8,256,128]{2,1,0:T(8,128)(2,1)}, bf16[8,256,128]{2,1,0:T(8,128)(2,1)S(1)}, u32[]{:S(2)}, u32[]{:S(2)}) collective-permute-start(bf16[8,256,128]{2,1,0:T(8,128)(2,1)} %get-tuple-element.24), channel_id=1, source_target_pairs={{0,128},{4,132},{8,136},{12,140},{16,144},{20,148},{24,152},{28,15... | collective-permute-start | bytes 1572872 | tf_op jit(solution)/shard_map/ppermute | solution.py:27
  51.4 23.1 %collective-permute-start.6 = (bf16[8,256,128]{2,1,0:T(8,128)(2,1)}, bf16[8,256,128]{2,1,0:T(8,128)(2,1)S(1)}, u32[]{:S(2)}, u32[]{:S(2)}) collective-permute-start(bf16[8,256,128]{2,1,0:T(8,128)(2,1)} %get-tuple-element.25), channel_id=1, source_target_pairs={{0,192},{4,196},{8,200},{12,204},{16,208},{20,212},{24,216},{28,22... | collective-permute-start | bytes 1572872 | tf_op jit(solution)/shard_map/ppermute | solution.py:27
  78.1 5.3 %collective-permute-start.7 = (bf16[32,128,256]{2,1,0:T(8,128)(2,1)}, bf16[32,128,256]{2,1,0:T(8,128)(2,1)S(1)}, u32[]{:S(2)}, u32[]{:S(2)}) collective-permute-start(bf16[32,128,256]{2,1,0:T(8,128)(2,1)} %after.1.own_ref), channel_id=1, source_target_pairs={{0,4},{4,0},{8,12},{12,8},{16,20},{20,16},{24,28},{28,24},{32,36},... | collective-permute-start | bytes 6291464 | tf_op jit(solution)/shard_map/ppermute | solution.py:27
  99.4 11.4 %collective-permute-start.10 = (bf16[256,128]{1,0:T(8,128)(2,1)S(1)}, bf16[256,128]{1,0:T(8,128)(2,1)S(1)}, u32[]{:S(2)}, u32[]{:S(2)}) collective-permute-start(bf16[256,128]{1,0:T(8,128)(2,1)S(1)} %copy-done.21), channel_id=1, source_target_pairs={{0,24},{4,28},{8,32},{12,36},{16,40},{20,44},{24,48},{28,52},{32,5... | collective-permute-start | bytes 196616 | tf_op jit(solution)/shard_map/ppermute | solution.py:27
  103.4 9.4 %collective-permute-start.11 = (bf16[256,128]{1,0:T(8,128)(2,1)S(1)}, bf16[256,128]{1,0:T(8,128)(2,1)S(1)}, u32[]{:S(2)}, u32[]{:S(2)}) collective-permute-start(bf16[256,128]{1,0:T(8,128)(2,1)S(1)} %copy-done.20), channel_id=1, source_target_pairs={{0,32},{4,36},{8,40},{12,44},{16,48},{20,52},{24,56},{28,60},{32,0... | collective-permute-start | bytes 196616 | tf_op jit(solution)/shard_map/ppermute | solution.py:27
  107.7 8.5 %collective-permute-start.12 = (bf16[256,128]{1,0:T(8,128)(2,1)S(1)}, bf16[256,128]{1,0:T(8,128)(2,1)S(1)}, u32[]{:S(2)}, u32[]{:S(2)}) collective-permute-start(bf16[256,128]{1,0:T(8,128)(2,1)S(1)} %copy-done.19), channel_id=1, source_target_pairs={{0,40},{4,44},{8,48},{12,52},{16,56},{20,60},{24,0},{28,4},{32,8},... | collective-permute-start | bytes 196616 | tf_op jit(solution)/shard_map/ppermute | solution.py:27
  110.4 9.8 %collective-permute-start.13 = (bf16[256,128]{1,0:T(8,128)(2,1)S(1)}, bf16[256,128]{1,0:T(8,128)(2,1)S(1)}, u32[]{:S(2)}, u32[]{:S(2)}) collective-permute-start(bf16[256,128]{1,0:T(8,128)(2,1)S(1)} %copy-done.18), channel_id=1, source_target_pairs={{0,48},{4,52},{8,56},{12,60},{16,0},{20,4},{24,8},{28,12},{32,16},... | collective-permute-start | bytes 196616 | tf_op jit(solution)/shard_map/ppermute | solution.py:27
  110.5 9.8 %collective-permute-start.14 = (bf16[256,128]{1,0:T(8,128)(2,1)S(1)}, bf16[256,128]{1,0:T(8,128)(2,1)S(1)}, u32[]{:S(2)}, u32[]{:S(2)}) collective-permute-start(bf16[256,128]{1,0:T(8,128)(2,1)S(1)} %copy-done.17), channel_id=1, source_target_pairs={{0,56},{4,60},{8,0},{12,4},{16,8},{20,12},{24,16},{28,20},{32,24},... | collective-permute-start | bytes 196616 | tf_op jit(solution)/shard_map/ppermute | solution.py:27
  110.8 9.4 %collective-permute-start.8 = (bf16[256,128]{1,0:T(8,128)(2,1)S(1)}, bf16[256,128]{1,0:T(8,128)(2,1)S(1)}, u32[]{:S(2)}, u32[]{:S(2)}) collective-permute-start(bf16[256,128]{1,0:T(8,128)(2,1)S(1)} %copy-done.16), channel_id=1, source_target_pairs={{0,8},{4,12},{8,16},{12,20},{16,24},{20,28},{24,32},{28,36},{32,40... | collective-permute-start | bytes 196616 | tf_op jit(solution)/shard_map/ppermute | solution.py:27
  112.8 7.5 %collective-permute-start.9 = (bf16[256,128]{1,0:T(8,128)(2,1)S(1)}, bf16[256,128]{1,0:T(8,128)(2,1)S(1)}, u32[]{:S(2)}, u32[]{:S(2)}) collective-permute-start(bf16[256,128]{1,0:T(8,128)(2,1)S(1)} %copy-done.15), channel_id=1, source_target_pairs={{0,16},{4,20},{8,24},{12,28},{16,32},{20,36},{24,40},{28,44},{32,4... | collective-permute-start | bytes 196616 | tf_op jit(solution)/shard_map/ppermute | solution.py:27
  120.4 9.9 %collective-permute-start.15 = (bf16[256,128]{1,0:T(8,128)(2,1)S(1)}, bf16[256,128]{1,0:T(8,128)(2,1)S(1)}, u32[]{:S(2)}, u32[]{:S(2)}) collective-permute-start(bf16[256,128]{1,0:T(8,128)(2,1)S(1)} %get-tuple-element.39), channel_id=1, source_target_pairs={{0,8},{4,12},{8,16},{12,20},{16,24},{20,28},{24,32},{28,36},{32,40... | collective-permute-start | bytes 196616 | tf_op jit(solution)/shard_map/ppermute | solution.py:27
  122.2 11.6 %collective-permute-start.16 = (bf16[256,128]{1,0:T(8,128)(2,1)S(1)}, bf16[256,128]{1,0:T(8,128)(2,1)S(1)}, u32[]{:S(2)}, u32[]{:S(2)}) collective-permute-start(bf16[256,128]{1,0:T(8,128)(2,1)S(1)} %get-tuple-element.39), channel_id=1, source_target_pairs={{0,16},{4,20},{8,24},{12,28},{16,32},{20,36},{24,40},{28,44},{32,4... | collective-permute-start | bytes 196616 | tf_op jit(solution)/shard_map/ppermute | solution.py:27
  124.1 9.9 %collective-permute-start.17 = (bf16[256,128]{1,0:T(8,128)(2,1)S(1)}, bf16[256,128]{1,0:T(8,128)(2,1)S(1)}, u32[]{:S(2)}, u32[]{:S(2)}) collective-permute-start(bf16[256,128]{1,0:T(8,128)(2,1)S(1)} %get-tuple-element.39), channel_id=1, source_target_pairs={{0,24},{4,28},{8,32},{12,36},{16,40},{20,44},{24,48},{28,52},{32,5... | collective-permute-start | bytes 196616 | tf_op jit(solution)/shard_map/ppermute | solution.py:27
  125.8 10.8 %collective-permute-start.18 = (bf16[256,128]{1,0:T(8,128)(2,1)S(1)}, bf16[256,128]{1,0:T(8,128)(2,1)S(1)}, u32[]{:S(2)}, u32[]{:S(2)}) collective-permute-start(bf16[256,128]{1,0:T(8,128)(2,1)S(1)} %get-tuple-element.39), channel_id=1, source_target_pairs={{0,32},{4,36},{8,40},{12,44},{16,48},{20,52},{24,56},{28,60},{32,0... | collective-permute-start | bytes 196616 | tf_op jit(solution)/shard_map/ppermute | solution.py:27
  128.2 8.4 %collective-permute-start.19 = (bf16[256,128]{1,0:T(8,128)(2,1)S(1)}, bf16[256,128]{1,0:T(8,128)(2,1)S(1)}, u32[]{:S(2)}, u32[]{:S(2)}) collective-permute-start(bf16[256,128]{1,0:T(8,128)(2,1)S(1)} %get-tuple-element.39), channel_id=1, source_target_pairs={{0,40},{4,44},{8,48},{12,52},{16,56},{20,60},{24,0},{28,4},{32,8},... | collective-permute-start | bytes 196616 | tf_op jit(solution)/shard_map/ppermute | solution.py:27
  130.3 9.6 %collective-permute-start.20 = (bf16[256,128]{1,0:T(8,128)(2,1)S(1)}, bf16[256,128]{1,0:T(8,128)(2,1)S(1)}, u32[]{:S(2)}, u32[]{:S(2)}) collective-permute-start(bf16[256,128]{1,0:T(8,128)(2,1)S(1)} %get-tuple-element.39), channel_id=1, source_target_pairs={{0,48},{4,52},{8,56},{12,60},{16,0},{20,4},{24,8},{28,12},{32,16},... | collective-permute-start | bytes 196616 | tf_op jit(solution)/shard_map/ppermute | solution.py:27
  133.8 7.1 %collective-permute-start.21 = (bf16[256,128]{1,0:T(8,128)(2,1)S(1)}, bf16[256,128]{1,0:T(8,128)(2,1)S(1)}, u32[]{:S(2)}, u32[]{:S(2)}) collective-permute-start(bf16[256,128]{1,0:T(8,128)(2,1)S(1)} %get-tuple-element.39), channel_id=1, source_target_pairs={{0,56},{4,60},{8,0},{12,4},{16,8},{20,12},{24,16},{28,20},{32,24},... | collective-permute-start | bytes 196616 | tf_op jit(solution)/shard_map/ppermute | solution.py:27
  140.9 12.3 %collective-permute-start.22 = (bf16[8,256,128]{2,1,0:T(8,128)(2,1)S(1)}, bf16[8,256,128]{2,1,0:T(8,128)(2,1)S(1)}, u32[]{:S(2)}, u32[]{:S(2)}) collective-permute-start(bf16[8,256,128]{2,1,0:T(8,128)(2,1)S(1)} %bitcast_dynamic-update-slice_fusion.refs_0_), channel_id=1, source_target_pairs={{0,64},{4,68},{8,72},{12,76},{16,80},{20,84},{24,88},{28,92},{32,9... | collective-permute-start | bytes 1572872 | tf_op jit(solution)/shard_map/ppermute | solution.py:27
  141.0 23.7 %collective-permute-start.23 = (bf16[8,256,128]{2,1,0:T(8,128)(2,1)S(1)}, bf16[8,256,128]{2,1,0:T(8,128)(2,1)S(1)}, u32[]{:S(2)}, u32[]{:S(2)}) collective-permute-start(bf16[8,256,128]{2,1,0:T(8,128)(2,1)S(1)} %bitcast_dynamic-update-slice_fusion.refs_0_), channel_id=1, source_target_pairs={{0,128},{4,132},{8,136},{12,140},{16,144},{20,148},{24,152},{28,15... | collective-permute-start | bytes 1572872 | tf_op jit(solution)/shard_map/ppermute | solution.py:27
  144.1 24.1 %collective-permute-start.24 = (bf16[8,256,128]{2,1,0:T(8,128)(2,1)S(1)}, bf16[8,256,128]{2,1,0:T(8,128)(2,1)S(1)}, u32[]{:S(2)}, u32[]{:S(2)}) collective-permute-start(bf16[8,256,128]{2,1,0:T(8,128)(2,1)S(1)} %bitcast_dynamic-update-slice_fusion.refs_0_), channel_id=1, source_target_pairs={{0,192},{4,196},{8,200},{12,204},{16,208},{20,212},{24,216},{28,22... | collective-permute-start | bytes 1572872 | tf_op jit(solution)/shard_map/ppermute | solution.py:27
  144.1 24.3 %collective-permute-start.25 = (bf16[8,256,128]{2,1,0:T(8,128)(2,1)S(1)}, bf16[8,256,128]{2,1,0:T(8,128)(2,1)S(1)}, u32[]{:S(2)}, u32[]{:S(2)}) collective-permute-start(bf16[8,256,128]{2,1,0:T(8,128)(2,1)S(1)} %bitcast_dynamic-update-slice_fusion.refs_0_), channel_id=1, source_target_pairs={{0,4},{4,0},{8,12},{12,8},{16,20},{20,16},{24,28},{28,24},{32,36},... | collective-permute-start | bytes 1572872 | tf_op jit(solution)/shard_map/ppermute | solution.py:27
  153.2 15.2 %collective-permute-start.26 = (bf16[8,256,128]{2,1,0:T(8,128)(2,1)S(1)}, bf16[8,256,128]{2,1,0:T(8,128)(2,1)S(1)}, u32[]{:S(2)}, u32[]{:S(2)}) collective-permute-start(bf16[8,256,128]{2,1,0:T(8,128)(2,1)S(1)} %collective-permute-done.22.refs_1_), channel_id=1, source_target_pairs={{0,4},{4,0},{8,12},{12,8},{16,20},{20,16},{24,28},{28,24},{32,36},... | collective-permute-start | bytes 1572872 | tf_op jit(solution)/shard_map/ppermute | solution.py:27
  164.7 5.0 %collective-permute-start.27 = (bf16[8,256,128]{2,1,0:T(8,128)(2,1)S(1)}, bf16[8,256,128]{2,1,0:T(8,128)(2,1)S(1)}, u32[]{:S(2)}, u32[]{:S(2)}) collective-permute-start(bf16[8,256,128]{2,1,0:T(8,128)(2,1)S(1)} %collective-permute-done.23.refs_2_), channel_id=1, source_target_pairs={{0,4},{4,0},{8,12},{12,8},{16,20},{20,16},{24,28},{28,24},{32,36},... | collective-permute-start | bytes 1572872 | tf_op jit(solution)/shard_map/ppermute | solution.py:27
  176.3 8.6 %collective-permute-start.29 = (bf16[7,128,128]{2,1,0:T(8,128)(2,1)}, bf16[7,128,128]{2,1,0:T(8,128)(2,1)S(1)}, u32[]{:S(2)}, u32[]{:S(2)}) collective-permute-start(bf16[7,128,128]{2,1,0:T(8,128)(2,1)} %get-tuple-element.35), channel_id=1, source_target_pairs={{0,1},{1,2},{2,3},{3,0},{4,5},{5,6},{6,7},{7,4},{8,9},{9,10},{10,1... | collective-permute-start | bytes 688136 | tf_op jit(solution)/shard_map/ppermute | solution.py:31
  177.6 13.3 %collective-permute-start.30 = (bf16[7,128,128]{2,1,0:T(8,128)(2,1)}, bf16[7,128,128]{2,1,0:T(8,128)(2,1)S(1)}, u32[]{:S(2)}, u32[]{:S(2)}) collective-permute-start(bf16[7,128,128]{2,1,0:T(8,128)(2,1)} %get-tuple-element.36), channel_id=1, source_target_pairs={{0,2},{1,3},{2,0},{3,1},{4,6},{5,7},{6,4},{7,5},{8,10},{9,11},{10,... | collective-permute-start | bytes 688136 | tf_op jit(solution)/shard_map/ppermute | solution.py:31
  180.4 10.5 %collective-permute-start.31 = (bf16[7,128,128]{2,1,0:T(8,128)(2,1)}, bf16[7,128,128]{2,1,0:T(8,128)(2,1)S(1)}, u32[]{:S(2)}, u32[]{:S(2)}) collective-permute-start(bf16[7,128,128]{2,1,0:T(8,128)(2,1)} %get-tuple-element.37), channel_id=1, source_target_pairs={{0,3},{1,0},{2,1},{3,2},{4,7},{5,4},{6,5},{7,6},{8,11},{9,8},{10,9... | collective-permute-start | bytes 688136 | tf_op jit(solution)/shard_map/ppermute | solution.py:31
  (24 other events, 191.6 us)
Sparse Core Ops, SparseCore 0:
  17.1 41.4 all-gather.2
  98.8 61.7 reduce-scatter.1

commit v2 on v1

--- a/solution.py
+++ b/solution.py
@@ -9,8 +9,9 @@
 F32 = jnp.float32
 NX, NZ, NC, NY = 4, 8, 2, 4
 BS = 128
-STEP_BLOCKS = 7
-VMEM = 56 * 2**20
+STEP_BLOCKS = 28
+OUT_STEP = 28
+CORE_STEP = 2
 
 
 def index_of(x, z, core):
@@ -27,12 +28,11 @@
     return lax.ppermute(value, "blk", pairs)
 
 
-def moved_smp(value, dy):
-    return lax.ppermute(value, "smp", [(i, (i + dy) % NY) for i in range(NY)])
-
-
-def params(**more):
-    return pltpu.CompilerParams(vmem_limit_bytes=VMEM, **more)
+LINES = [[index_of(x, z, c) for z in range(NZ)] for x in range(NX) for c in range(NC)]
+
+
+def params(mib):
+    return pltpu.CompilerParams(vmem_limit_bytes=mib * 2**20)
 
 
 def contract(lhs, rhs, over):
@@ -100,7 +100,7 @@
             jax.ShapeDtypeStruct((count, rows, BS), BF16),
             jax.ShapeDtypeStruct((count, rows, BS), F32),
         ],
-        compiler_params=params(),
+        compiler_params=params(56),
         cost_estimate=pl.CostEstimate(flops=3 * 10**9, bytes_accessed=2**24, transcendentals=0),
         name="hidden_sums",
     )(place, contacts, cotangent, weights)
@@ -110,35 +110,37 @@
     x = place[0]
     for d in range(NX):
         at = (x + d) & (NX - 1)
-        outs[d][0] = (keep_ref[at, 0] + got_ref[at, 0].astype(F32)).astype(outs[d].dtype)
+        for n in range(CORE_STEP):
+            outs[d][n] = (keep_ref[at, n] + got_ref[at, n].astype(F32)).astype(outs[d].dtype)
 
 
 def core_sums(place, keep, got):
     rows = keep.shape[1]
-    spec = pl.BlockSpec((NX, 1, rows, BS), lambda g, *_: (0, g, 0, 0))
+    spec = pl.BlockSpec((NX, CORE_STEP, rows, BS), lambda g, *_: (0, g, 0, 0))
     return pl.pallas_call(
         core_kernel,
         grid_spec=pltpu.PrefetchScalarGridSpec(
             num_scalar_prefetch=1,
-            grid=(NZ,),
+            grid=(NZ // CORE_STEP,),
             in_specs=[spec, spec],
-            out_specs=[pl.BlockSpec((1, rows, BS), lambda g, *_: (g, 0, 0))] * NX,
+            out_specs=[pl.BlockSpec((CORE_STEP, rows, BS), lambda g, *_: (g, 0, 0))] * NX,
         ),
         out_shape=[
             jax.ShapeDtypeStruct((NZ, rows, BS), BF16 if d else F32) for d in range(NX)
         ],
-        compiler_params=params(),
+        compiler_params=params(16),
         cost_estimate=pl.CostEstimate(flops=10**6, bytes_accessed=2**23, transcendentals=0),
         name="core_sums",
     )(place, keep.reshape(NX, NZ, rows, BS), got.reshape(NX, NZ, rows, BS))
 
 
-def line_kernel(place, keep_ref, a_ref, b_ref, c_ref, *outs):
-    z = place[1]
-    for d in range(NZ):
-        at = (z + d) & (NZ - 1)
-        total = keep_ref[at] + a_ref[at].astype(F32) + b_ref[at].astype(F32) + c_ref[at].astype(F32)
-        outs[d][...] = total.astype(outs[d].dtype)
+def line_kernel(place, keep_ref, a_ref, b_ref, c_ref, send_ref, own_ref):
+    def total(at):
+        return keep_ref[at] + a_ref[at].astype(F32) + b_ref[at].astype(F32) + c_ref[at].astype(F32)
+
+    for at in range(NZ):
+        send_ref[at] = total(at).astype(BF16)
+    own_ref[...] = total(place[1])
 
 
 def line_sums(place, keep, *got):
@@ -147,9 +149,12 @@
     return pl.pallas_call(
         line_kernel,
         in_specs=[pl.BlockSpec(memory_space=pltpu.SMEM)] + [whole] * NX,
-        out_specs=[whole] * NZ,
-        out_shape=[jax.ShapeDtypeStruct((rows, BS), BF16 if d else F32) for d in range(NZ)],
-        compiler_params=params(),
+        out_specs=[whole] * 2,
+        out_shape=[
+            jax.ShapeDtypeStruct((NZ, rows, BS), BF16),
+            jax.ShapeDtypeStruct((rows, BS), F32),
+        ],
+        compiler_params=params(8),
         cost_estimate=pl.CostEstimate(flops=10**6, bytes_accessed=2**22, transcendentals=0),
         name="line_sums",
     )(place, keep, *got)
@@ -170,12 +175,14 @@
         for copy in copies:
             copy.wait()
 
-    for o in range(STEP_BLOCKS):
+    def block(k):
+        return held[k & 1, ((k >> 1) & (NZ - 1)) * NX + ((x - (k >> 4)) & (NX - 1))]
+
+    for o in range(OUT_STEP):
+        pair = [block(contacts[m, step * OUT_STEP + o]) for m in range(2)]
         cot = cot_ref[:, o * BS : (o + 1) * BS]
-        for m in range(2):
-            k = contacts[m, step * STEP_BLOCKS + o]
-            slot = ((k >> 1) & (NZ - 1)) * NX + ((x - (k >> 4)) & (NX - 1))
-            out_ref[2 * o + m] = contract(held[k & 1, slot], cot, (1, 0)).astype(BF16)
+        terms = contract(jnp.concatenate(pair), cot, (1, 0)).astype(BF16)
+        out_ref[2 * o : 2 * o + 2] = terms.reshape(2, BS, BS)
 
 
 def out_terms(place, contacts, cotangent, own, other):
@@ -185,28 +192,28 @@
         out_kernel,
         grid_spec=pltpu.PrefetchScalarGridSpec(
             num_scalar_prefetch=2,
-            grid=(count // STEP_BLOCKS,),
+            grid=(count // OUT_STEP,),
             in_specs=[
-                pl.BlockSpec((rows, STEP_BLOCKS * BS), lambda g, *_: (0, g)),
+                pl.BlockSpec((rows, OUT_STEP * BS), lambda g, *_: (0, g)),
                 pl.BlockSpec(memory_space=pl.ANY),
                 pl.BlockSpec(memory_space=pl.ANY),
             ],
-            out_specs=pl.BlockSpec((2 * STEP_BLOCKS, BS, BS), lambda g, *_: (g, 0, 0)),
+            out_specs=pl.BlockSpec((2 * OUT_STEP, BS, BS), lambda g, *_: (g, 0, 0)),
             scratch_shapes=[
                 pltpu.VMEM((NC, NX * NZ, BS, rows), BF16),
                 pltpu.SemaphoreType.DMA((2,)),
             ],
         ),
         out_shape=jax.ShapeDtypeStruct((2 * count, BS, BS), BF16),
-        compiler_params=params(),
+        compiler_params=params(56),
         cost_estimate=pl.CostEstimate(flops=3 * 10**9, bytes_accessed=2**24, transcendentals=0),
         name="out_terms",
     )(place, contacts, cotangent, own, other)
 
 
 def in_kernel(place, contacts, enc_ref, *refs):
-    parts, outs, (held, made, sems) = refs[: NC * NX], refs[NC * NX : NC * NX + NY], refs[NC * NX + NY :]
-    x, z, core, y = place[0], place[1], place[2], place[3]
+    parts, (send_ref, mine_ref, held, made, sems) = refs[: NC * NX], refs[NC * NX :]
+    x, core, y = place[0], place[2], place[3]
     copies = [
         pltpu.make_async_copy(part, held.at[n], sems.at[n]) for n, part in enumerate(parts)
     ]
@@ -220,13 +227,12 @@
         for m in range(per_in):
             k = contacts[m, i]
             slot = ((k & 1) ^ core) * NX + ((x - (k >> 4)) & (NX - 1))
-            value = held[slot, (z - (k >> 1)) & (NZ - 1)]
-            made[i * per_in + m] = contract(turned, value, (1, 0))
+            made[i * per_in + m] = contract(turned, held[slot, (k >> 1) & (NZ - 1)], (1, 0))
+    for n in range(count * per_in):
+        send_ref[n] = made[n].astype(BF16)
     each = count * per_in // NY
-    for d in range(NY):
-        first = ((y + d) & (NY - 1)) * each
-        for n in range(each):
-            outs[d][n] = made[first + n].astype(outs[d].dtype)
+    for n in range(each):
+        mine_ref[n] = made[y * each + n]
 
 
 def in_terms(place, contacts, encodings, parts):
@@ -238,17 +244,25 @@
     return pl.pallas_call(
         in_kernel,
         in_specs=[smem, smem, whole] + [pl.BlockSpec(memory_space=pl.ANY)] * (NC * NX),
-        out_specs=[whole] * NY,
+        out_specs=[whole] * 2,
         scratch_shapes=[
             pltpu.VMEM((NC * NX, NZ, rows, BS), BF16),
             pltpu.VMEM((per_in * count, BS, BS), F32),
             pltpu.SemaphoreType.DMA((NC * NX,)),
         ],
-        out_shape=[jax.ShapeDtypeStruct((each, BS, BS), BF16 if d else F32) for d in range(NY)],
-        compiler_params=params(),
+        out_shape=[
+            jax.ShapeDtypeStruct((per_in * count, BS, BS), BF16),
+            jax.ShapeDtypeStruct((each, BS, BS), F32),
+        ],
+        compiler_params=params(14),
         cost_estimate=pl.CostEstimate(flops=5 * 10**8, bytes_accessed=2**23, transcendentals=0),
         name="in_terms",
     )(place, contacts, encodings, *parts)
+
+
+def sum_parts(parts, own, at):
+    which = lax.broadcasted_iota(jnp.int32, parts.shape, 0)
+    return jnp.sum(jnp.where(which == at, own[None], parts.astype(F32)), axis=0)
 
 
 def silu_slope(values):
@@ -265,30 +279,33 @@
     pre = hidden_pre.astype(F32)
 
     activation = jax.nn.silu(pre).astype(BF16).T
-    along_x = jnp.stack([activation] + [moved(activation, dx=d) for d in range(1, NX)])
-    lines = [[index_of(x, z, c) for z in range(NZ)] for x in range(NX) for c in range(NC)]
-    act_own = lax.all_gather(along_x, "blk", axis_index_groups=lines)
+    arrived = [moved(activation, dx=d) for d in range(1, NX)]
+
+    send, keep = hidden_sums(place, out_index, cotangent, out_weights)
+    along_x = jnp.stack([after(activation, send)] + arrived)
+    send = after(send, along_x)
+    act_own = lax.all_gather(along_x, "blk", axis_index_groups=LINES)
     act_own = act_own.reshape(NZ * NX, BS, -1)
 
-    send, keep = hidden_sums(place, out_index, cotangent, out_weights)
-
     by_x = core_sums(place, keep, moved(send, dc=1))
-    by_z = line_sums(place, by_x[0], *[moved(by_x[d], dx=d) for d in range(1, NX)])
-    act_own = after(act_own, by_z[0])
-    got = [moved(by_z[d], dz=d) for d in range(1, NZ)]
-    grad_act = sum((g.astype(F32) for g in got), by_z[0])
-    grad_pre = (grad_act * silu_slope(pre)).astype(BF16)
-
-    along_z = jnp.stack([grad_pre] + [moved(grad_pre, dz=d) for d in range(1, NZ)])
+    by_z, own_z = line_sums(place, by_x[0], *[moved(by_x[d], dx=d) for d in range(1, NX)])
+    got = lax.all_to_all(by_z, "blk", 0, 0, axis_index_groups=LINES)
+    grad_pre = (sum_parts(got, own_z, place[1]) * silu_slope(pre)).astype(BF16)
+
+    act_own = after(act_own, by_z)
+    terms = out_terms(place, out_index, cotangent, act_own, moved(act_own, dc=1))
+    out_grad = lax.psum_scatter(terms, "smp", scatter_dimension=0, tiled=True)
+
+    copies = jnp.broadcast_to(grad_pre, (NZ, *grad_pre.shape))
+    along_z = lax.all_to_all(copies, "blk", 0, 0, axis_index_groups=LINES)
     own = [along_z] + [moved(along_z, dx=d) for d in range(1, NX)]
     parts = own + [moved(part, dc=1) for part in own]
 
-    terms = out_terms(place, out_index, cotangent, act_own, moved(act_own, dc=1))
-    out_grad = lax.psum_scatter(terms, "smp", scatter_dimension=0, tiled=True)
-
-    mine, *away = in_terms(place, in_index, encodings, parts)
-    in_grad = sum((moved_smp(a, d + 1).astype(F32) for d, a in enumerate(away)), mine)
-    return (out_grad, in_grad.astype(BF16))
+    away, mine = in_terms(place, in_index, encodings, parts)
+    away = away.reshape(NY, *mine.shape)
+    away = lax.all_to_all(away, "smp", 0, 0)
+    in_grad = sum_parts(away, mine, place[3]).astype(BF16)
+    return (out_grad, in_grad)
 
 
 def solution(mesh):

time: 201 us -> 187 us (0.930)
  starting transfers between devices: 62.6 us -> 33.7 us
  blocking collectives: 0 us -> 20.1 us
  Pallas kernels: 43.7 us -> 27 us
  waiting for transfers between devices: 69.1 us -> 83.5 us
    ppermute x29 -> x15, starting transfers between devices: 57.5 us -> 25.6 us  [moved(): return lax.ppermute(value, 'blk', pairs)]
    all_to_all x0 -> x2, waiting for transfers between devices: none -> 31.1 us  [the longest x1 17.9 us: per_device(): got = lax.all_to_all(by_z, 'blk', 0, 0, axis_index_groups=LINES)]
    all_to_all x0 -> x1, blocking collectives: none -> 20.1 us  [per_device(): along_z = lax.all_to_all(copies, 'blk', 0, 0, axis_index_groups=LINES)]
    ppermute x3 -> x0, waiting for transfers between devices: 9.5 us -> none  [moved_smp(): return lax.ppermute(value, 'smp', [(i, (i + dy) % NY) for i in range(NY)])]
    ppermute x29 -> x15, waiting for transfers between devices: 59.6 us -> 50.3 us  [moved(): return lax.ppermute(value, 'blk', pairs)]
    all_to_all x0 -> x2, starting transfers between devices: none -> 8.01 us  [the longest x1 4.01 us: per_device(): got = lax.all_to_all(by_z, 'blk', 0, 0, axis_index_groups=LINES)]
    pallas_call x1, Pallas kernels: 7.26 us -> 1.4 us  [core_sums(): pl.pallas_call(core_kernel, grid_spec=pltpu.PrefetchScalarGridSpec(num_sc...]
    ppermute x3 -> x0, starting transfers between devices: 5.06 us -> none  [moved_smp(): return lax.ppermute(value, 'smp', [(i, (i + dy) % NY) for i in range(NY)])]
  transfers between devices with their start and end apart: 34 -> 19, of which waited for: 18 -> 12; matrix products, arithmetic and copies ran while one was open for 1% -> 1% of each run, Pallas kernels for 15% -> 9%
where the time goes in v2:
time: 187 us
  waiting for transfers between devices  83.5 us (45%)
  starting transfers between devices  33.7 us (18%)
  Pallas kernels  27 us (14%)
  blocking collectives  20.1 us (11%)
  between operations  14.2 us (8%)
  local copies, waits for them, and re-layouts  4.8 us (3%)
  other arithmetic  3.43 us (2%)
    ppermute x15, waiting for transfers between devices, moved(): return lax.ppermute(value, 'blk', pairs)  50.3 us
    ppermute x15, starting transfers between devices, moved(): return lax.ppermute(value, 'blk', pairs)  25.6 us
    all_to_all x1, blocking collectives, per_device(): along_z = lax.all_to_all(copies, 'blk', 0, 0, axis_index_groups=LINES)  20.1 us
    all_to_all x1, waiting for transfers between devices, per_device(): got = lax.all_to_all(by_z, 'blk', 0, 0, axis_index_groups=LINES)  17.9 us
    all_to_all x1, waiting for transfers between devices, per_device(): away = lax.all_to_all(away, 'smp', 0, 0)  13.1 us
    pallas_call x1, Pallas kernels, hidden_sums(): pl.pallas_call(hidden_kernel, grid_spec=pltpu.PrefetchScalarGridSpec(num_...  11.1 us
    pallas_call x1, Pallas kernels, out_terms(): pl.pallas_call(out_kernel, grid_spec=pltpu.PrefetchScalarGridSpec(num_sca...  10.4 us
    unnamed x15, local copies, waits for them, and re-layouts  4.52 us
  transfers between devices with their start and end apart: 19, of which 12 were waited for; matrix products, arithmetic and copies ran while one was open for 1% of the time, Pallas kernels for 9%

profile of v2, /device:TPU:1, one launch (start us, length us, event | category | flops | bytes accessed | tf_op | source)
XLA Modules:
  0.0 186.8 jit_solution(17544571820979694970)
XLA Ops:
  8.2 2.1 %collective-permute-start = (bf16[128,256]{1,0:T(8,128)(2,1)S(1)}, bf16[128,256]{1,0:T(8,128)(2,1)S(1)}, u32[]{:S(2)}, u32[]{:S(2)}) collective-permute-start(bf16[128,256]{1,0:T(8,128)(2,1)S(1)} %fusion.8.refs_0_), channel_id=1, source_target_pairs={{0,64},{4,68},{8,72},{12,76},{16,80},{20,84},{24,88},{28,92},{32,9... | collective-permute-start | bytes 196616 | tf_op jit(solution)/shard_map/ppermute | solution.py:28
  10.3 2.5 %collective-permute-start.1 = (bf16[128,256]{1,0:T(8,128)(2,1)S(1)}, bf16[128,256]{1,0:T(8,128)(2,1)S(1)}, u32[]{:S(2)}, u32[]{:S(2)}) collective-permute-start(bf16[128,256]{1,0:T(8,128)(2,1)S(1)} %fusion.8.refs_0_), channel_id=1, source_target_pairs={{0,128},{4,132},{8,136},{12,140},{16,144},{20,148},{24,152},{28,15... | collective-permute-start | bytes 196616 | tf_op jit(solution)/shard_map/ppermute | solution.py:28
  12.8 1.2 collective-permute-start.2
  14.6 11.1 %hidden_sums.1 = (bf16[32,256,128]{2,1,0:T(8,128)(2,1)}, f32[32,256,128]{2,1,0:T(8,128)}) custom-call(s32[4]{0:T(128)} %pad_add_fusion.place, s32[2,84]{1,0:T(2,128)} %bitcast.22, bf16[256,10752]{1,0:T(8,128)(2,1)} %cot_ref.3, bf16[168,128,128]{2,1,0:T(8,128)(2,1)} %weight_ref.1), custom_call_target="tpu_custom_call" | custom-call | flops 3000000000 | bytes 16777216 | tf_op jit(solution)/shard_map/hidden_sums/pallas_call | solution.py:84
  25.7 1.6 pad_maximum_fusion.refs_1_
  27.4 1.6 collective-permute-start.3
  29.0 4.0 %collective-permute-done.3 = bf16[32,256,128]{2,1,0:T(8,128)(2,1)S(1)} collective-permute-done((bf16[32,256,128]{2,1,0:T(8,128)(2,1)}, bf16[32,256,128]{2,1,0:T(8,128)(2,1)S(1)}, u32[]{:S(2)}, u32[]{:S(2)}) %collective-permute-start.3) | collective-permute-done | bytes 2097184 | tf_op jit(solution)/shard_map/ppermute | solution.py:28
  33.0 2.2 %copy-done = f32[32,256,128]{2,1,0:T(8,128)S(1)} copy-done((f32[32,256,128]{2,1,0:T(8,128)S(1)}, f32[32,256,128]{2,1,0:T(8,128)}, u32[]{:S(2)}) %copy-start) | copy-done | bytes 4194328
  35.2 1.4 core_sums.1
  37.0 1.7 collective-permute-start.5
  38.7 2.0 %collective-permute-start.6 = (bf16[8,256,128]{2,1,0:T(8,128)(2,1)S(1)}, bf16[8,256,128]{2,1,0:T(8,128)(2,1)S(1)}, u32[]{:S(2)}, u32[]{:S(2)}) collective-permute-start(bf16[8,256,128]{2,1,0:T(8,128)(2,1)S(1)} %get-tuple-element.17), channel_id=1, source_target_pairs={{0,192},{4,196},{8,200},{12,204},{16,208},{20,212},{24,216},{28,22... | collective-permute-start | bytes 1572872 | tf_op jit(solution)/shard_map/ppermute | solution.py:28
  40.7 10.7 %collective-permute-done.4.a_ref = bf16[8,256,128]{2,1,0:T(8,128)(2,1)S(1)} collective-permute-done((bf16[8,256,128]{2,1,0:T(8,128)(2,1)S(1)}, bf16[8,256,128]{2,1,0:T(8,128)(2,1)S(1)}, u32[]{:S(2)}, u32[]{:S(2)}) %collective-permute-start.4) | collective-permute-done | bytes 524320 | tf_op jit(solution)/shard_map/ppermute | solution.py:28
  51.4 10.5 %collective-permute-done.5.b_ref = bf16[8,256,128]{2,1,0:T(8,128)(2,1)S(1)} collective-permute-done((bf16[8,256,128]{2,1,0:T(8,128)(2,1)S(1)}, bf16[8,256,128]{2,1,0:T(8,128)(2,1)S(1)}, u32[]{:S(2)}, u32[]{:S(2)}) %collective-permute-start.5) | collective-permute-done | bytes 524320 | tf_op jit(solution)/shard_map/ppermute | solution.py:28
  62.5 1.6 line_sums.1
  64.1 2.1 %all-gather.3.cloned.1.call-done.refs_0_ = bf16[32,128,256]{2,1,0:T(8,128)(2,1)} async-done(((bf16[4,128,256]{2,1,0:T(8,128)(2,1)}), bf16[32,128,256]{2,1,0:T(8,128)(2,1)}) %all-gather.3.cloned.1.call-update) | async-done | bytes 2097168 | tf_op jit(solution)/shard_map/all_gather | solution.py:287
  66.2 4.6 %collective-permute-start.7 = (bf16[32,128,256]{2,1,0:T(8,128)(2,1)}, bf16[32,128,256]{2,1,0:T(8,128)(2,1)S(1)}, u32[]{:S(2)}, u32[]{:S(2)}) collective-permute-start(bf16[32,128,256]{2,1,0:T(8,128)(2,1)} %after.5.own_ref), channel_id=1, source_target_pairs={{0,4},{4,0},{8,12},{12,8},{16,20},{20,16},{24,28},{28,24},{32,36},... | collective-permute-start | bytes 6291464 | tf_op jit(solution)/shard_map/ppermute | solution.py:28
  70.9 4.0 %collective-permute-done.7.other_ref = bf16[32,128,256]{2,1,0:T(8,128)(2,1)S(1)} collective-permute-done((bf16[32,128,256]{2,1,0:T(8,128)(2,1)}, bf16[32,128,256]{2,1,0:T(8,128)(2,1)S(1)}, u32[]{:S(2)}, u32[]{:S(2)}) %collective-permute-start.7) | collective-permute-done | bytes 2097184 | tf_op jit(solution)/shard_map/ppermute | solution.py:28
  74.9 1.4 copy-done.5
  76.2 10.4 %out_terms.1 = bf16[168,128,128]{2,1,0:T(8,128)(2,1)} custom-call(s32[4]{0:T(128)} %pad_add_fusion.place, s32[2,84]{1,0:T(2,128)} %bitcast.23, bf16[256,10752]{1,0:T(8,128)(2,1)} %cot_ref.3, bf16[32,128,256]{2,1,0:T(8,128)(2,1)} %after.5.own_ref, bf16[32,128,256]{2,1,0:T(8,128)(2,1)} %copy-done.5), custom_call_target="tpu_custom_call" | custom-call | flops 3000000000 | bytes 16777216 | tf_op jit(solution)/shard_map/out_terms/pallas_call | solution.py:191
  86.7 4.0 %all-to-all-start = ((bf16[8,256,128]{2,1,0:T(8,128)(2,1)}), bf16[8,256,128]{2,1,0:T(8,128)(2,1)S(1)}, u32[]{:S(2)}, u32[]{:S(2)}) async-start(bf16[8,256,128]{2,1,0:T(8,128)(2,1)} %get-tuple-element.18.refs_1_), calls=%async_computation.1 | async-start | bytes 1048576 | tf_op jit(solution)/shard_map/all_to_all | solution.py:292
  90.7 17.9 %all-to-all-done = bf16[8,256,128]{2,1,0:T(8,128)(2,1)S(1)} async-done(((bf16[8,256,128]{2,1,0:T(8,128)(2,1)}), bf16[8,256,128]{2,1,0:T(8,128)(2,1)S(1)}, u32[]{:S(2)}, u32[]{:S(2)}) %all-to-all-start) | async-done | bytes 524320 | tf_op jit(solution)/shard_map/all_to_all | solution.py:292
  109.2 20.1 %all_to_all.15.refs_0_ = bf16[8,256,128]{2,1,0:T(8,128)(2,1)S(1)} all-to-all(bf16[8,256,128]{2,1,0:T(8,128)(2,1)S(1)} %broadcast_in_dim.22), channel_id=1, replica_groups={{0,8,16,24,32,40,48,56},{4,12,20,28,36,44,52,60},{64,72,80,88,96,104,11..., dimensions={0} | all-to-all | bytes 1048576 | tf_op jit(solution)/shard_map/all_to_all | solution.py:300
  130.4 2.5 %collective-permute-start.9 = (bf16[8,256,128]{2,1,0:T(8,128)(2,1)S(1)}, bf16[8,256,128]{2,1,0:T(8,128)(2,1)S(1)}, u32[]{:S(2)}, u32[]{:S(2)}) collective-permute-start(bf16[8,256,128]{2,1,0:T(8,128)(2,1)S(1)} %all_to_all.15.refs_0_), channel_id=1, source_target_pairs={{0,128},{4,132},{8,136},{12,140},{16,144},{20,148},{24,152},{28,15... | collective-permute-start | bytes 1572872 | tf_op jit(solution)/shard_map/ppermute | solution.py:28
  134.0 1.6 collective-permute-start.11
  135.6 7.8 %collective-permute-done.8.refs_1_ = bf16[8,256,128]{2,1,0:T(8,128)(2,1)S(1)} collective-permute-done((bf16[8,256,128]{2,1,0:T(8,128)(2,1)S(1)}, bf16[8,256,128]{2,1,0:T(8,128)(2,1)S(1)}, u32[]{:S(2)}, u32[]{:S(2)}) %collective-permute-start.8) | collective-permute-done | bytes 524320 | tf_op jit(solution)/shard_map/ppermute | solution.py:28
  143.4 1.7 collective-permute-start.12
  145.2 10.3 %collective-permute-done.9.refs_2_ = bf16[8,256,128]{2,1,0:T(8,128)(2,1)S(1)} collective-permute-done((bf16[8,256,128]{2,1,0:T(8,128)(2,1)S(1)}, bf16[8,256,128]{2,1,0:T(8,128)(2,1)S(1)}, u32[]{:S(2)}, u32[]{:S(2)}) %collective-permute-start.9) | collective-permute-done | bytes 524320 | tf_op jit(solution)/shard_map/ppermute | solution.py:28
  155.5 1.6 collective-permute-start.13
  157.1 1.5 collective-permute-done.13.refs_6_
  159.4 2.6 %in_terms.1 = (bf16[28,128,128]{2,1,0:T(8,128)(2,1)}, f32[7,128,128]{2,1,0:T(8,128)S(1)}) custom-call(s32[4]{0:T(128)S(1)} %copy-done.3, s32[4,7]{1,0:T(4,128)S(1)} %bitcast.17, bf16[256,896]{1,0:T(8,128)(2,1)S(1)} %copy-done.1, bf16[8,256,128]{2,1,0:T(8,128)(2,1)S(1)} %all_to_all.15.refs_0_, bf16[8,256,128]{2,1,0:T(8,128)(2,1)S(1)} %collective-permute-done.8.refs_1_, ...), custom_call_target="tpu_custom_call" | custom-call | flops 500000000 | bytes 8388608 | tf_op jit(solution)/shard_map/in_terms/pallas_call | solution.py:244
  161.9 4.0 %all-to-all-start.2 = ((bf16[4,7,128,128]{3,2,1,0:T(8,128)(2,1)}), bf16[4,7,128,128]{3,2,1,0:T(8,128)(2,1)S(1)}, u32[]{:S(2)}, u32[]{:S(2)}) async-start(bf16[4,7,128,128]{3,2,1,0:T(8,128)(2,1)} %bitcast.13), calls=%async_computation.3 | async-start | bytes 1835008 | tf_op jit(solution)/shard_map/all_to_all | solution.py:306
  165.9 13.1 %all-to-all-done.2 = bf16[4,7,128,128]{3,2,1,0:T(8,128)(2,1)S(1)} async-done(((bf16[4,7,128,128]{3,2,1,0:T(8,128)(2,1)}), bf16[4,7,128,128]{3,2,1,0:T(8,128)(2,1)S(1)}, u32[]{:S(2)}, u32[]{:S(2)}) %all-to-all-start.2) | async-done | bytes 917536 | tf_op jit(solution)/shard_map/all_to_all | solution.py:306
  (43 shorter events, 7.1 us)
Async XLA Ops:
  7.2 59.1 %all-gather.3.cloned.1.call-start = ((), (), s32[]{:S(2)}) async-start(), calls=%async_computation.5 | async-start | bytes 2359296 | tf_op jit(solution)/shard_map/all_gather | solution.py:287
  8.2 17.5 %copy-start.6 = (bf16[128,256]{1,0:T(8,128)(2,1)}, bf16[128,256]{1,0:T(8,128)(2,1)S(1)}, u32[]{:S(2)}) copy-start(bf16[128,256]{1,0:T(8,128)(2,1)S(1)} %fusion.8.refs_0_) | copy-start | bytes 196612
  8.2 17.4 %collective-permute-start = (bf16[128,256]{1,0:T(8,128)(2,1)S(1)}, bf16[128,256]{1,0:T(8,128)(2,1)S(1)}, u32[]{:S(2)}, u32[]{:S(2)}) collective-permute-start(bf16[128,256]{1,0:T(8,128)(2,1)S(1)} %fusion.8.refs_0_), channel_id=1, source_target_pairs={{0,64},{4,68},{8,72},{12,76},{16,80},{20,84},{24,88},{28,92},{32,9... | collective-permute-start | bytes 196616 | tf_op jit(solution)/shard_map/ppermute | solution.py:28
  10.3 15.3 %collective-permute-start.1 = (bf16[128,256]{1,0:T(8,128)(2,1)S(1)}, bf16[128,256]{1,0:T(8,128)(2,1)S(1)}, u32[]{:S(2)}, u32[]{:S(2)}) collective-permute-start(bf16[128,256]{1,0:T(8,128)(2,1)S(1)} %fusion.8.refs_0_), channel_id=1, source_target_pairs={{0,128},{4,132},{8,136},{12,140},{16,144},{20,148},{24,152},{28,15... | collective-permute-start | bytes 196616 | tf_op jit(solution)/shard_map/ppermute | solution.py:28
  12.8 12.9 %collective-permute-start.2 = (bf16[128,256]{1,0:T(8,128)(2,1)S(1)}, bf16[128,256]{1,0:T(8,128)(2,1)S(1)}, u32[]{:S(2)}, u32[]{:S(2)}) collective-permute-start(bf16[128,256]{1,0:T(8,128)(2,1)S(1)} %fusion.8.refs_0_), channel_id=1, source_target_pairs={{0,192},{4,196},{8,200},{12,204},{16,208},{20,212},{24,216},{28,22... | collective-permute-start | bytes 196616 | tf_op jit(solution)/shard_map/ppermute | solution.py:28
  27.3 5.7 %copy-start.2 = (s32[4]{0:T(128)S(1)}, s32[4]{0:T(128)}, u32[]{:S(2)}) copy-start(s32[4]{0:T(128)} %pad_add_fusion.place) | copy-start | bytes 52
  27.3 152.7 %reduce-scatter.2.cloned.1.call-start = ((), (), s32[]{:S(2)}) async-start(), calls=%async_computation.4 | async-start | bytes 6881280 | tf_op jit(solution)/shard_map/reduce_scatter | solution.py:297
  27.4 5.6 %collective-permute-start.3 = (bf16[32,256,128]{2,1,0:T(8,128)(2,1)}, bf16[32,256,128]{2,1,0:T(8,128)(2,1)S(1)}, u32[]{:S(2)}, u32[]{:S(2)}) collective-permute-start(bf16[32,256,128]{2,1,0:T(8,128)(2,1)} %after.4), channel_id=1, source_target_pairs={{0,4},{4,0},{8,12},{12,8},{16,20},{20,16},{24,28},{28,24},{32,36},... | collective-permute-start | bytes 6291464 | tf_op jit(solution)/shard_map/ppermute | solution.py:28
  33.0 2.2 %copy-start = (f32[32,256,128]{2,1,0:T(8,128)S(1)}, f32[32,256,128]{2,1,0:T(8,128)}, u32[]{:S(2)}) copy-start(f32[32,256,128]{2,1,0:T(8,128)} %get-tuple-element.13) | copy-start | bytes 12582916
  36.6 14.8 %collective-permute-start.4 = (bf16[8,256,128]{2,1,0:T(8,128)(2,1)S(1)}, bf16[8,256,128]{2,1,0:T(8,128)(2,1)S(1)}, u32[]{:S(2)}, u32[]{:S(2)}) collective-permute-start(bf16[8,256,128]{2,1,0:T(8,128)(2,1)S(1)} %get-tuple-element.15), channel_id=1, source_target_pairs={{0,64},{4,68},{8,72},{12,76},{16,80},{20,84},{24,88},{28,92},{32,9... | collective-permute-start | bytes 1572872 | tf_op jit(solution)/shard_map/ppermute | solution.py:28
  37.0 24.9 %collective-permute-start.5 = (bf16[8,256,128]{2,1,0:T(8,128)(2,1)S(1)}, bf16[8,256,128]{2,1,0:T(8,128)(2,1)S(1)}, u32[]{:S(2)}, u32[]{:S(2)}) collective-permute-start(bf16[8,256,128]{2,1,0:T(8,128)(2,1)S(1)} %get-tuple-element.16), channel_id=1, source_target_pairs={{0,128},{4,132},{8,136},{12,140},{16,144},{20,148},{24,152},{28,15... | collective-permute-start | bytes 1572872 | tf_op jit(solution)/shard_map/ppermute | solution.py:28
  38.7 23.8 %collective-permute-start.6 = (bf16[8,256,128]{2,1,0:T(8,128)(2,1)S(1)}, bf16[8,256,128]{2,1,0:T(8,128)(2,1)S(1)}, u32[]{:S(2)}, u32[]{:S(2)}) collective-permute-start(bf16[8,256,128]{2,1,0:T(8,128)(2,1)S(1)} %get-tuple-element.17), channel_id=1, source_target_pairs={{0,192},{4,196},{8,200},{12,204},{16,208},{20,212},{24,216},{28,22... | collective-permute-start | bytes 1572872 | tf_op jit(solution)/shard_map/ppermute | solution.py:28
  66.2 8.6 %collective-permute-start.7 = (bf16[32,128,256]{2,1,0:T(8,128)(2,1)}, bf16[32,128,256]{2,1,0:T(8,128)(2,1)S(1)}, u32[]{:S(2)}, u32[]{:S(2)}) collective-permute-start(bf16[32,128,256]{2,1,0:T(8,128)(2,1)} %after.5.own_ref), channel_id=1, source_target_pairs={{0,4},{4,0},{8,12},{12,8},{16,20},{20,16},{24,28},{28,24},{32,36},... | collective-permute-start | bytes 6291464 | tf_op jit(solution)/shard_map/ppermute | solution.py:28
  74.9 1.4 copy-start.5
  86.7 72.7 %copy-start.1 = (bf16[256,896]{1,0:T(8,128)(2,1)S(1)}, bf16[256,896]{1,0:T(8,128)(2,1)}, u32[]{:S(2)}) copy-start(bf16[256,896]{1,0:T(8,128)(2,1)} %enc_ref.1) | copy-start | bytes 1376260
  86.7 72.7 %copy-start.3 = (s32[4]{0:T(128)S(1)}, s32[4]{0:T(128)}, u32[]{:S(2)}) copy-start(s32[4]{0:T(128)} %pad_add_fusion.place) | copy-start | bytes 52
  86.7 72.7 %copy-start.4 = (s32[7,4]{0,1:T(4,128)S(1)}, s32[7,4]{0,1:T(4,128)}, u32[]{:S(2)}) copy-start(s32[7,4]{0,1:T(4,128)} %param.11) | copy-start | bytes 340
  86.7 22.0 %all-to-all-start = ((bf16[8,256,128]{2,1,0:T(8,128)(2,1)}), bf16[8,256,128]{2,1,0:T(8,128)(2,1)S(1)}, u32[]{:S(2)}, u32[]{:S(2)}) async-start(bf16[8,256,128]{2,1,0:T(8,128)(2,1)} %get-tuple-element.18.refs_1_), calls=%async_computation.1 | async-start | bytes 1048576 | tf_op jit(solution)/shard_map/all_to_all | solution.py:292
  129.3 14.1 %collective-permute-start.8 = (bf16[8,256,128]{2,1,0:T(8,128)(2,1)S(1)}, bf16[8,256,128]{2,1,0:T(8,128)(2,1)S(1)}, u32[]{:S(2)}, u32[]{:S(2)}) collective-permute-start(bf16[8,256,128]{2,1,0:T(8,128)(2,1)S(1)} %all_to_all.15.refs_0_), channel_id=1, source_target_pairs={{0,64},{4,68},{8,72},{12,76},{16,80},{20,84},{24,88},{28,92},{32,9... | collective-permute-start | bytes 1572872 | tf_op jit(solution)/shard_map/ppermute | solution.py:28
  130.4 25.1 %collective-permute-start.9 = (bf16[8,256,128]{2,1,0:T(8,128)(2,1)S(1)}, bf16[8,256,128]{2,1,0:T(8,128)(2,1)S(1)}, u32[]{:S(2)}, u32[]{:S(2)}) collective-permute-start(bf16[8,256,128]{2,1,0:T(8,128)(2,1)S(1)} %all_to_all.15.refs_0_), channel_id=1, source_target_pairs={{0,128},{4,132},{8,136},{12,140},{16,144},{20,148},{24,152},{28,15... | collective-permute-start | bytes 1572872 | tf_op jit(solution)/shard_map/ppermute | solution.py:28
  133.0 24.1 %collective-permute-start.10 = (bf16[8,256,128]{2,1,0:T(8,128)(2,1)S(1)}, bf16[8,256,128]{2,1,0:T(8,128)(2,1)S(1)}, u32[]{:S(2)}, u32[]{:S(2)}) collective-permute-start(bf16[8,256,128]{2,1,0:T(8,128)(2,1)S(1)} %all_to_all.15.refs_0_), channel_id=1, source_target_pairs={{0,192},{4,196},{8,200},{12,204},{16,208},{20,212},{24,216},{28,22... | collective-permute-start | bytes 1572872 | tf_op jit(solution)/shard_map/ppermute | solution.py:28
  134.0 23.1 %collective-permute-start.11 = (bf16[8,256,128]{2,1,0:T(8,128)(2,1)S(1)}, bf16[8,256,128]{2,1,0:T(8,128)(2,1)S(1)}, u32[]{:S(2)}, u32[]{:S(2)}) collective-permute-start(bf16[8,256,128]{2,1,0:T(8,128)(2,1)S(1)} %all_to_all.15.refs_0_), channel_id=1, source_target_pairs={{0,4},{4,0},{8,12},{12,8},{16,20},{20,16},{24,28},{28,24},{32,36},... | collective-permute-start | bytes 1572872 | tf_op jit(solution)/shard_map/ppermute | solution.py:28
  143.4 13.7 %collective-permute-start.12 = (bf16[8,256,128]{2,1,0:T(8,128)(2,1)S(1)}, bf16[8,256,128]{2,1,0:T(8,128)(2,1)S(1)}, u32[]{:S(2)}, u32[]{:S(2)}) collective-permute-start(bf16[8,256,128]{2,1,0:T(8,128)(2,1)S(1)} %collective-permute-done.8.refs_1_), channel_id=1, source_target_pairs={{0,4},{4,0},{8,12},{12,8},{16,20},{20,16},{24,28},{28,24},{32,36},... | collective-permute-start | bytes 1572872 | tf_op jit(solution)/shard_map/ppermute | solution.py:28
  155.5 3.1 %collective-permute-start.13 = (bf16[8,256,128]{2,1,0:T(8,128)(2,1)S(1)}, bf16[8,256,128]{2,1,0:T(8,128)(2,1)S(1)}, u32[]{:S(2)}, u32[]{:S(2)}) collective-permute-start(bf16[8,256,128]{2,1,0:T(8,128)(2,1)S(1)} %collective-permute-done.9.refs_2_), channel_id=1, source_target_pairs={{0,4},{4,0},{8,12},{12,8},{16,20},{20,16},{24,28},{28,24},{32,36},... | collective-permute-start | bytes 1572872 | tf_op jit(solution)/shard_map/ppermute | solution.py:28
  157.1 2.3 %collective-permute-start.14 = (bf16[8,256,128]{2,1,0:T(8,128)(2,1)S(1)}, bf16[8,256,128]{2,1,0:T(8,128)(2,1)S(1)}, u32[]{:S(2)}, u32[]{:S(2)}) collective-permute-start(bf16[8,256,128]{2,1,0:T(8,128)(2,1)S(1)} %collective-permute-done.10.refs_3_), channel_id=1, source_target_pairs={{0,4},{4,0},{8,12},{12,8},{16,20},{20,16},{24,28},{28,24},{32,36},... | collective-permute-start | bytes 1572872 | tf_op jit(solution)/shard_map/ppermute | solution.py:28
  161.9 17.1 %all-to-all-start.2 = ((bf16[4,7,128,128]{3,2,1,0:T(8,128)(2,1)}), bf16[4,7,128,128]{3,2,1,0:T(8,128)(2,1)S(1)}, u32[]{:S(2)}, u32[]{:S(2)}) async-start(bf16[4,7,128,128]{3,2,1,0:T(8,128)(2,1)} %bitcast.13), calls=%async_computation.3 | async-start | bytes 1835008 | tf_op jit(solution)/shard_map/all_to_all | solution.py:306
Sparse Core Ops, SparseCore 0:
  27.4 38.7 all-gather.2
  86.8 58.1 reduce-scatter.1

commit v3 on v2

--- a/solution.py
+++ b/solution.py
@@ -12,6 +12,7 @@
 STEP_BLOCKS = 28
 OUT_STEP = 28
 CORE_STEP = 2
+FIRST, LAST = 176, 80
 
 
 def index_of(x, z, core):
@@ -41,12 +42,14 @@
 
 def after(value, other):
     anywhere = pl.BlockSpec(memory_space=pl.ANY)
+    other = other[(0,) * (other.ndim - 2)][:16]
     return pl.pallas_call(
         lambda *refs: None,
         in_specs=[anywhere, anywhere],
         out_specs=anywhere,
         out_shape=jax.ShapeDtypeStruct(value.shape, value.dtype),
         input_output_aliases={0: 0},
+        compiler_params=params(56),
         name="after",
     )(value, other)
 
@@ -107,11 +110,24 @@
 
 
 def core_kernel(place, keep_ref, got_ref, *outs):
-    x = place[0]
-    for d in range(NX):
-        at = (x + d) & (NX - 1)
-        for n in range(CORE_STEP):
-            outs[d][n] = (keep_ref[at, n] + got_ref[at, n].astype(F32)).astype(outs[d].dtype)
+    x, z = place[0], place[1]
+    step = pl.program_id(0)
+    z_send, z_own = outs[NX:]
+
+    def last(at, n):
+        return keep_ref[at, n, FIRST:] + got_ref[at, n, FIRST:].astype(F32)
+
+    for n in range(CORE_STEP):
+        for d in range(NX):
+            at = (x + d) & (NX - 1)
+            total = keep_ref[at, n, :FIRST] + got_ref[at, n, :FIRST].astype(F32)
+            outs[d][n] = total.astype(outs[d].dtype)
+            z_send[n, d] = last(d, n).astype(BF16)
+
+        @pl.when(step * CORE_STEP + n == z)
+        def _():
+            for d in range(NX):
+                z_own[d] = last(d, n)
 
 
 def core_sums(place, keep, got):
@@ -123,10 +139,18 @@
             num_scalar_prefetch=1,
             grid=(NZ // CORE_STEP,),
             in_specs=[spec, spec],
-            out_specs=[pl.BlockSpec((CORE_STEP, rows, BS), lambda g, *_: (g, 0, 0))] * NX,
+            out_specs=[pl.BlockSpec((CORE_STEP, FIRST, BS), lambda g, *_: (g, 0, 0))] * NX
+            + [
+                pl.BlockSpec((CORE_STEP, NX, LAST, BS), lambda g, *_: (g, 0, 0, 0)),
+                pl.BlockSpec((NX, LAST, BS), lambda g, *_: (0, 0, 0)),
+            ],
         ),
         out_shape=[
-            jax.ShapeDtypeStruct((NZ, rows, BS), BF16 if d else F32) for d in range(NX)
+            jax.ShapeDtypeStruct((NZ, FIRST, BS), BF16 if d else F32) for d in range(NX)
+        ]
+        + [
+            jax.ShapeDtypeStruct((NZ, NX, LAST, BS), BF16),
+            jax.ShapeDtypeStruct((NX, LAST, BS), F32),
         ],
         compiler_params=params(16),
         cost_estimate=pl.CostEstimate(flops=10**6, bytes_accessed=2**23, transcendentals=0),
@@ -144,20 +168,42 @@
 
 
 def line_sums(place, keep, *got):
-    rows = keep.shape[1]
     whole = pl.BlockSpec(memory_space=pltpu.VMEM)
     return pl.pallas_call(
         line_kernel,
         in_specs=[pl.BlockSpec(memory_space=pltpu.SMEM)] + [whole] * NX,
         out_specs=[whole] * 2,
         out_shape=[
-            jax.ShapeDtypeStruct((NZ, rows, BS), BF16),
-            jax.ShapeDtypeStruct((rows, BS), F32),
+            jax.ShapeDtypeStruct((NZ, FIRST, BS), BF16),
+            jax.ShapeDtypeStruct((FIRST, BS), F32),
         ],
         compiler_params=params(8),
         cost_estimate=pl.CostEstimate(flops=10**6, bytes_accessed=2**22, transcendentals=0),
         name="line_sums",
     )(place, keep, *got)
+
+
+def plane_kernel(place, own_ref, got_ref, *outs):
+    x, z = place[0], place[1]
+    for d in range(NX):
+        at = (x + d) & (NX - 1)
+        total = own_ref[at]
+        for n in range(NZ):
+            total += jnp.where(z == n, 0.0, got_ref[n, at].astype(F32))
+        outs[d][...] = total.astype(outs[d].dtype)
+
+
+def plane_sums(place, own, got):
+    whole = pl.BlockSpec(memory_space=pltpu.VMEM)
+    return pl.pallas_call(
+        plane_kernel,
+        in_specs=[pl.BlockSpec(memory_space=pltpu.SMEM), whole, whole],
+        out_specs=[whole] * NX,
+        out_shape=[jax.ShapeDtypeStruct((LAST, BS), BF16 if d else F32) for d in range(NX)],
+        compiler_params=params(8),
+        cost_estimate=pl.CostEstimate(flops=10**6, bytes_accessed=2**20, transcendentals=0),
+        name="plane_sums",
+    )(place, own, got)
 
 
 def out_kernel(place, contacts, cot_ref, own_ref, other_ref, out_ref, held, sems):
@@ -212,11 +258,16 @@
 
 
 def in_kernel(place, contacts, enc_ref, *refs):
-    parts, (send_ref, mine_ref, held, made, sems) = refs[: NC * NX], refs[NC * NX :]
+    firsts, lasts = refs[: NC * NX], refs[NC * NX : NC * NX + NC]
+    send_ref, mine_ref, held, made, sems = refs[NC * NX + NC :]
     x, core, y = place[0], place[2], place[3]
-    copies = [
-        pltpu.make_async_copy(part, held.at[n], sems.at[n]) for n, part in enumerate(parts)
-    ]
+    copies = []
+    for n, first in enumerate(firsts):
+        last = lasts[n // NX].at[:, n % NX]
+        copies += [
+            pltpu.make_async_copy(first, held.at[n, :, pl.ds(0, FIRST)], sems.at[n, 0]),
+            pltpu.make_async_copy(last, held.at[n, :, pl.ds(FIRST, LAST)], sems.at[n, 1]),
+        ]
     for copy in copies:
         copy.start()
     for copy in copies:
@@ -243,12 +294,12 @@
     whole = pl.BlockSpec(memory_space=pltpu.VMEM)
     return pl.pallas_call(
         in_kernel,
-        in_specs=[smem, smem, whole] + [pl.BlockSpec(memory_space=pl.ANY)] * (NC * NX),
+        in_specs=[smem, smem, whole] + [pl.BlockSpec(memory_space=pl.ANY)] * (NC * NX + NC),
         out_specs=[whole] * 2,
         scratch_shapes=[
             pltpu.VMEM((NC * NX, NZ, rows, BS), BF16),
             pltpu.VMEM((per_in * count, BS, BS), F32),
-            pltpu.SemaphoreType.DMA((NC * NX,)),
+            pltpu.SemaphoreType.DMA((NC * NX, 2)),
         ],
         out_shape=[
             jax.ShapeDtypeStruct((per_in * count, BS, BS), BF16),
@@ -287,19 +338,33 @@
     act_own = lax.all_gather(along_x, "blk", axis_index_groups=LINES)
     act_own = act_own.reshape(NZ * NX, BS, -1)
 
-    by_x = core_sums(place, keep, moved(send, dc=1))
-    by_z, own_z = line_sums(place, by_x[0], *[moved(by_x[d], dx=d) for d in range(1, NX)])
-    got = lax.all_to_all(by_z, "blk", 0, 0, axis_index_groups=LINES)
-    grad_pre = (sum_parts(got, own_z, place[1]) * silu_slope(pre)).astype(BF16)
+    *by_x, by_plane, own_plane = core_sums(place, keep, moved(send, dc=1))
+    from_x = [moved(by_x[d], dx=d) for d in range(1, NX)]
+    from_z = lax.all_to_all(by_plane, "blk", 0, 0, axis_index_groups=LINES)
+    last_own, *last_x = plane_sums(place, own_plane, from_z)
+    by_z, own_z = line_sums(place, after(by_x[0], last_own), *from_x)
+    got_z = lax.all_to_all(by_z, "blk", 0, 0, axis_index_groups=LINES)
+    got_x = [moved(part, dx=d + 1) for d, part in enumerate(last_x)]
 
     act_own = after(act_own, by_z)
     terms = out_terms(place, out_index, cotangent, act_own, moved(act_own, dc=1))
+    both = got_z[0, :16] + terms[0, :16]
+    terms = after(terms, both)
     out_grad = lax.psum_scatter(terms, "smp", scatter_dimension=0, tiled=True)
 
-    copies = jnp.broadcast_to(grad_pre, (NZ, *grad_pre.shape))
+    slope = silu_slope(pre)
+    grad_act = sum_parts(got_z, after(own_z, both), place[1])
+    first = (grad_act * slope[:FIRST]).astype(BF16)
+    grad_act = sum((part.astype(F32) for part in got_x), last_own)
+    last = (grad_act * slope[FIRST:]).astype(BF16)
+
+    copies = jnp.broadcast_to(first, (NZ, *first.shape))
     along_z = lax.all_to_all(copies, "blk", 0, 0, axis_index_groups=LINES)
+    last_x = jnp.stack([last] + [moved(last, dx=d) for d in range(1, NX)])
     own = [along_z] + [moved(along_z, dx=d) for d in range(1, NX)]
-    parts = own + [moved(part, dc=1) for part in own]
+    copies = jnp.broadcast_to(last_x, (NZ, *last_x.shape))
+    last_own = lax.all_to_all(copies, "blk", 0, 0, axis_index_groups=LINES)
+    parts = own + [moved(part, dc=1) for part in own] + [last_own, moved(last_own, dc=1)]
 
     away, mine = in_terms(place, in_index, encodings, parts)
     away = away.reshape(NY, *mine.shape)

time: 187 us -> 185 us (0.989)
  starting transfers between devices: 33.7 us -> 56.1 us
  blocking collectives: 20.1 us -> 0 us
  waiting for transfers between devices: 83.5 us -> 67.3 us
  local copies, waits for them, and re-layouts: 4.8 us -> 12.8 us
  Pallas kernels: 27 us -> 29.1 us
    ppermute x15 -> x22, waiting for transfers between devices: 50.3 us -> 11.8 us  [moved(): return lax.ppermute(value, 'blk', pairs)]
    all_to_all x1 -> x4, waiting for transfers between devices: 17.9 us -> 39.3 us  [the longest x1 22.2 us: per_device(): from_z = lax.all_to_all(by_plane, 'blk', 0, 0, axis_index_groups=LINES)]
    all_to_all x1 -> x0, blocking collectives: 20.1 us -> none  [per_device(): along_z = lax.all_to_all(copies, 'blk', 0, 0, axis_index_groups=LINES)]
    all_to_all x1 -> x4, starting transfers between devices: 4.01 us -> 22.4 us  [the longest x1 8.19 us: per_device(): from_z = lax.all_to_all(by_plane, 'blk', 0, 0, axis_index_groups=LINES)]
    slice x0 -> x4, local copies, waits for them, and re-layouts: none -> 4.45 us  [after(): other = other[(0,) * (other.ndim - 2)][:16]]
    ppermute x15 -> x22, starting transfers between devices: 25.6 us -> 29.6 us  [moved(): return lax.ppermute(value, 'blk', pairs)]
    unnamed x15 -> x18, local copies, waits for them, and re-layouts: 4.52 us -> 4.03 us
  transfers between devices with their start and end apart: 19 -> 29, of which waited for: 12 -> 17; matrix products, arithmetic and copies ran while one was open for 1% -> 6% of each run, Pallas kernels for 9% -> 16%
where the time goes in v3:
time: 185 us; the launch traced here: 184 us
  waiting for transfers between devices  67.3 us (36%)
  starting transfers between devices  56.1 us (30%)
  Pallas kernels  29.1 us (16%)
  between operations  14.2 us (8%)
  local copies, waits for them, and re-layouts  12.8 us (7%)
  other arithmetic  4.97 us (3%)
    ppermute x22, starting transfers between devices, moved(): return lax.ppermute(value, 'blk', pairs)  29.6 us
    all_to_all x1, waiting for transfers between devices, per_device(): from_z = lax.all_to_all(by_plane, 'blk', 0, 0, axis_index_groups=LINES)  22.2 us
    all_to_all x1, waiting for transfers between devices, per_device(): last_own = lax.all_to_all(copies, 'blk', 0, 0, axis_index_groups=LINES)  14 us
    all_to_all x1, waiting for transfers between devices, per_device(): away = lax.all_to_all(away, 'smp', 0, 0)  13.1 us
    ppermute x22, waiting for transfers between devices, moved(): return lax.ppermute(value, 'blk', pairs)  11.8 us
    pallas_call x1, Pallas kernels, hidden_sums(): pl.pallas_call(hidden_kernel, grid_spec=pltpu.PrefetchScalarGridSpec(num_...  11.1 us
    pallas_call x1, Pallas kernels, out_terms(): pl.pallas_call(out_kernel, grid_spec=pltpu.PrefetchScalarGridSpec(num_sca...  10.4 us
    all_to_all x1, starting transfers between devices, per_device(): from_z = lax.all_to_all(by_plane, 'blk', 0, 0, axis_index_groups=LINES)  8.19 us
  transfers between devices with their start and end apart: 29, of which 17 were waited for; matrix products, arithmetic and copies ran while one was open for 6% of the time, Pallas kernels for 16%

profile of v3, /device:TPU:1, one launch (start us, length us, event | category | flops | bytes accessed | tf_op | source)
XLA Modules:
  0.0 184.5 jit_solution(16202746322868494994)
XLA Ops:
  8.1 3.4 %collective-permute-start.2 = (bf16[128,256]{0,1:T(8,128)(2,1)S(1)}, bf16[128,256]{0,1:T(8,128)(2,1)S(1)}, u32[]{:S(2)}, u32[]{:S(2)}) collective-permute-start(bf16[128,256]{0,1:T(8,128)(2,1)S(1)} %get-tuple-element.35), channel_id=1, source_target_pairs={{0,192},{4,196},{8,200},{12,204},{16,208},{20,212},{24,216},{28,22... | collective-permute-start | bytes 196616 | tf_op jit(solution)/shard_map/ppermute | solution.py:29
  11.5 1.7 collective-permute-start.1
  13.9 11.1 %hidden_sums.1 = (bf16[32,256,128]{2,1,0:T(8,128)(2,1)}, f32[32,256,128]{2,1,0:T(8,128)}) custom-call(s32[4]{0:T(128)} %pad_add_fusion.place, s32[2,84]{1,0:T(2,128)} %bitcast.36, bf16[256,10752]{1,0:T(8,128)(2,1)} %cot_ref.3, bf16[168,128,128]{2,1,0:T(8,128)(2,1)} %weight_ref.1), custom_call_target="tpu_custom_call" | custom-call | flops 3000000000 | bytes 16777216 | tf_op jit(solution)/shard_map/hidden_sums/pallas_call | solution.py:87
  29.0 1.3 slice.44.refs_1_
  30.3 1.5 collective-permute-start.3
  31.8 4.0 %collective-permute-done.3 = bf16[32,256,128]{2,1,0:T(8,128)(2,1)S(1)} collective-permute-done((bf16[32,256,128]{2,1,0:T(8,128)(2,1)}, bf16[32,256,128]{2,1,0:T(8,128)(2,1)S(1)}, u32[]{:S(2)}, u32[]{:S(2)}) %collective-permute-start.3) | collective-permute-done | bytes 2097184 | tf_op jit(solution)/shard_map/ppermute | solution.py:29
  35.8 2.6 %core_sums.1 = (f32[8,176,128]{2,1,0:T(8,128)S(1)}, bf16[8,176,128]{2,1,0:T(8,128)(2,1)S(1)}, bf16[8,176,128]{2,1,0:T(8,128)(2,1)S(1)}, bf16[8,176,128]{2,1,0:T(...) custom-call(s32[4]{0:T(128)S(1)} %copy-done.5, f32[4,8,256,128]{3,2,1,0:T(8,128)S(1)} %bitcast.25, ...), custom_call_target="tpu_custom_call" | custom-call | flops 1000000 | bytes 8388608 | tf_op jit(solution)/shard_map/core_sums/pallas_call | solution.py:136
  39.2 8.2 %all-to-all-start = ((bf16[8,4,80,128]{3,2,1,0:T(8,128)(2,1)}), bf16[8,4,80,128]{3,2,1,0:T(8,128)(2,1)S(1)}, u32[]{:S(2)}, u32[]{:S(2)}) async-start(bf16[8,4,80,128]{3,2,1,0:T(8,128)(2,1)} %get-tuple-element.22), calls=%async_computation | async-start | bytes 1310720 | tf_op jit(solution)/shard_map/all_to_all | solution.py:343
  47.4 1.5 collective-permute-start.4
  49.4 2.0 %collective-permute-start.6 = (bf16[8,176,128]{2,1,0:T(8,128)(2,1)S(1)}, bf16[8,176,128]{2,1,0:T(8,128)(2,1)S(1)}, u32[]{:S(2)}, u32[]{:S(2)}) collective-permute-start(bf16[8,176,128]{2,1,0:T(8,128)(2,1)S(1)} %get-tuple-element.26), channel_id=1, source_target_pairs={{0,192},{4,196},{8,200},{12,204},{16,208},{20,212},{24,216},{28,22... | collective-permute-start | bytes 1081352 | tf_op jit(solution)/shard_map/ppermute | solution.py:29
  51.4 22.2 %all-to-all-done.got_ref = bf16[8,4,80,128]{3,2,1,0:T(8,128)(2,1)S(1)} async-done(((bf16[8,4,80,128]{3,2,1,0:T(8,128)(2,1)}), bf16[8,4,80,128]{3,2,1,0:T(8,128)(2,1)S(1)}, u32[]{:S(2)}, u32[]{:S(2)}) %all-to-all-start) | async-done | bytes 655392 | tf_op jit(solution)/shard_map/all_to_all | solution.py:343
  76.1 1.4 line_sums.1
  78.1 1.3 slice_bitcast_fusion.refs_1_
  79.4 3.0 %all-gather.3.cloned.1.call-done.refs_0_ = bf16[32,128,256]{2,1,0:T(8,128)(2,1)} async-done(((bf16[4,128,256]{2,1,0:T(8,128)(2,1)}), bf16[32,128,256]{2,1,0:T(8,128)(2,1)}) %all-gather.3.cloned.1.call-update) | async-done | bytes 2097168 | tf_op jit(solution)/shard_map/all_gather | solution.py:338
  82.5 2.6 %collective-permute-start.7 = (bf16[32,128,256]{2,1,0:T(8,128)(2,1)}, bf16[32,128,256]{2,1,0:T(8,128)(2,1)S(1)}, u32[]{:S(2)}, u32[]{:S(2)}) collective-permute-start(bf16[32,128,256]{2,1,0:T(8,128)(2,1)} %after.9.own_ref), channel_id=1, source_target_pairs={{0,4},{4,0},{8,12},{12,8},{16,20},{20,16},{24,28},{28,24},{32,36},... | collective-permute-start | bytes 6291464 | tf_op jit(solution)/shard_map/ppermute | solution.py:29
  85.0 4.1 %all-to-all-start.1 = ((bf16[8,176,128]{2,1,0:T(8,128)(2,1)}), bf16[8,176,128]{2,1,0:T(8,128)(2,1)S(1)}, u32[]{:S(2)}, u32[]{:S(2)}) async-start(bf16[8,176,128]{2,1,0:T(8,128)(2,1)} %get-tuple-element.27), calls=%async_computation.1 | async-start | bytes 720896 | tf_op jit(solution)/shard_map/all_to_all | solution.py:346
  89.2 1.4 copy-done.8
  90.6 10.4 %out_terms.1.refs_0_ = bf16[168,128,128]{2,1,0:T(8,128)(2,1)} custom-call(s32[4]{0:T(128)} %pad_add_fusion.place, s32[2,84]{1,0:T(2,128)} %bitcast.37, bf16[256,10752]{1,0:T(8,128)(2,1)} %cot_ref.3, bf16[32,128,256]{2,1,0:T(8,128)(2,1)} %after.9.own_ref, bf16[32,128,256]{2,1,0:T(8,128)(2,1)} %copy-done.8), custom_call_target="tpu_custom_call" | custom-call | flops 3000000000 | bytes 16777216 | tf_op jit(solution)/shard_map/out_terms/pallas_call | solution.py:237
  101.0 2.6 %all-to-all-done.1 = bf16[8,176,128]{2,1,0:T(8,128)(2,1)S(1)} async-done(((bf16[8,176,128]{2,1,0:T(8,128)(2,1)}), bf16[8,176,128]{2,1,0:T(8,128)(2,1)S(1)}, u32[]{:S(2)}, u32[]{:S(2)}) %all-to-all-start.1) | async-done | bytes 360480 | tf_op jit(solution)/shard_map/all_to_all | solution.py:346
  103.6 1.3 fusion.9.refs_1_
  106.9 4.0 %all-to-all-start.2 = ((bf16[8,176,128]{2,1,0:T(8,128)(2,1)}), bf16[8,176,128]{2,1,0:T(8,128)(2,1)S(1)}, u32[]{:S(2)}, u32[]{:S(2)}) async-start(bf16[8,176,128]{2,1,0:T(8,128)(2,1)} %broadcast_in_dim.25), calls=%async_computation.3 | async-start | bytes 720896 | tf_op jit(solution)/shard_map/all_to_all | solution.py:362
  110.9 1.5 collective-permute-start.15
  112.4 2.0 %collective-permute-start.16 = (bf16[80,128]{1,0:T(8,128)(2,1)S(1)}, bf16[80,128]{1,0:T(8,128)(2,1)S(1)}, u32[]{:S(2)}, u32[]{:S(2)}) collective-permute-start(bf16[80,128]{1,0:T(8,128)(2,1)S(1)} %get-tuple-element.30), channel_id=1, source_target_pairs={{0,128},{4,132},{8,136},{12,140},{16,144},{20,148},{24,152},{28,15... | collective-permute-start | bytes 61448 | tf_op jit(solution)/shard_map/ppermute | solution.py:29
  117.7 3.4 %collective-permute-start.19 = (bf16[80,128]{1,0:T(8,128)(2,1)S(1)}, bf16[80,128]{1,0:T(8,128)(2,1)S(1)}, u32[]{:S(2)}, u32[]{:S(2)}) collective-permute-start(bf16[80,128]{1,0:T(8,128)(2,1)S(1)} %fusion.8), channel_id=1, source_target_pairs={{0,128},{4,132},{8,136},{12,140},{16,144},{20,148},{24,152},{28,15... | collective-permute-start | bytes 61448 | tf_op jit(solution)/shard_map/ppermute | solution.py:29
  122.5 1.6 collective-permute-done.20
  125.6 6.0 %all-to-all-start.3 = ((bf16[8,4,80,128]{3,2,1,0:T(8,128)(2,1)}), bf16[8,4,80,128]{3,2,1,0:T(8,128)(2,1)S(1)}, u32[]{:S(2)}, u32[]{:S(2)}) async-start(bf16[8,4,80,128]{3,2,1,0:T(8,128)(2,1)} %broadcast_in_dim.26), calls=%async_computation.4 | async-start | bytes 1310720 | tf_op jit(solution)/shard_map/all_to_all | solution.py:366
  131.6 2.4 %collective-permute-start.9 = (bf16[8,176,128]{2,1,0:T(8,128)(2,1)S(1)}, bf16[8,176,128]{2,1,0:T(8,128)(2,1)S(1)}, u32[]{:S(2)}, u32[]{:S(2)}) collective-permute-start(bf16[8,176,128]{2,1,0:T(8,128)(2,1)S(1)} %all-to-all-done.2.refs_0_), channel_id=1, source_target_pairs={{0,128},{4,132},{8,136},{12,140},{16,144},{20,148},{24,152},{28,15... | collective-permute-start | bytes 1081352 | tf_op jit(solution)/shard_map/ppermute | solution.py:29
  135.2 14.0 %all-to-all-done.3.refs_8_ = bf16[8,4,80,128]{3,2,1,0:T(8,128)(2,1)S(1)} async-done(((bf16[8,4,80,128]{3,2,1,0:T(8,128)(2,1)}), bf16[8,4,80,128]{3,2,1,0:T(8,128)(2,1)S(1)}, u32[]{:S(2)}, u32[]{:S(2)}) %all-to-all-start.3) | async-done | bytes 655392 | tf_op jit(solution)/shard_map/all_to_all | solution.py:366
  149.2 3.7 %collective-permute-start.21 = (bf16[8,4,80,128]{3,2,1,0:T(8,128)(2,1)S(1)}, bf16[8,4,80,128]{3,2,1,0:T(8,128)(2,1)S(1)}, u32[]{:S(2)}, u32[]{:S(2)}) collective-permute-start(bf16[8,4,80,128]{3,2,1,0:T(8,128)(2,1)S(1)} %all-to-all-done.3.refs_8_), channel_id=1, source_target_pairs={{0,4},{4,0},{8,12},{12,8},{16,20},{20,16},{24,28},{28,24},{32,36},... | collective-permute-start | bytes 1966088 | tf_op jit(solution)/shard_map/ppermute | solution.py:29
  156.7 2.8 %in_terms.1 = (bf16[28,128,128]{2,1,0:T(8,128)(2,1)}, f32[7,128,128]{2,1,0:T(8,128)S(1)}) custom-call(s32[4]{0:T(128)S(1)} %copy-done.6, s32[4,7]{1,0:T(4,128)S(1)} %bitcast.27, bf16[256,896]{1,0:T(8,128)(2,1)S(1)} %copy-done.3, bf16[8,176,128]{2,1,0:T(8,128)(2,1)S(1)} %all-to-all-done.2.refs_0_, bf16[8,176,128]{2,1,0:T(8,128)(2,1)S(1)} %collective-permute-done.8.refs_1_, ...), custom_call_target="tpu_custom_call" | custom-call | flops 500000000 | bytes 8388608 | tf_op jit(solution)/shard_map/in_terms/pallas_call | solution.py:295
  159.5 4.0 %all-to-all-start.4 = ((bf16[4,7,128,128]{3,2,1,0:T(8,128)(2,1)}), bf16[4,7,128,128]{3,2,1,0:T(8,128)(2,1)S(1)}, u32[]{:S(2)}, u32[]{:S(2)}) async-start(bf16[4,7,128,128]{3,2,1,0:T(8,128)(2,1)} %bitcast.20), calls=%async_computation.5 | async-start | bytes 1835008 | tf_op jit(solution)/shard_map/all_to_all | solution.py:371
  163.6 13.1 %all-to-all-done.4 = bf16[4,7,128,128]{3,2,1,0:T(8,128)(2,1)S(1)} async-done(((bf16[4,7,128,128]{3,2,1,0:T(8,128)(2,1)}), bf16[4,7,128,128]{3,2,1,0:T(8,128)(2,1)S(1)}, u32[]{:S(2)}, u32[]{:S(2)}) %all-to-all-start.4) | async-done | bytes 917536 | tf_op jit(solution)/shard_map/all_to_all | solution.py:371
  (78 shorter events, 24.0 us)
Async XLA Ops:
  7.2 75.3 %all-gather.3.cloned.1.call-start = ((), (), s32[]{:S(2)}) async-start(), calls=%async_computation.7 | async-start | bytes 2359296 | tf_op jit(solution)/shard_map/all_gather | solution.py:338
  8.1 19.9 %collective-permute-start.2 = (bf16[128,256]{0,1:T(8,128)(2,1)S(1)}, bf16[128,256]{0,1:T(8,128)(2,1)S(1)}, u32[]{:S(2)}, u32[]{:S(2)}) collective-permute-start(bf16[128,256]{0,1:T(8,128)(2,1)S(1)} %get-tuple-element.35), channel_id=1, source_target_pairs={{0,192},{4,196},{8,200},{12,204},{16,208},{20,212},{24,216},{28,22... | collective-permute-start | bytes 196616 | tf_op jit(solution)/shard_map/ppermute | solution.py:29
  11.5 16.5 %collective-permute-start = (bf16[128,256]{0,1:T(8,128)(2,1)S(1)}, bf16[128,256]{0,1:T(8,128)(2,1)S(1)}, u32[]{:S(2)}, u32[]{:S(2)}) collective-permute-start(bf16[128,256]{0,1:T(8,128)(2,1)S(1)} %get-tuple-element.35), channel_id=1, source_target_pairs={{0,64},{4,68},{8,72},{12,76},{16,80},{20,84},{24,88},{28,92},{32,9... | collective-permute-start | bytes 196616 | tf_op jit(solution)/shard_map/ppermute | solution.py:29
  11.5 16.5 %collective-permute-start.1 = (bf16[128,256]{0,1:T(8,128)(2,1)S(1)}, bf16[128,256]{0,1:T(8,128)(2,1)S(1)}, u32[]{:S(2)}, u32[]{:S(2)}) collective-permute-start(bf16[128,256]{0,1:T(8,128)(2,1)S(1)} %get-tuple-element.35), channel_id=1, source_target_pairs={{0,128},{4,132},{8,136},{12,140},{16,144},{20,148},{24,152},{28,15... | collective-permute-start | bytes 196616 | tf_op jit(solution)/shard_map/ppermute | solution.py:29
  30.3 5.5 %collective-permute-start.3 = (bf16[32,256,128]{2,1,0:T(8,128)(2,1)}, bf16[32,256,128]{2,1,0:T(8,128)(2,1)S(1)}, u32[]{:S(2)}, u32[]{:S(2)}) collective-permute-start(bf16[32,256,128]{2,1,0:T(8,128)(2,1)} %after.7), channel_id=1, source_target_pairs={{0,4},{4,0},{8,12},{12,8},{16,20},{20,16},{24,28},{28,24},{32,36},... | collective-permute-start | bytes 6291464 | tf_op jit(solution)/shard_map/ppermute | solution.py:29
  39.2 34.4 %all-to-all-start = ((bf16[8,4,80,128]{3,2,1,0:T(8,128)(2,1)}), bf16[8,4,80,128]{3,2,1,0:T(8,128)(2,1)S(1)}, u32[]{:S(2)}, u32[]{:S(2)}) async-start(bf16[8,4,80,128]{3,2,1,0:T(8,128)(2,1)} %get-tuple-element.22), calls=%async_computation | async-start | bytes 1310720 | tf_op jit(solution)/shard_map/all_to_all | solution.py:343
  47.4 27.5 %collective-permute-start.4 = (bf16[8,176,128]{2,1,0:T(8,128)(2,1)S(1)}, bf16[8,176,128]{2,1,0:T(8,128)(2,1)S(1)}, u32[]{:S(2)}, u32[]{:S(2)}) collective-permute-start(bf16[8,176,128]{2,1,0:T(8,128)(2,1)S(1)} %get-tuple-element.24), channel_id=1, source_target_pairs={{0,64},{4,68},{8,72},{12,76},{16,80},{20,84},{24,88},{28,92},{32,9... | collective-permute-start | bytes 1081352 | tf_op jit(solution)/shard_map/ppermute | solution.py:29
  48.9 26.0 %collective-permute-start.5 = (bf16[8,176,128]{2,1,0:T(8,128)(2,1)S(1)}, bf16[8,176,128]{2,1,0:T(8,128)(2,1)S(1)}, u32[]{:S(2)}, u32[]{:S(2)}) collective-permute-start(bf16[8,176,128]{2,1,0:T(8,128)(2,1)S(1)} %get-tuple-element.25), channel_id=1, source_target_pairs={{0,128},{4,132},{8,136},{12,140},{16,144},{20,148},{24,152},{28,15... | collective-permute-start | bytes 1081352 | tf_op jit(solution)/shard_map/ppermute | solution.py:29
  49.4 25.5 %collective-permute-start.6 = (bf16[8,176,128]{2,1,0:T(8,128)(2,1)S(1)}, bf16[8,176,128]{2,1,0:T(8,128)(2,1)S(1)}, u32[]{:S(2)}, u32[]{:S(2)}) collective-permute-start(bf16[8,176,128]{2,1,0:T(8,128)(2,1)S(1)} %get-tuple-element.26), channel_id=1, source_target_pairs={{0,192},{4,196},{8,200},{12,204},{16,208},{20,212},{24,216},{28,22... | collective-permute-start | bytes 1081352 | tf_op jit(solution)/shard_map/ppermute | solution.py:29
  82.5 6.7 %collective-permute-start.7 = (bf16[32,128,256]{2,1,0:T(8,128)(2,1)}, bf16[32,128,256]{2,1,0:T(8,128)(2,1)S(1)}, u32[]{:S(2)}, u32[]{:S(2)}) collective-permute-start(bf16[32,128,256]{2,1,0:T(8,128)(2,1)} %after.9.own_ref), channel_id=1, source_target_pairs={{0,4},{4,0},{8,12},{12,8},{16,20},{20,16},{24,28},{28,24},{32,36},... | collective-permute-start | bytes 6291464 | tf_op jit(solution)/shard_map/ppermute | solution.py:29
  85.0 18.6 %all-to-all-start.1 = ((bf16[8,176,128]{2,1,0:T(8,128)(2,1)}), bf16[8,176,128]{2,1,0:T(8,128)(2,1)S(1)}, u32[]{:S(2)}, u32[]{:S(2)}) async-start(bf16[8,176,128]{2,1,0:T(8,128)(2,1)} %get-tuple-element.27), calls=%async_computation.1 | async-start | bytes 720896 | tf_op jit(solution)/shard_map/all_to_all | solution.py:346
  89.1 88.5 %reduce-scatter.2.cloned.1.call-start = ((), (), s32[]{:S(2)}) async-start(), calls=%async_computation.6 | async-start | bytes 6881280 | tf_op jit(solution)/shard_map/reduce_scatter | solution.py:353
  104.9 51.8 %copy-start.3 = (bf16[256,896]{1,0:T(8,128)(2,1)S(1)}, bf16[256,896]{1,0:T(8,128)(2,1)}, u32[]{:S(2)}) copy-start(bf16[256,896]{1,0:T(8,128)(2,1)} %enc_ref.1) | copy-start | bytes 1376260
  105.0 51.8 %copy-start.6 = (s32[4]{0:T(128)S(1)}, s32[4]{0:T(128)}, u32[]{:S(2)}) copy-start(s32[4]{0:T(128)} %pad_add_fusion.place) | copy-start | bytes 52
  105.0 51.7 %copy-start.7 = (s32[7,4]{0,1:T(4,128)S(1)}, s32[7,4]{0,1:T(4,128)}, u32[]{:S(2)}) copy-start(s32[7,4]{0,1:T(4,128)} %param.11) | copy-start | bytes 340
  106.9 17.7 %all-to-all-start.2 = ((bf16[8,176,128]{2,1,0:T(8,128)(2,1)}), bf16[8,176,128]{2,1,0:T(8,128)(2,1)S(1)}, u32[]{:S(2)}, u32[]{:S(2)}) async-start(bf16[8,176,128]{2,1,0:T(8,128)(2,1)} %broadcast_in_dim.25), calls=%async_computation.3 | async-start | bytes 720896 | tf_op jit(solution)/shard_map/all_to_all | solution.py:362
  110.9 4.6 %collective-permute-start.15 = (bf16[80,128]{1,0:T(8,128)(2,1)S(1)}, bf16[80,128]{1,0:T(8,128)(2,1)S(1)}, u32[]{:S(2)}, u32[]{:S(2)}) collective-permute-start(bf16[80,128]{1,0:T(8,128)(2,1)S(1)} %get-tuple-element.29), channel_id=1, source_target_pairs={{0,64},{4,68},{8,72},{12,76},{16,80},{20,84},{24,88},{28,92},{32,9... | collective-permute-start | bytes 61448 | tf_op jit(solution)/shard_map/ppermute | solution.py:29
  112.4 4.1 %collective-permute-start.16 = (bf16[80,128]{1,0:T(8,128)(2,1)S(1)}, bf16[80,128]{1,0:T(8,128)(2,1)S(1)}, u32[]{:S(2)}, u32[]{:S(2)}) collective-permute-start(bf16[80,128]{1,0:T(8,128)(2,1)S(1)} %get-tuple-element.30), channel_id=1, source_target_pairs={{0,128},{4,132},{8,136},{12,140},{16,144},{20,148},{24,152},{28,15... | collective-permute-start | bytes 61448 | tf_op jit(solution)/shard_map/ppermute | solution.py:29
  114.4 3.2 %collective-permute-start.17 = (bf16[80,128]{1,0:T(8,128)(2,1)S(1)}, bf16[80,128]{1,0:T(8,128)(2,1)S(1)}, u32[]{:S(2)}, u32[]{:S(2)}) collective-permute-start(bf16[80,128]{1,0:T(8,128)(2,1)S(1)} %get-tuple-element.31), channel_id=1, source_target_pairs={{0,192},{4,196},{8,200},{12,204},{16,208},{20,212},{24,216},{28,22... | collective-permute-start | bytes 61448 | tf_op jit(solution)/shard_map/ppermute | solution.py:29
  117.6 4.3 %collective-permute-start.18 = (bf16[80,128]{1,0:T(8,128)(2,1)S(1)}, bf16[80,128]{1,0:T(8,128)(2,1)S(1)}, u32[]{:S(2)}, u32[]{:S(2)}) collective-permute-start(bf16[80,128]{1,0:T(8,128)(2,1)S(1)} %fusion.8), channel_id=1, source_target_pairs={{0,64},{4,68},{8,72},{12,76},{16,80},{20,84},{24,88},{28,92},{32,9... | collective-permute-start | bytes 61448 | tf_op jit(solution)/shard_map/ppermute | solution.py:29
  117.7 4.8 %collective-permute-start.19 = (bf16[80,128]{1,0:T(8,128)(2,1)S(1)}, bf16[80,128]{1,0:T(8,128)(2,1)S(1)}, u32[]{:S(2)}, u32[]{:S(2)}) collective-permute-start(bf16[80,128]{1,0:T(8,128)(2,1)S(1)} %fusion.8), channel_id=1, source_target_pairs={{0,128},{4,132},{8,136},{12,140},{16,144},{20,148},{24,152},{28,15... | collective-permute-start | bytes 61448 | tf_op jit(solution)/shard_map/ppermute | solution.py:29
  121.1 3.0 %collective-permute-start.20 = (bf16[80,128]{1,0:T(8,128)(2,1)S(1)}, bf16[80,128]{1,0:T(8,128)(2,1)S(1)}, u32[]{:S(2)}, u32[]{:S(2)}) collective-permute-start(bf16[80,128]{1,0:T(8,128)(2,1)S(1)} %fusion.8), channel_id=1, source_target_pairs={{0,192},{4,196},{8,200},{12,204},{16,208},{20,212},{24,216},{28,22... | collective-permute-start | bytes 61448 | tf_op jit(solution)/shard_map/ppermute | solution.py:29
  125.6 23.6 %all-to-all-start.3 = ((bf16[8,4,80,128]{3,2,1,0:T(8,128)(2,1)}), bf16[8,4,80,128]{3,2,1,0:T(8,128)(2,1)S(1)}, u32[]{:S(2)}, u32[]{:S(2)}) async-start(bf16[8,4,80,128]{3,2,1,0:T(8,128)(2,1)} %broadcast_in_dim.26), calls=%async_computation.4 | async-start | bytes 1310720 | tf_op jit(solution)/shard_map/all_to_all | solution.py:366
  131.6 21.3 %collective-permute-start.8 = (bf16[8,176,128]{2,1,0:T(8,128)(2,1)S(1)}, bf16[8,176,128]{2,1,0:T(8,128)(2,1)S(1)}, u32[]{:S(2)}, u32[]{:S(2)}) collective-permute-start(bf16[8,176,128]{2,1,0:T(8,128)(2,1)S(1)} %all-to-all-done.2.refs_0_), channel_id=1, source_target_pairs={{0,64},{4,68},{8,72},{12,76},{16,80},{20,84},{24,88},{28,92},{32,9... | collective-permute-start | bytes 1081352 | tf_op jit(solution)/shard_map/ppermute | solution.py:29
  131.6 21.8 %collective-permute-start.9 = (bf16[8,176,128]{2,1,0:T(8,128)(2,1)S(1)}, bf16[8,176,128]{2,1,0:T(8,128)(2,1)S(1)}, u32[]{:S(2)}, u32[]{:S(2)}) collective-permute-start(bf16[8,176,128]{2,1,0:T(8,128)(2,1)S(1)} %all-to-all-done.2.refs_0_), channel_id=1, source_target_pairs={{0,128},{4,132},{8,136},{12,140},{16,144},{20,148},{24,152},{28,15... | collective-permute-start | bytes 1081352 | tf_op jit(solution)/shard_map/ppermute | solution.py:29
  134.0 19.5 %collective-permute-start.10 = (bf16[8,176,128]{2,1,0:T(8,128)(2,1)S(1)}, bf16[8,176,128]{2,1,0:T(8,128)(2,1)S(1)}, u32[]{:S(2)}, u32[]{:S(2)}) collective-permute-start(bf16[8,176,128]{2,1,0:T(8,128)(2,1)S(1)} %all-to-all-done.2.refs_0_), channel_id=1, source_target_pairs={{0,192},{4,196},{8,200},{12,204},{16,208},{20,212},{24,216},{28,22... | collective-permute-start | bytes 1081352 | tf_op jit(solution)/shard_map/ppermute | solution.py:29
  149.2 5.5 %collective-permute-start.21 = (bf16[8,4,80,128]{3,2,1,0:T(8,128)(2,1)S(1)}, bf16[8,4,80,128]{3,2,1,0:T(8,128)(2,1)S(1)}, u32[]{:S(2)}, u32[]{:S(2)}) collective-permute-start(bf16[8,4,80,128]{3,2,1,0:T(8,128)(2,1)S(1)} %all-to-all-done.3.refs_8_), channel_id=1, source_target_pairs={{0,4},{4,0},{8,12},{12,8},{16,20},{20,16},{24,28},{28,24},{32,36},... | collective-permute-start | bytes 1966088 | tf_op jit(solution)/shard_map/ppermute | solution.py:29
  152.9 2.2 %collective-permute-start.11 = (bf16[8,176,128]{2,1,0:T(8,128)(2,1)S(1)}, bf16[8,176,128]{2,1,0:T(8,128)(2,1)S(1)}, u32[]{:S(2)}, u32[]{:S(2)}) collective-permute-start(bf16[8,176,128]{2,1,0:T(8,128)(2,1)S(1)} %all-to-all-done.2.refs_0_), channel_id=1, source_target_pairs={{0,4},{4,0},{8,12},{12,8},{16,20},{20,16},{24,28},{28,24},{32,36},... | collective-permute-start | bytes 1081352 | tf_op jit(solution)/shard_map/ppermute | solution.py:29
  152.9 2.7 %collective-permute-start.12 = (bf16[8,176,128]{2,1,0:T(8,128)(2,1)S(1)}, bf16[8,176,128]{2,1,0:T(8,128)(2,1)S(1)}, u32[]{:S(2)}, u32[]{:S(2)}) collective-permute-start(bf16[8,176,128]{2,1,0:T(8,128)(2,1)S(1)} %collective-permute-done.8.refs_1_), channel_id=1, source_target_pairs={{0,4},{4,0},{8,12},{12,8},{16,20},{20,16},{24,28},{28,24},{32,36},... | collective-permute-start | bytes 1081352 | tf_op jit(solution)/shard_map/ppermute | solution.py:29
  153.4 2.8 %collective-permute-start.13 = (bf16[8,176,128]{2,1,0:T(8,128)(2,1)S(1)}, bf16[8,176,128]{2,1,0:T(8,128)(2,1)S(1)}, u32[]{:S(2)}, u32[]{:S(2)}) collective-permute-start(bf16[8,176,128]{2,1,0:T(8,128)(2,1)S(1)} %collective-permute-done.9.refs_2_), channel_id=1, source_target_pairs={{0,4},{4,0},{8,12},{12,8},{16,20},{20,16},{24,28},{28,24},{32,36},... | collective-permute-start | bytes 1081352 | tf_op jit(solution)/shard_map/ppermute | solution.py:29
  153.5 3.2 %collective-permute-start.14 = (bf16[8,176,128]{2,1,0:T(8,128)(2,1)S(1)}, bf16[8,176,128]{2,1,0:T(8,128)(2,1)S(1)}, u32[]{:S(2)}, u32[]{:S(2)}) collective-permute-start(bf16[8,176,128]{2,1,0:T(8,128)(2,1)S(1)} %collective-permute-done.10.refs_3_), channel_id=1, source_target_pairs={{0,4},{4,0},{8,12},{12,8},{16,20},{20,16},{24,28},{28,24},{32,36},... | collective-permute-start | bytes 1081352 | tf_op jit(solution)/shard_map/ppermute | solution.py:29
  159.5 17.1 %all-to-all-start.4 = ((bf16[4,7,128,128]{3,2,1,0:T(8,128)(2,1)}), bf16[4,7,128,128]{3,2,1,0:T(8,128)(2,1)S(1)}, u32[]{:S(2)}, u32[]{:S(2)}) async-start(bf16[4,7,128,128]{3,2,1,0:T(8,128)(2,1)} %bitcast.20), calls=%async_computation.5 | async-start | bytes 1835008 | tf_op jit(solution)/shard_map/all_to_all | solution.py:371
  (6 other events, 15.1 us)
Sparse Core Ops, SparseCore 0:
  29.1 53.3 all-gather.2
  105.0 58.4 reduce-scatter.1

commit v4 on v2

--- a/solution.py
+++ b/solution.py
@@ -28,6 +28,10 @@
     return lax.ppermute(value, "blk", pairs)
 
 
+def moved_smp(value, dy):
+    return lax.ppermute(value, "smp", [(i, (i + dy) % NY) for i in range(NY)])
+
+
 LINES = [[index_of(x, z, c) for z in range(NZ)] for x in range(NX) for c in range(NC)]
 
 
@@ -41,6 +45,7 @@
 
 def after(value, other):
     anywhere = pl.BlockSpec(memory_space=pl.ANY)
+    other = other[(0,) * (other.ndim - 2)][:16] if other.ndim > 2 else other
     return pl.pallas_call(
         lambda *refs: None,
         in_specs=[anywhere, anywhere],
@@ -51,7 +56,7 @@
     )(value, other)
 
 
-def hidden_kernel(place, contacts, cot_ref, weight_ref, send_ref, keep_ref, total):
+def hidden_kernel(place, contacts, cot_ref, weight_ref, send_ref, keep_ref, mark_ref, total):
     step = pl.program_id(0)
     core = place[2]
 
@@ -75,6 +80,7 @@
             return carry
 
         lax.fori_loop(0, NX * NZ, write, 0)
+        mark_ref[...] = jnp.zeros_like(mark_ref)
 
 
 def hidden_sums(place, contacts, cotangent, weights):
@@ -93,12 +99,14 @@
             out_specs=[
                 pl.BlockSpec((count, rows, BS), lambda g, *_: (0, 0, 0)),
                 pl.BlockSpec((count, rows, BS), lambda g, *_: (0, 0, 0)),
+                pl.BlockSpec((8, BS), lambda g, *_: (0, 0)),
             ],
             scratch_shapes=[pltpu.VMEM((2 * count, rows, BS), F32)],
         ),
         out_shape=[
             jax.ShapeDtypeStruct((count, rows, BS), BF16),
             jax.ShapeDtypeStruct((count, rows, BS), F32),
+            jax.ShapeDtypeStruct((8, BS), F32),
         ],
         compiler_params=params(56),
         cost_estimate=pl.CostEstimate(flops=3 * 10**9, bytes_accessed=2**24, transcendentals=0),
@@ -212,7 +220,8 @@
 
 
 def in_kernel(place, contacts, enc_ref, *refs):
-    parts, (send_ref, mine_ref, held, made, sems) = refs[: NC * NX], refs[NC * NX :]
+    parts, outs = refs[: NC * NX], refs[NC * NX : NC * NX + NY]
+    held, made, sems = refs[NC * NX + NY :]
     x, core, y = place[0], place[2], place[3]
     copies = [
         pltpu.make_async_copy(part, held.at[n], sems.at[n]) for n, part in enumerate(parts)
@@ -228,11 +237,11 @@
             k = contacts[m, i]
             slot = ((k & 1) ^ core) * NX + ((x - (k >> 4)) & (NX - 1))
             made[i * per_in + m] = contract(turned, held[slot, (k >> 1) & (NZ - 1)], (1, 0))
-    for n in range(count * per_in):
-        send_ref[n] = made[n].astype(BF16)
     each = count * per_in // NY
-    for n in range(each):
-        mine_ref[n] = made[y * each + n]
+    for d in range(NY):
+        first = ((y + d) & (NY - 1)) * each
+        for n in range(each):
+            outs[d][n] = made[first + n].astype(outs[d].dtype)
 
 
 def in_terms(place, contacts, encodings, parts):
@@ -244,16 +253,13 @@
     return pl.pallas_call(
         in_kernel,
         in_specs=[smem, smem, whole] + [pl.BlockSpec(memory_space=pl.ANY)] * (NC * NX),
-        out_specs=[whole] * 2,
+        out_specs=[whole] * NY,
         scratch_shapes=[
             pltpu.VMEM((NC * NX, NZ, rows, BS), BF16),
             pltpu.VMEM((per_in * count, BS, BS), F32),
             pltpu.SemaphoreType.DMA((NC * NX,)),
         ],
-        out_shape=[
-            jax.ShapeDtypeStruct((per_in * count, BS, BS), BF16),
-            jax.ShapeDtypeStruct((each, BS, BS), F32),
-        ],
+        out_shape=[jax.ShapeDtypeStruct((each, BS, BS), BF16 if d else F32) for d in range(NY)],
         compiler_params=params(14),
         cost_estimate=pl.CostEstimate(flops=5 * 10**8, bytes_accessed=2**23, transcendentals=0),
         name="in_terms",
@@ -281,8 +287,8 @@
     activation = jax.nn.silu(pre).astype(BF16).T
     arrived = [moved(activation, dx=d) for d in range(1, NX)]
 
-    send, keep = hidden_sums(place, out_index, cotangent, out_weights)
-    along_x = jnp.stack([after(activation, send)] + arrived)
+    send, keep, mark = hidden_sums(place, out_index, cotangent, out_weights)
+    along_x = jnp.stack([after(activation, mark)] + arrived)
     send = after(send, along_x)
     act_own = lax.all_gather(along_x, "blk", axis_index_groups=LINES)
     act_own = act_own.reshape(NZ * NX, BS, -1)
@@ -290,21 +296,22 @@
     by_x = core_sums(place, keep, moved(send, dc=1))
     by_z, own_z = line_sums(place, by_x[0], *[moved(by_x[d], dx=d) for d in range(1, NX)])
     got = lax.all_to_all(by_z, "blk", 0, 0, axis_index_groups=LINES)
-    grad_pre = (sum_parts(got, own_z, place[1]) * silu_slope(pre)).astype(BF16)
-
-    act_own = after(act_own, by_z)
+    act_own = after(act_own, own_z)
     terms = out_terms(place, out_index, cotangent, act_own, moved(act_own, dc=1))
+    both = got[0, :16] + terms[0, :16]
+    terms = after(terms, both)
     out_grad = lax.psum_scatter(terms, "smp", scatter_dimension=0, tiled=True)
+
+    grad_act = sum_parts(got, after(own_z, both), place[1])
+    grad_pre = (grad_act * silu_slope(pre)).astype(BF16)
 
     copies = jnp.broadcast_to(grad_pre, (NZ, *grad_pre.shape))
     along_z = lax.all_to_all(copies, "blk", 0, 0, axis_index_groups=LINES)
     own = [along_z] + [moved(along_z, dx=d) for d in range(1, NX)]
     parts = own + [moved(part, dc=1) for part in own]
 
-    away, mine = in_terms(place, in_index, encodings, parts)
-    away = away.reshape(NY, *mine.shape)
-    away = lax.all_to_all(away, "smp", 0, 0)
-    in_grad = sum_parts(away, mine, place[3]).astype(BF16)
+    mine, *away = in_terms(place, in_index, encodings, parts)
+    in_grad = sum((moved_smp(a, d + 1).astype(F32) for d, a in enumerate(away)), mine).astype(BF16)
     return (out_grad, in_grad)
 
 

time: 187 us -> 172 us (0.920)
  waiting for transfers between devices: 83.5 us -> 55.9 us
  starting transfers between devices: 33.7 us -> 42 us
  other arithmetic: 3.43 us -> 5.5 us
  local copies, waits for them, and re-layouts: 4.8 us -> 6.76 us
    all_to_all x1 -> x0, waiting for transfers between devices: 13.1 us -> none  [per_device(): away = lax.all_to_all(away, 'smp', 0, 0)]
    all_to_all x1, waiting for transfers between devices: 17.9 us -> 6.1 us  [per_device(): got = lax.all_to_all(by_z, 'blk', 0, 0, axis_index_groups=LINES)]
    ppermute x15, waiting for transfers between devices: 50.3 us -> 38.9 us  [moved(): return lax.ppermute(value, 'blk', pairs)]
    ppermute x0 -> x3, waiting for transfers between devices: none -> 9.11 us  [moved_smp(): return lax.ppermute(value, 'smp', [(i, (i + dy) % NY) for i in range(NY)])]
    ppermute x15, starting transfers between devices: 25.6 us -> 33.2 us  [moved(): return lax.ppermute(value, 'blk', pairs)]
    ppermute x0 -> x3, starting transfers between devices: none -> 4.89 us  [moved_smp(): return lax.ppermute(value, 'smp', [(i, (i + dy) % NY) for i in range(NY)])]
    all_to_all x1 -> x0, starting transfers between devices: 4 us -> none  [per_device(): away = lax.all_to_all(away, 'smp', 0, 0)]
    unnamed x15 -> x17, local copies, waits for them, and re-layouts: 4.52 us -> 5.19 us
  transfers between devices with their start and end apart: 19 -> 21, of which waited for: 12 -> 11; matrix products, arithmetic and copies ran while one was open for 1% -> 2% of each run, Pallas kernels for 9% -> 15%
where the time goes in v4:
time: 172 us; the launch traced here: 171 us
  waiting for transfers between devices  55.9 us (32%)
  starting transfers between devices  42 us (24%)
  Pallas kernels  26.4 us (15%)
  blocking collectives  20.3 us (12%)
  between operations  14.2 us (8%)
  local copies, waits for them, and re-layouts  6.76 us (4%)
  other arithmetic  5.5 us (3%)
    ppermute x15, waiting for transfers between devices, moved(): return lax.ppermute(value, 'blk', pairs)  38.9 us
    ppermute x15, starting transfers between devices, moved(): return lax.ppermute(value, 'blk', pairs)  33.2 us
    all_to_all x1, blocking collectives, per_device(): along_z = lax.all_to_all(copies, 'blk', 0, 0, axis_index_groups=LINES)  20.3 us
    pallas_call x1, Pallas kernels, hidden_sums(): pl.pallas_call(hidden_kernel, grid_spec=pltpu.PrefetchScalarGridSpec(num_...  11.2 us
    pallas_call x1, Pallas kernels, out_terms(): pl.pallas_call(out_kernel, grid_spec=pltpu.PrefetchScalarGridSpec(num_sca...  10.4 us
    ppermute x3, waiting for transfers between devices, moved_smp(): return lax.ppermute(value, 'smp', [(i, (i + dy) % NY) for i in range(NY)])  9.11 us
    all_to_all x1, waiting for transfers between devices, per_device(): got = lax.all_to_all(by_z, 'blk', 0, 0, axis_index_groups=LINES)  6.1 us
    unnamed x17, local copies, waits for them, and re-layouts  5.19 us
  transfers between devices with their start and end apart: 21, of which 11 were waited for; matrix products, arithmetic and copies ran while one was open for 2% of the time, Pallas kernels for 15%

profile of v4, /device:TPU:1, one launch (start us, length us, event | category | flops | bytes accessed | tf_op | source)
XLA Modules:
  0.0 171.0 jit_solution(3862569682406322096)
XLA Ops:
  8.2 3.4 %collective-permute-start.2 = (bf16[128,256]{1,0:T(8,128)(2,1)S(1)}, bf16[128,256]{1,0:T(8,128)(2,1)S(1)}, u32[]{:S(2)}, u32[]{:S(2)}) collective-permute-start(bf16[128,256]{1,0:T(8,128)(2,1)S(1)} %fusion.8.refs_0_), channel_id=1, source_target_pairs={{0,192},{4,196},{8,200},{12,204},{16,208},{20,212},{24,216},{28,22... | collective-permute-start | bytes 196616 | tf_op jit(solution)/shard_map/ppermute | solution.py:28
  13.3 11.2 %hidden_sums.1 = (bf16[32,256,128]{2,1,0:T(8,128)(2,1)}, f32[32,256,128]{2,1,0:T(8,128)}, f32[8,128]{1,0:T(8,128)}) custom-call(s32[4]{0:T(128)} %pad_add_fusion.place, s32[2,84]{1,0:T(2,128)} %bitcast.23, bf16[256,10752]{1,0:T(8,128)(2,1)} %cot_ref.3, bf16[168,128,128]{2,1,0:T(8,128)(2,1)} %weight_ref.1), custom_call_target="tpu_custom_call" | custom-call | flops 3000000000 | bytes 16777216 | tf_op jit(solution)/shard_map/hidden_sums/pallas_call | solution.py:90
  24.6 1.6 pad_maximum_fusion
  26.2 1.3 slice.12.refs_1_
  27.5 1.5 collective-permute-start.3
  29.0 4.0 %collective-permute-done.3 = bf16[32,256,128]{2,1,0:T(8,128)(2,1)S(1)} collective-permute-done((bf16[32,256,128]{2,1,0:T(8,128)(2,1)}, bf16[32,256,128]{2,1,0:T(8,128)(2,1)S(1)}, u32[]{:S(2)}, u32[]{:S(2)}) %collective-permute-start.3) | collective-permute-done | bytes 2097184 | tf_op jit(solution)/shard_map/ppermute | solution.py:28
  33.0 2.2 %copy-done = f32[32,256,128]{2,1,0:T(8,128)S(1)} copy-done((f32[32,256,128]{2,1,0:T(8,128)S(1)}, f32[32,256,128]{2,1,0:T(8,128)}, u32[]{:S(2)}) %copy-start) | copy-done | bytes 4194328
  35.2 1.4 core_sums.1
  36.6 1.6 collective-permute-start.4
  38.2 1.7 %collective-permute-start.5 = (bf16[8,256,128]{2,1,0:T(8,128)(2,1)S(1)}, bf16[8,256,128]{2,1,0:T(8,128)(2,1)S(1)}, u32[]{:S(2)}, u32[]{:S(2)}) collective-permute-start(bf16[8,256,128]{2,1,0:T(8,128)(2,1)S(1)} %get-tuple-element.20), channel_id=1, source_target_pairs={{0,128},{4,132},{8,136},{12,140},{16,144},{20,148},{24,152},{28,15... | collective-permute-start | bytes 1572872 | tf_op jit(solution)/shard_map/ppermute | solution.py:28
  40.0 2.0 %collective-permute-start.6 = (bf16[8,256,128]{2,1,0:T(8,128)(2,1)S(1)}, bf16[8,256,128]{2,1,0:T(8,128)(2,1)S(1)}, u32[]{:S(2)}, u32[]{:S(2)}) collective-permute-start(bf16[8,256,128]{2,1,0:T(8,128)(2,1)S(1)} %get-tuple-element.21), channel_id=1, source_target_pairs={{0,192},{4,196},{8,200},{12,204},{16,208},{20,212},{24,216},{28,22... | collective-permute-start | bytes 1572872 | tf_op jit(solution)/shard_map/ppermute | solution.py:28
  42.0 9.2 %collective-permute-done.4.a_ref = bf16[8,256,128]{2,1,0:T(8,128)(2,1)S(1)} collective-permute-done((bf16[8,256,128]{2,1,0:T(8,128)(2,1)S(1)}, bf16[8,256,128]{2,1,0:T(8,128)(2,1)S(1)}, u32[]{:S(2)}, u32[]{:S(2)}) %collective-permute-start.4) | collective-permute-done | bytes 524320 | tf_op jit(solution)/shard_map/ppermute | solution.py:28
  51.2 11.7 %collective-permute-done.5.b_ref = bf16[8,256,128]{2,1,0:T(8,128)(2,1)S(1)} collective-permute-done((bf16[8,256,128]{2,1,0:T(8,128)(2,1)S(1)}, bf16[8,256,128]{2,1,0:T(8,128)(2,1)S(1)}, u32[]{:S(2)}, u32[]{:S(2)}) %collective-permute-start.5) | collective-permute-done | bytes 524320 | tf_op jit(solution)/shard_map/ppermute | solution.py:28
  62.9 1.6 line_sums.1
  65.1 1.8 %all-gather.3.cloned.1.call-done.refs_0_ = bf16[32,128,256]{2,1,0:T(8,128)(2,1)} async-done(((bf16[4,128,256]{2,1,0:T(8,128)(2,1)}), bf16[32,128,256]{2,1,0:T(8,128)(2,1)}) %all-gather.3.cloned.1.call-update) | async-done | bytes 2097168 | tf_op jit(solution)/shard_map/all_gather | solution.py:293
  66.9 4.6 %collective-permute-start.7 = (bf16[32,128,256]{2,1,0:T(8,128)(2,1)}, bf16[32,128,256]{2,1,0:T(8,128)(2,1)S(1)}, u32[]{:S(2)}, u32[]{:S(2)}) collective-permute-start(bf16[32,128,256]{2,1,0:T(8,128)(2,1)} %after.7.own_ref), channel_id=1, source_target_pairs={{0,4},{4,0},{8,12},{12,8},{16,20},{20,16},{24,28},{28,24},{32,36},... | collective-permute-start | bytes 6291464 | tf_op jit(solution)/shard_map/ppermute | solution.py:28
  71.5 3.9 %all-to-all-start = ((bf16[8,256,128]{2,1,0:T(8,128)(2,1)}), bf16[8,256,128]{2,1,0:T(8,128)(2,1)S(1)}, u32[]{:S(2)}, u32[]{:S(2)}) async-start(bf16[8,256,128]{2,1,0:T(8,128)(2,1)} %get-tuple-element.23), calls=%async_computation | async-start | bytes 1048576 | tf_op jit(solution)/shard_map/all_to_all | solution.py:298
  75.5 1.4 copy-done.6
  76.9 10.4 %out_terms.1.refs_0_ = bf16[168,128,128]{2,1,0:T(8,128)(2,1)} custom-call(s32[4]{0:T(128)} %pad_add_fusion.place, s32[2,84]{1,0:T(2,128)} %bitcast.24, bf16[256,10752]{1,0:T(8,128)(2,1)} %cot_ref.3, bf16[32,128,256]{2,1,0:T(8,128)(2,1)} %after.7.own_ref, bf16[32,128,256]{2,1,0:T(8,128)(2,1)} %copy-done.6), custom_call_target="tpu_custom_call" | custom-call | flops 3000000000 | bytes 16777216 | tf_op jit(solution)/shard_map/out_terms/pallas_call | solution.py:199
  87.3 6.1 %all-to-all-done = bf16[8,256,128]{2,1,0:T(8,128)(2,1)S(1)} async-done(((bf16[8,256,128]{2,1,0:T(8,128)(2,1)}), bf16[8,256,128]{2,1,0:T(8,128)(2,1)S(1)}, u32[]{:S(2)}, u32[]{:S(2)}) %all-to-all-start) | async-done | bytes 524320 | tf_op jit(solution)/shard_map/all_to_all | solution.py:298
  93.4 1.3 fusion.9.refs_1_
  96.3 20.3 %all_to_all.10.refs_0_ = bf16[8,256,128]{2,1,0:T(8,128)(2,1)S(1)} all-to-all(bf16[8,256,128]{2,1,0:T(8,128)(2,1)S(1)} %broadcast_in_dim.13), channel_id=1, replica_groups={{0,8,16,24,32,40,48,56},{4,12,20,28,36,44,52,60},{64,72,80,88,96,104,11..., dimensions={0} | all-to-all | bytes 1048576 | tf_op jit(solution)/shard_map/all_to_all | solution.py:309
  116.6 2.4 %collective-permute-start.10 = (bf16[8,256,128]{2,1,0:T(8,128)(2,1)S(1)}, bf16[8,256,128]{2,1,0:T(8,128)(2,1)S(1)}, u32[]{:S(2)}, u32[]{:S(2)}) collective-permute-start(bf16[8,256,128]{2,1,0:T(8,128)(2,1)S(1)} %all_to_all.10.refs_0_), channel_id=1, source_target_pairs={{0,192},{4,196},{8,200},{12,204},{16,208},{20,212},{24,216},{28,22... | collective-permute-start | bytes 1572872 | tf_op jit(solution)/shard_map/ppermute | solution.py:28
  120.0 1.4 collective-permute-start.11
  121.4 9.0 %collective-permute-done.10.refs_3_ = bf16[8,256,128]{2,1,0:T(8,128)(2,1)S(1)} collective-permute-done((bf16[8,256,128]{2,1,0:T(8,128)(2,1)S(1)}, bf16[8,256,128]{2,1,0:T(8,128)(2,1)S(1)}, u32[]{:S(2)}, u32[]{:S(2)}) %collective-permute-start.10) | collective-permute-done | bytes 524320 | tf_op jit(solution)/shard_map/ppermute | solution.py:28
  130.5 11.9 %collective-permute-start.14 = (bf16[8,256,128]{2,1,0:T(8,128)(2,1)S(1)}, bf16[8,256,128]{2,1,0:T(8,128)(2,1)S(1)}, u32[]{:S(2)}, u32[]{:S(2)}) collective-permute-start(bf16[8,256,128]{2,1,0:T(8,128)(2,1)S(1)} %collective-permute-done.10.refs_3_), channel_id=1, source_target_pairs={{0,4},{4,0},{8,12},{12,8},{16,20},{20,16},{24,28},{28,24},{32,36},... | collective-permute-start | bytes 1572872 | tf_op jit(solution)/shard_map/ppermute | solution.py:28
  142.4 3.3 %collective-permute-done.8.refs_1_ = bf16[8,256,128]{2,1,0:T(8,128)(2,1)S(1)} collective-permute-done((bf16[8,256,128]{2,1,0:T(8,128)(2,1)S(1)}, bf16[8,256,128]{2,1,0:T(8,128)(2,1)S(1)}, u32[]{:S(2)}, u32[]{:S(2)}) %collective-permute-start.8) | collective-permute-done | bytes 524320 | tf_op jit(solution)/shard_map/ppermute | solution.py:28
  146.1 1.5 collective-permute-done.12.refs_5_
  147.6 1.7 %in_terms.1 = (f32[7,128,128]{2,1,0:T(8,128)S(1)}, bf16[7,128,128]{2,1,0:T(8,128)(2,1)S(1)}, bf16[7,128,128]{2,1,0:T(8,128)(2,1)S(1)}, bf16[7,128,128]{2,1,0:T(8,128)(2,1)S(1)}) custom-call(s32[4]{0:T(128)S(1)} %copy-done.4, s32[4,7]{1,0:T(4,128)S(1)} %bitcast.18, bf16[256,896]{1,0:T(8,128)(2,1)S(1)} %copy-done.2, ...), custom_call_target="tpu_custom_call" | custom-call | flops 500000000 | bytes 8388608 | tf_op jit(solution)/shard_map/in_terms/pallas_call | solution.py:253
  150.7 2.5 %collective-permute-start.16 = (bf16[7,128,128]{2,1,0:T(8,128)(2,1)S(1)}, bf16[7,128,128]{2,1,0:T(8,128)(2,1)S(1)}, u32[]{:S(2)}, u32[]{:S(2)}) collective-permute-start(bf16[7,128,128]{2,1,0:T(8,128)(2,1)S(1)} %get-tuple-element.26), channel_id=1, source_target_pairs={{0,2},{1,3},{2,0},{3,1},{4,6},{5,7},{6,4},{7,5},{8,10},{9,11},{10,... | collective-permute-start | bytes 688136 | tf_op jit(solution)/shard_map/ppermute | solution.py:32
  154.3 3.2 %collective-permute-done.15 = bf16[7,128,128]{2,1,0:T(8,128)(2,1)S(1)} collective-permute-done((bf16[7,128,128]{2,1,0:T(8,128)(2,1)S(1)}, bf16[7,128,128]{2,1,0:T(8,128)(2,1)S(1)}, u32[]{:S(2)}, u32[]{:S(2)}) %collective-permute-start.15) | collective-permute-done | bytes 229408 | tf_op jit(solution)/shard_map/ppermute | solution.py:32
  157.5 5.9 %collective-permute-done.16 = bf16[7,128,128]{2,1,0:T(8,128)(2,1)S(1)} collective-permute-done((bf16[7,128,128]{2,1,0:T(8,128)(2,1)S(1)}, bf16[7,128,128]{2,1,0:T(8,128)(2,1)S(1)}, u32[]{:S(2)}, u32[]{:S(2)}) %collective-permute-start.16) | collective-permute-done | bytes 229408 | tf_op jit(solution)/shard_map/ppermute | solution.py:32
  (52 shorter events, 9.7 us)
Async XLA Ops:
  7.2 59.8 %all-gather.3.cloned.1.call-start = ((), (), s32[]{:S(2)}) async-start(), calls=%async_computation.4 | async-start | bytes 2359296 | tf_op jit(solution)/shard_map/all_gather | solution.py:293
  8.2 16.4 %copy-start.7 = (bf16[128,256]{1,0:T(8,128)(2,1)}, bf16[128,256]{1,0:T(8,128)(2,1)S(1)}, u32[]{:S(2)}) copy-start(bf16[128,256]{1,0:T(8,128)(2,1)S(1)} %fusion.8.refs_0_) | copy-start | bytes 196612
  8.2 16.4 %collective-permute-start.2 = (bf16[128,256]{1,0:T(8,128)(2,1)S(1)}, bf16[128,256]{1,0:T(8,128)(2,1)S(1)}, u32[]{:S(2)}, u32[]{:S(2)}) collective-permute-start(bf16[128,256]{1,0:T(8,128)(2,1)S(1)} %fusion.8.refs_0_), channel_id=1, source_target_pairs={{0,192},{4,196},{8,200},{12,204},{16,208},{20,212},{24,216},{28,22... | collective-permute-start | bytes 196616 | tf_op jit(solution)/shard_map/ppermute | solution.py:28
  11.6 13.0 %collective-permute-start.1 = (bf16[128,256]{1,0:T(8,128)(2,1)S(1)}, bf16[128,256]{1,0:T(8,128)(2,1)S(1)}, u32[]{:S(2)}, u32[]{:S(2)}) collective-permute-start(bf16[128,256]{1,0:T(8,128)(2,1)S(1)} %fusion.8.refs_0_), channel_id=1, source_target_pairs={{0,128},{4,132},{8,136},{12,140},{16,144},{20,148},{24,152},{28,15... | collective-permute-start | bytes 196616 | tf_op jit(solution)/shard_map/ppermute | solution.py:28
  12.1 12.5 %collective-permute-start = (bf16[128,256]{1,0:T(8,128)(2,1)S(1)}, bf16[128,256]{1,0:T(8,128)(2,1)S(1)}, u32[]{:S(2)}, u32[]{:S(2)}) collective-permute-start(bf16[128,256]{1,0:T(8,128)(2,1)S(1)} %fusion.8.refs_0_), channel_id=1, source_target_pairs={{0,64},{4,68},{8,72},{12,76},{16,80},{20,84},{24,88},{28,92},{32,9... | collective-permute-start | bytes 196616 | tf_op jit(solution)/shard_map/ppermute | solution.py:28
  27.5 5.5 %copy-start.3 = (s32[4]{0:T(128)S(1)}, s32[4]{0:T(128)}, u32[]{:S(2)}) copy-start(s32[4]{0:T(128)} %pad_add_fusion.place) | copy-start | bytes 52
  27.5 5.5 %collective-permute-start.3 = (bf16[32,256,128]{2,1,0:T(8,128)(2,1)}, bf16[32,256,128]{2,1,0:T(8,128)(2,1)S(1)}, u32[]{:S(2)}, u32[]{:S(2)}) collective-permute-start(bf16[32,256,128]{2,1,0:T(8,128)(2,1)} %after.6), channel_id=1, source_target_pairs={{0,4},{4,0},{8,12},{12,8},{16,20},{20,16},{24,28},{28,24},{32,36},... | collective-permute-start | bytes 6291464 | tf_op jit(solution)/shard_map/ppermute | solution.py:28
  33.0 2.2 %copy-start = (f32[32,256,128]{2,1,0:T(8,128)S(1)}, f32[32,256,128]{2,1,0:T(8,128)}, u32[]{:S(2)}) copy-start(f32[32,256,128]{2,1,0:T(8,128)} %get-tuple-element.16) | copy-start | bytes 12582916
  36.6 14.5 %collective-permute-start.4 = (bf16[8,256,128]{2,1,0:T(8,128)(2,1)S(1)}, bf16[8,256,128]{2,1,0:T(8,128)(2,1)S(1)}, u32[]{:S(2)}, u32[]{:S(2)}) collective-permute-start(bf16[8,256,128]{2,1,0:T(8,128)(2,1)S(1)} %get-tuple-element.19), channel_id=1, source_target_pairs={{0,64},{4,68},{8,72},{12,76},{16,80},{20,84},{24,88},{28,92},{32,9... | collective-permute-start | bytes 1572872 | tf_op jit(solution)/shard_map/ppermute | solution.py:28
  38.2 24.6 %collective-permute-start.5 = (bf16[8,256,128]{2,1,0:T(8,128)(2,1)S(1)}, bf16[8,256,128]{2,1,0:T(8,128)(2,1)S(1)}, u32[]{:S(2)}, u32[]{:S(2)}) collective-permute-start(bf16[8,256,128]{2,1,0:T(8,128)(2,1)S(1)} %get-tuple-element.20), channel_id=1, source_target_pairs={{0,128},{4,132},{8,136},{12,140},{16,144},{20,148},{24,152},{28,15... | collective-permute-start | bytes 1572872 | tf_op jit(solution)/shard_map/ppermute | solution.py:28
  40.0 22.9 %collective-permute-start.6 = (bf16[8,256,128]{2,1,0:T(8,128)(2,1)S(1)}, bf16[8,256,128]{2,1,0:T(8,128)(2,1)S(1)}, u32[]{:S(2)}, u32[]{:S(2)}) collective-permute-start(bf16[8,256,128]{2,1,0:T(8,128)(2,1)S(1)} %get-tuple-element.21), channel_id=1, source_target_pairs={{0,192},{4,196},{8,200},{12,204},{16,208},{20,212},{24,216},{28,22... | collective-permute-start | bytes 1572872 | tf_op jit(solution)/shard_map/ppermute | solution.py:28
  64.4 0.7 copy-start.1
  66.9 8.6 %collective-permute-start.7 = (bf16[32,128,256]{2,1,0:T(8,128)(2,1)}, bf16[32,128,256]{2,1,0:T(8,128)(2,1)S(1)}, u32[]{:S(2)}, u32[]{:S(2)}) collective-permute-start(bf16[32,128,256]{2,1,0:T(8,128)(2,1)} %after.7.own_ref), channel_id=1, source_target_pairs={{0,4},{4,0},{8,12},{12,8},{16,20},{20,16},{24,28},{28,24},{32,36},... | collective-permute-start | bytes 6291464 | tf_op jit(solution)/shard_map/ppermute | solution.py:28
  71.5 21.9 %all-to-all-start = ((bf16[8,256,128]{2,1,0:T(8,128)(2,1)}), bf16[8,256,128]{2,1,0:T(8,128)(2,1)S(1)}, u32[]{:S(2)}, u32[]{:S(2)}) async-start(bf16[8,256,128]{2,1,0:T(8,128)(2,1)} %get-tuple-element.23), calls=%async_computation | async-start | bytes 1048576 | tf_op jit(solution)/shard_map/all_to_all | solution.py:298
  75.4 88.8 %reduce-scatter.2.cloned.1.call-start = ((), (), s32[]{:S(2)}) async-start(), calls=%async_computation.3 | async-start | bytes 6881280 | tf_op jit(solution)/shard_map/reduce_scatter | solution.py:303
  75.5 1.4 copy-start.6
  94.7 52.9 %copy-start.2 = (bf16[256,896]{1,0:T(8,128)(2,1)S(1)}, bf16[256,896]{1,0:T(8,128)(2,1)}, u32[]{:S(2)}) copy-start(bf16[256,896]{1,0:T(8,128)(2,1)} %enc_ref.1) | copy-start | bytes 1376260
  94.7 52.9 %copy-start.4 = (s32[4]{0:T(128)S(1)}, s32[4]{0:T(128)}, u32[]{:S(2)}) copy-start(s32[4]{0:T(128)} %pad_add_fusion.place) | copy-start | bytes 52
  94.8 52.9 %copy-start.5 = (s32[7,4]{0,1:T(4,128)S(1)}, s32[7,4]{0,1:T(4,128)}, u32[]{:S(2)}) copy-start(s32[7,4]{0,1:T(4,128)} %param.11) | copy-start | bytes 340
  116.6 13.9 %collective-permute-start.10 = (bf16[8,256,128]{2,1,0:T(8,128)(2,1)S(1)}, bf16[8,256,128]{2,1,0:T(8,128)(2,1)S(1)}, u32[]{:S(2)}, u32[]{:S(2)}) collective-permute-start(bf16[8,256,128]{2,1,0:T(8,128)(2,1)S(1)} %all_to_all.10.refs_0_), channel_id=1, source_target_pairs={{0,192},{4,196},{8,200},{12,204},{16,208},{20,212},{24,216},{28,22... | collective-permute-start | bytes 1572872 | tf_op jit(solution)/shard_map/ppermute | solution.py:28
  119.0 23.4 %collective-permute-start.9 = (bf16[8,256,128]{2,1,0:T(8,128)(2,1)S(1)}, bf16[8,256,128]{2,1,0:T(8,128)(2,1)S(1)}, u32[]{:S(2)}, u32[]{:S(2)}) collective-permute-start(bf16[8,256,128]{2,1,0:T(8,128)(2,1)S(1)} %all_to_all.10.refs_0_), channel_id=1, source_target_pairs={{0,128},{4,132},{8,136},{12,140},{16,144},{20,148},{24,152},{28,15... | collective-permute-start | bytes 1572872 | tf_op jit(solution)/shard_map/ppermute | solution.py:28
  119.4 26.3 %collective-permute-start.8 = (bf16[8,256,128]{2,1,0:T(8,128)(2,1)S(1)}, bf16[8,256,128]{2,1,0:T(8,128)(2,1)S(1)}, u32[]{:S(2)}, u32[]{:S(2)}) collective-permute-start(bf16[8,256,128]{2,1,0:T(8,128)(2,1)S(1)} %all_to_all.10.refs_0_), channel_id=1, source_target_pairs={{0,64},{4,68},{8,72},{12,76},{16,80},{20,84},{24,88},{28,92},{32,9... | collective-permute-start | bytes 1572872 | tf_op jit(solution)/shard_map/ppermute | solution.py:28
  120.0 26.1 %collective-permute-start.11 = (bf16[8,256,128]{2,1,0:T(8,128)(2,1)S(1)}, bf16[8,256,128]{2,1,0:T(8,128)(2,1)S(1)}, u32[]{:S(2)}, u32[]{:S(2)}) collective-permute-start(bf16[8,256,128]{2,1,0:T(8,128)(2,1)S(1)} %all_to_all.10.refs_0_), channel_id=1, source_target_pairs={{0,4},{4,0},{8,12},{12,8},{16,20},{20,16},{24,28},{28,24},{32,36},... | collective-permute-start | bytes 1572872 | tf_op jit(solution)/shard_map/ppermute | solution.py:28
  130.5 15.6 %collective-permute-start.14 = (bf16[8,256,128]{2,1,0:T(8,128)(2,1)S(1)}, bf16[8,256,128]{2,1,0:T(8,128)(2,1)S(1)}, u32[]{:S(2)}, u32[]{:S(2)}) collective-permute-start(bf16[8,256,128]{2,1,0:T(8,128)(2,1)S(1)} %collective-permute-done.10.refs_3_), channel_id=1, source_target_pairs={{0,4},{4,0},{8,12},{12,8},{16,20},{20,16},{24,28},{28,24},{32,36},... | collective-permute-start | bytes 1572872 | tf_op jit(solution)/shard_map/ppermute | solution.py:28
  142.4 3.7 %collective-permute-start.13 = (bf16[8,256,128]{2,1,0:T(8,128)(2,1)S(1)}, bf16[8,256,128]{2,1,0:T(8,128)(2,1)S(1)}, u32[]{:S(2)}, u32[]{:S(2)}) collective-permute-start(bf16[8,256,128]{2,1,0:T(8,128)(2,1)S(1)} %collective-permute-done.9.refs_2_), channel_id=1, source_target_pairs={{0,4},{4,0},{8,12},{12,8},{16,20},{20,16},{24,28},{28,24},{32,36},... | collective-permute-start | bytes 1572872 | tf_op jit(solution)/shard_map/ppermute | solution.py:28
  145.7 1.9 %collective-permute-start.12 = (bf16[8,256,128]{2,1,0:T(8,128)(2,1)S(1)}, bf16[8,256,128]{2,1,0:T(8,128)(2,1)S(1)}, u32[]{:S(2)}, u32[]{:S(2)}) collective-permute-start(bf16[8,256,128]{2,1,0:T(8,128)(2,1)S(1)} %collective-permute-done.8.refs_1_), channel_id=1, source_target_pairs={{0,4},{4,0},{8,12},{12,8},{16,20},{20,16},{24,28},{28,24},{32,36},... | collective-permute-start | bytes 1572872 | tf_op jit(solution)/shard_map/ppermute | solution.py:28
  149.4 8.1 %collective-permute-start.15 = (bf16[7,128,128]{2,1,0:T(8,128)(2,1)S(1)}, bf16[7,128,128]{2,1,0:T(8,128)(2,1)S(1)}, u32[]{:S(2)}, u32[]{:S(2)}) collective-permute-start(bf16[7,128,128]{2,1,0:T(8,128)(2,1)S(1)} %get-tuple-element.25), channel_id=1, source_target_pairs={{0,1},{1,2},{2,3},{3,0},{4,5},{5,6},{6,7},{7,4},{8,9},{9,10},{10,1... | collective-permute-start | bytes 688136 | tf_op jit(solution)/shard_map/ppermute | solution.py:32
  150.7 12.7 %collective-permute-start.16 = (bf16[7,128,128]{2,1,0:T(8,128)(2,1)S(1)}, bf16[7,128,128]{2,1,0:T(8,128)(2,1)S(1)}, u32[]{:S(2)}, u32[]{:S(2)}) collective-permute-start(bf16[7,128,128]{2,1,0:T(8,128)(2,1)S(1)} %get-tuple-element.26), channel_id=1, source_target_pairs={{0,2},{1,3},{2,0},{3,1},{4,6},{5,7},{6,4},{7,5},{8,10},{9,11},{10,... | collective-permute-start | bytes 688136 | tf_op jit(solution)/shard_map/ppermute | solution.py:32
  153.1 10.3 %collective-permute-start.17 = (bf16[7,128,128]{2,1,0:T(8,128)(2,1)S(1)}, bf16[7,128,128]{2,1,0:T(8,128)(2,1)S(1)}, u32[]{:S(2)}, u32[]{:S(2)}) collective-permute-start(bf16[7,128,128]{2,1,0:T(8,128)(2,1)S(1)} %get-tuple-element.27), channel_id=1, source_target_pairs={{0,3},{1,0},{2,1},{3,2},{4,7},{5,4},{6,5},{7,6},{8,11},{9,8},{10,9... | collective-permute-start | bytes 688136 | tf_op jit(solution)/shard_map/ppermute | solution.py:32
Sparse Core Ops, SparseCore 0:
  26.3 40.5 all-gather.2
  94.9 55.9 reduce-scatter.1

commit v5 on v4

--- a/solution.py
+++ b/solution.py
@@ -11,6 +11,7 @@
 BS = 128
 STEP_BLOCKS = 28
 OUT_STEP = 28
+FIRST, LAST = 192, 64
 CORE_STEP = 2
 
 
@@ -45,7 +46,6 @@
 
 def after(value, other):
     anywhere = pl.BlockSpec(memory_space=pl.ANY)
-    other = other[(0,) * (other.ndim - 2)][:16] if other.ndim > 2 else other
     return pl.pallas_call(
         lambda *refs: None,
         in_specs=[anywhere, anywhere],
@@ -56,7 +56,8 @@
     )(value, other)
 
 
-def hidden_kernel(place, contacts, cot_ref, weight_ref, send_ref, keep_ref, mark_ref, total):
+def hidden_kernel(place, contacts, cot_ref, weight_ref, before_ref, send_ref, keep_ref, total):
+    del before_ref
     step = pl.program_id(0)
     core = place[2]
 
@@ -80,10 +81,9 @@
             return carry
 
         lax.fori_loop(0, NX * NZ, write, 0)
-        mark_ref[...] = jnp.zeros_like(mark_ref)
-
-
-def hidden_sums(place, contacts, cotangent, weights):
+
+
+def hidden_sums(place, contacts, cotangent, weights, before):
     rows = cotangent.shape[0]
     count = NX * NZ
     steps = weights.shape[0] // (2 * STEP_BLOCKS)
@@ -95,23 +95,22 @@
             in_specs=[
                 pl.BlockSpec((rows, STEP_BLOCKS * BS), lambda g, *_: (0, g)),
                 pl.BlockSpec((2 * STEP_BLOCKS, BS, BS), lambda g, *_: (g, 0, 0)),
+                pl.BlockSpec(memory_space=pl.ANY),
             ],
             out_specs=[
                 pl.BlockSpec((count, rows, BS), lambda g, *_: (0, 0, 0)),
                 pl.BlockSpec((count, rows, BS), lambda g, *_: (0, 0, 0)),
-                pl.BlockSpec((8, BS), lambda g, *_: (0, 0)),
             ],
             scratch_shapes=[pltpu.VMEM((2 * count, rows, BS), F32)],
         ),
         out_shape=[
             jax.ShapeDtypeStruct((count, rows, BS), BF16),
             jax.ShapeDtypeStruct((count, rows, BS), F32),
-            jax.ShapeDtypeStruct((8, BS), F32),
         ],
         compiler_params=params(56),
         cost_estimate=pl.CostEstimate(flops=3 * 10**9, bytes_accessed=2**24, transcendentals=0),
         name="hidden_sums",
-    )(place, contacts, cotangent, weights)
+    )(place, contacts, cotangent, weights, before)
 
 
 def core_kernel(place, keep_ref, got_ref, *outs):
@@ -168,7 +167,7 @@
     )(place, keep, *got)
 
 
-def out_kernel(place, contacts, cot_ref, own_ref, other_ref, out_ref, held, sems):
+def out_kernel(place, contacts, cot_ref, own_ref, other_ref, out_ref, mark_ref, held, sems):
     step = pl.program_id(0)
     x, core = place[0], place[2]
 
@@ -182,6 +181,7 @@
             copy.start()
         for copy in copies:
             copy.wait()
+        mark_ref[...] = jnp.zeros_like(mark_ref)
 
     def block(k):
         return held[k & 1, ((k >> 1) & (NZ - 1)) * NX + ((x - (k >> 4)) & (NX - 1))]
@@ -206,13 +206,19 @@
                 pl.BlockSpec(memory_space=pl.ANY),
                 pl.BlockSpec(memory_space=pl.ANY),
             ],
-            out_specs=pl.BlockSpec((2 * OUT_STEP, BS, BS), lambda g, *_: (g, 0, 0)),
+            out_specs=[
+                pl.BlockSpec((2 * OUT_STEP, BS, BS), lambda g, *_: (g, 0, 0)),
+                pl.BlockSpec((8, BS), lambda g, *_: (0, 0)),
+            ],
             scratch_shapes=[
                 pltpu.VMEM((NC, NX * NZ, BS, rows), BF16),
                 pltpu.SemaphoreType.DMA((2,)),
             ],
         ),
-        out_shape=jax.ShapeDtypeStruct((2 * count, BS, BS), BF16),
+        out_shape=[
+            jax.ShapeDtypeStruct((2 * count, BS, BS), BF16),
+            jax.ShapeDtypeStruct((8, BS), F32),
+        ],
         compiler_params=params(56),
         cost_estimate=pl.CostEstimate(flops=3 * 10**9, bytes_accessed=2**24, transcendentals=0),
         name="out_terms",
@@ -220,12 +226,16 @@
 
 
 def in_kernel(place, contacts, enc_ref, *refs):
-    parts, outs = refs[: NC * NX], refs[NC * NX : NC * NX + NY]
-    held, made, sems = refs[NC * NX + NY :]
+    firsts, lasts = refs[: NC * NX], refs[NC * NX : NC * NX + NC]
+    outs, (held, made, sems) = refs[NC * NX + NC :][:NY], refs[NC * NX + NC + NY :]
     x, core, y = place[0], place[2], place[3]
-    copies = [
-        pltpu.make_async_copy(part, held.at[n], sems.at[n]) for n, part in enumerate(parts)
-    ]
+    copies = []
+    for n, first in enumerate(firsts):
+        last = lasts[n // NX].at[:, n % NX]
+        copies += [
+            pltpu.make_async_copy(first, held.at[n, :, pl.ds(0, FIRST)], sems.at[n, 0]),
+            pltpu.make_async_copy(last, held.at[n, :, pl.ds(FIRST, LAST)], sems.at[n, 1]),
+        ]
     for copy in copies:
         copy.start()
     for copy in copies:
@@ -252,12 +262,12 @@
     whole = pl.BlockSpec(memory_space=pltpu.VMEM)
     return pl.pallas_call(
         in_kernel,
-        in_specs=[smem, smem, whole] + [pl.BlockSpec(memory_space=pl.ANY)] * (NC * NX),
+        in_specs=[smem, smem, whole] + [pl.BlockSpec(memory_space=pl.ANY)] * (NC * NX + NC),
         out_specs=[whole] * NY,
         scratch_shapes=[
             pltpu.VMEM((NC * NX, NZ, rows, BS), BF16),
             pltpu.VMEM((per_in * count, BS, BS), F32),
-            pltpu.SemaphoreType.DMA((NC * NX,)),
+            pltpu.SemaphoreType.DMA((NC * NX, 2)),
         ],
         out_shape=[jax.ShapeDtypeStruct((each, BS, BS), BF16 if d else F32) for d in range(NY)],
         compiler_params=params(14),
@@ -285,30 +295,30 @@
     pre = hidden_pre.astype(F32)
 
     activation = jax.nn.silu(pre).astype(BF16).T
-    arrived = [moved(activation, dx=d) for d in range(1, NX)]
-
-    send, keep, mark = hidden_sums(place, out_index, cotangent, out_weights)
-    along_x = jnp.stack([after(activation, mark)] + arrived)
-    send = after(send, along_x)
+    along_x = jnp.stack([activation] + [moved(activation, dx=d) for d in range(1, NX)])
     act_own = lax.all_gather(along_x, "blk", axis_index_groups=LINES)
     act_own = act_own.reshape(NZ * NX, BS, -1)
+    send, keep = hidden_sums(place, out_index, cotangent, out_weights, along_x)
 
     by_x = core_sums(place, keep, moved(send, dc=1))
     by_z, own_z = line_sums(place, by_x[0], *[moved(by_x[d], dx=d) for d in range(1, NX)])
     got = lax.all_to_all(by_z, "blk", 0, 0, axis_index_groups=LINES)
+
     act_own = after(act_own, own_z)
-    terms = out_terms(place, out_index, cotangent, act_own, moved(act_own, dc=1))
-    both = got[0, :16] + terms[0, :16]
-    terms = after(terms, both)
-    out_grad = lax.psum_scatter(terms, "smp", scatter_dimension=0, tiled=True)
-
-    grad_act = sum_parts(got, after(own_z, both), place[1])
-    grad_pre = (grad_act * silu_slope(pre)).astype(BF16)
-
-    copies = jnp.broadcast_to(grad_pre, (NZ, *grad_pre.shape))
+    terms, done = out_terms(place, out_index, cotangent, act_own, moved(act_own, dc=1))
+    grad_act = sum_parts(got, after(own_z, done), place[1])
+    slope = silu_slope(pre)
+    first = (grad_act[:FIRST] * slope[:FIRST]).astype(BF16)
+    last = (grad_act[FIRST:] * slope[FIRST:]).astype(BF16)
+    out_grad = lax.psum_scatter(after(terms, first), "smp", scatter_dimension=0, tiled=True)
+
+    last_x = jnp.stack([last] + [moved(last, dx=d) for d in range(1, NX)])
+    copies = jnp.broadcast_to(first, (NZ, *first.shape))
     along_z = lax.all_to_all(copies, "blk", 0, 0, axis_index_groups=LINES)
     own = [along_z] + [moved(along_z, dx=d) for d in range(1, NX)]
-    parts = own + [moved(part, dc=1) for part in own]
+    copies = jnp.broadcast_to(last_x, (NZ, *last_x.shape))
+    last_own = lax.all_to_all(copies, "blk", 0, 0, axis_index_groups=LINES)
+    parts = own + [moved(part, dc=1) for part in own] + [last_own, moved(last_own, dc=1)]
 
     mine, *away = in_terms(place, in_index, encodings, parts)
     in_grad = sum((moved_smp(a, d + 1).astype(F32) for d, a in enumerate(away)), mine).astype(BF16)

time: 172 us -> 171 us (level)
  waiting for transfers between devices: 55.9 us -> 76.2 us
  blocking collectives: 20.3 us -> 0 us
    all_to_all x0 -> x2, waiting for transfers between devices: none -> 24.1 us  [the longest x1 15.2 us: per_device(): last_own = lax.all_to_all(copies, 'blk', 0, 0, axis_index_groups=LINES)]
    all_to_all x1 -> x0, blocking collectives: 20.3 us -> none  [per_device(): along_z = lax.all_to_all(copies, 'blk', 0, 0, axis_index_groups=LINES)]
    ppermute x15 -> x19, starting transfers between devices: 33.2 us -> 21 us  [moved(): return lax.ppermute(value, 'blk', pairs)]
    all_to_all x0 -> x2, starting transfers between devices: none -> 6.94 us  [the longest x1 3.49 us: per_device(): last_own = lax.all_to_all(copies, 'blk', 0, 0, axis_index_groups=LINES)]
    all_to_all x1, starting transfers between devices: 3.87 us -> 8.23 us  [per_device(): got = lax.all_to_all(by_z, 'blk', 0, 0, axis_index_groups=LINES)]
    ppermute x15 -> x19, waiting for transfers between devices: 38.9 us -> 36.8 us  [moved(): return lax.ppermute(value, 'blk', pairs)]
    all_gather x1, waiting for transfers between devices: 1.83 us -> 0.01 us  [per_device(): act_own = lax.all_gather(along_x, 'blk', axis_index_groups=LINES)]
    unnamed x17 -> x16, local copies, waits for them, and re-layouts: 5.19 us -> 5.01 us
  transfers between devices with their start and end apart: 21 -> 27, of which waited for: 11 -> 14; matrix products, arithmetic and copies ran while one was open for 2% -> 2% of each run, Pallas kernels for 15% -> 16%
where the time goes in v5:
time: 171 us; the launch traced here: 170 us
  waiting for transfers between devices  76.2 us (45%)
  starting transfers between devices  41.3 us (24%)
  Pallas kernels  26.8 us (16%)
  between operations  14.2 us (8%)
  local copies, waits for them, and re-layouts  7.61 us (4%)
  other arithmetic  4.07 us (2%)
    ppermute x19, waiting for transfers between devices, moved(): return lax.ppermute(value, 'blk', pairs)  36.8 us
    ppermute x19, starting transfers between devices, moved(): return lax.ppermute(value, 'blk', pairs)  21 us
    all_to_all x1, waiting for transfers between devices, per_device(): last_own = lax.all_to_all(copies, 'blk', 0, 0, axis_index_groups=LINES)  15.2 us
    pallas_call x1, Pallas kernels, hidden_sums(): pl.pallas_call(hidden_kernel, grid_spec=pltpu.PrefetchScalarGridSpec(num_...  11.3 us
    pallas_call x1, Pallas kernels, out_terms(): pl.pallas_call(out_kernel, grid_spec=pltpu.PrefetchScalarGridSpec(num_sca...  10.4 us
    ppermute x3, waiting for transfers between devices, moved_smp(): return lax.ppermute(value, 'smp', [(i, (i + dy) % NY) for i in range(NY)])  9.18 us
    all_to_all x1, waiting for transfers between devices, per_device(): along_z = lax.all_to_all(copies, 'blk', 0, 0, axis_index_groups=LINES)  8.87 us
    all_to_all x1, starting transfers between devices, per_device(): got = lax.all_to_all(by_z, 'blk', 0, 0, axis_index_groups=LINES)  8.23 us
  transfers between devices with their start and end apart: 27, of which 14 were waited for; matrix products, arithmetic and copies ran while one was open for 2% of the time, Pallas kernels for 16%

profile of v5, /device:TPU:1, one launch (start us, length us, event | category | flops | bytes accessed | tf_op | source)
XLA Modules:
  0.0 170.2 jit_solution(12309954067364631156)
XLA Ops:
  8.1 3.7 %collective-permute-start.1 = (bf16[128,256]{0,1:T(8,128)(2,1)S(1)}, bf16[128,256]{0,1:T(8,128)(2,1)S(1)}, u32[]{:S(2)}, u32[]{:S(2)}) collective-permute-start(bf16[128,256]{0,1:T(8,128)(2,1)S(1)} %get-tuple-element.32), channel_id=1, source_target_pairs={{0,128},{4,132},{8,136},{12,140},{16,144},{20,148},{24,152},{28,15... | collective-permute-start | bytes 196616 | tf_op jit(solution)/shard_map/ppermute | solution.py:29
  12.1 2.4 %collective-permute-start.2 = (bf16[128,256]{0,1:T(8,128)(2,1)S(1)}, bf16[128,256]{0,1:T(8,128)(2,1)S(1)}, u32[]{:S(2)}, u32[]{:S(2)}) collective-permute-start(bf16[128,256]{0,1:T(8,128)(2,1)S(1)} %get-tuple-element.32), channel_id=1, source_target_pairs={{0,192},{4,196},{8,200},{12,204},{16,208},{20,212},{24,216},{28,22... | collective-permute-start | bytes 196616 | tf_op jit(solution)/shard_map/ppermute | solution.py:29
  14.5 2.4 %collective-permute-done = bf16[128,256]{0,1:T(8,128)(2,1)S(1)} collective-permute-done((bf16[128,256]{0,1:T(8,128)(2,1)S(1)}, bf16[128,256]{0,1:T(8,128)(2,1)S(1)}, u32[]{:S(2)}, u32[]{:S(2)}) %collective-permute-start) | collective-permute-done | bytes 65568 | tf_op jit(solution)/shard_map/ppermute | solution.py:29
  18.4 11.3 %hidden_sums.1 = (bf16[32,256,128]{2,1,0:T(8,128)(2,1)}, f32[32,256,128]{2,1,0:T(8,128)}) custom-call(s32[4]{0:T(128)} %pad_add_fusion.place, s32[2,84]{1,0:T(2,128)} %bitcast.30, bf16[256,10752]{1,0:T(8,128)(2,1)} %cot_ref.3, bf16[168,128,128]{2,1,0:T(8,128)(2,1)} %weight_ref.1, bf16[4,128,256]{2,1,0:T(8,128)(2,1)} %copy.13.before_ref), custom_call_target="tpu_custom_call" | custom-call | flops 3000000000 | bytes 16777216 | tf_op jit(solution)/shard_map/hidden_sums/pallas_call | solution.py:90
  29.7 1.4 collective-permute-start.3
  31.1 4.0 %collective-permute-done.3 = bf16[32,256,128]{2,1,0:T(8,128)(2,1)S(1)} collective-permute-done((bf16[32,256,128]{2,1,0:T(8,128)(2,1)}, bf16[32,256,128]{2,1,0:T(8,128)(2,1)S(1)}, u32[]{:S(2)}, u32[]{:S(2)}) %collective-permute-start.3) | collective-permute-done | bytes 2097184 | tf_op jit(solution)/shard_map/ppermute | solution.py:29
  35.1 2.2 %copy-done = f32[32,256,128]{2,1,0:T(8,128)S(1)} copy-done((f32[32,256,128]{2,1,0:T(8,128)S(1)}, f32[32,256,128]{2,1,0:T(8,128)}, u32[]{:S(2)}) %copy-start) | copy-done | bytes 4194328
  37.3 1.4 core_sums.1
  39.5 3.4 %collective-permute-start.5 = (bf16[8,256,128]{2,1,0:T(8,128)(2,1)S(1)}, bf16[8,256,128]{2,1,0:T(8,128)(2,1)S(1)}, u32[]{:S(2)}, u32[]{:S(2)}) collective-permute-start(bf16[8,256,128]{2,1,0:T(8,128)(2,1)S(1)} %get-tuple-element.20), channel_id=1, source_target_pairs={{0,128},{4,132},{8,136},{12,140},{16,144},{20,148},{24,152},{28,15... | collective-permute-start | bytes 1572872 | tf_op jit(solution)/shard_map/ppermute | solution.py:29
  42.9 10.9 %collective-permute-done.4.a_ref = bf16[8,256,128]{2,1,0:T(8,128)(2,1)S(1)} collective-permute-done((bf16[8,256,128]{2,1,0:T(8,128)(2,1)S(1)}, bf16[8,256,128]{2,1,0:T(8,128)(2,1)S(1)}, u32[]{:S(2)}, u32[]{:S(2)}) %collective-permute-start.4) | collective-permute-done | bytes 524320 | tf_op jit(solution)/shard_map/ppermute | solution.py:29
  53.8 12.0 %collective-permute-done.5.b_ref = bf16[8,256,128]{2,1,0:T(8,128)(2,1)S(1)} collective-permute-done((bf16[8,256,128]{2,1,0:T(8,128)(2,1)S(1)}, bf16[8,256,128]{2,1,0:T(8,128)(2,1)S(1)}, u32[]{:S(2)}, u32[]{:S(2)}) %collective-permute-start.5) | collective-permute-done | bytes 524320 | tf_op jit(solution)/shard_map/ppermute | solution.py:29
  65.8 1.6 line_sums.1
  68.0 1.2 collective-permute-start.7
  69.2 8.2 %all-to-all-start = ((bf16[8,256,128]{2,1,0:T(8,128)(2,1)}), bf16[8,256,128]{2,1,0:T(8,128)(2,1)S(1)}, u32[]{:S(2)}, u32[]{:S(2)}) async-start(bf16[8,256,128]{2,1,0:T(8,128)(2,1)} %get-tuple-element.25), calls=%async_computation | async-start | bytes 1048576 | tf_op jit(solution)/shard_map/all_to_all | solution.py:305
  77.5 1.4 copy-done.7
  78.9 10.4 %out_terms.1 = (bf16[168,128,128]{2,1,0:T(8,128)(2,1)}, f32[8,128]{1,0:T(8,128)}) custom-call(s32[4]{0:T(128)} %pad_add_fusion.place, s32[2,84]{1,0:T(2,128)} %bitcast.31, bf16[256,10752]{1,0:T(8,128)(2,1)} %cot_ref.3, bf16[32,128,256]{2,1,0:T(8,128)(2,1)} %after.3.own_ref, bf16[32,128,256]{2,1,0:T(8,128)(2,1)} %copy-done.7), custom_call_target="tpu_custom_call" | custom-call | flops 3000000000 | bytes 16777216 | tf_op jit(solution)/shard_map/out_terms/pallas_call | solution.py:199
  89.4 6.1 %all-to-all-done = bf16[8,256,128]{2,1,0:T(8,128)(2,1)S(1)} async-done(((bf16[8,256,128]{2,1,0:T(8,128)(2,1)}), bf16[8,256,128]{2,1,0:T(8,128)(2,1)S(1)}, u32[]{:S(2)}, u32[]{:S(2)}) %all-to-all-start) | async-done | bytes 524320 | tf_op jit(solution)/shard_map/all_to_all | solution.py:305
  98.8 3.5 %all-to-all-start.1 = ((bf16[8,192,128]{2,1,0:T(8,128)(2,1)}), bf16[8,192,128]{2,1,0:T(8,128)(2,1)S(1)}, u32[]{:S(2)}, u32[]{:S(2)}) async-start(bf16[8,192,128]{2,1,0:T(8,128)(2,1)} %broadcast_in_dim.16), calls=%async_computation.2 | async-start | bytes 786432 | tf_op jit(solution)/shard_map/all_to_all | solution.py:317
  102.3 2.0 %collective-permute-start.17 = (bf16[64,128]{1,0:T(8,128)(2,1)S(1)}, bf16[64,128]{1,0:T(8,128)(2,1)S(1)}, u32[]{:S(2)}, u32[]{:S(2)}) collective-permute-start(bf16[64,128]{1,0:T(8,128)(2,1)S(1)} %fusion.7), channel_id=1, source_target_pairs={{0,192},{4,196},{8,200},{12,204},{16,208},{20,212},{24,216},{28,22... | collective-permute-start | bytes 49160 | tf_op jit(solution)/shard_map/ppermute | solution.py:29
  105.1 3.2 %collective-permute-done.16 = bf16[64,128]{1,0:T(8,128)(2,1)S(1)} collective-permute-done((bf16[64,128]{1,0:T(8,128)(2,1)S(1)}, bf16[64,128]{1,0:T(8,128)(2,1)S(1)}, u32[]{:S(2)}, u32[]{:S(2)}) %collective-permute-start.16) | collective-permute-done | bytes 16416 | tf_op jit(solution)/shard_map/ppermute | solution.py:29
  108.5 8.9 %all-to-all-done.1.refs_0_ = bf16[8,192,128]{2,1,0:T(8,128)(2,1)S(1)} async-done(((bf16[8,192,128]{2,1,0:T(8,128)(2,1)}), bf16[8,192,128]{2,1,0:T(8,128)(2,1)S(1)}, u32[]{:S(2)}, u32[]{:S(2)}) %all-to-all-start.1) | async-done | bytes 393248 | tf_op jit(solution)/shard_map/all_to_all | solution.py:317
  118.3 3.5 %all-to-all-start.2 = ((bf16[8,4,64,128]{3,2,1,0:T(8,128)(2,1)}), bf16[8,4,64,128]{3,2,1,0:T(8,128)(2,1)S(1)}, u32[]{:S(2)}, u32[]{:S(2)}) async-start(bf16[8,4,64,128]{3,2,1,0:T(8,128)(2,1)} %broadcast_in_dim.17), calls=%async_computation.3 | async-start | bytes 1048576 | tf_op jit(solution)/shard_map/all_to_all | solution.py:320
  121.8 2.0 %collective-permute-start.10 = (bf16[8,192,128]{2,1,0:T(8,128)(2,1)S(1)}, bf16[8,192,128]{2,1,0:T(8,128)(2,1)S(1)}, u32[]{:S(2)}, u32[]{:S(2)}) collective-permute-start(bf16[8,192,128]{2,1,0:T(8,128)(2,1)S(1)} %all-to-all-done.1.refs_0_), channel_id=1, source_target_pairs={{0,192},{4,196},{8,200},{12,204},{16,208},{20,212},{24,216},{28,22... | collective-permute-start | bytes 1179656 | tf_op jit(solution)/shard_map/ppermute | solution.py:29
  124.4 15.2 %all-to-all-done.2.refs_8_ = bf16[8,4,64,128]{3,2,1,0:T(8,128)(2,1)S(1)} async-done(((bf16[8,4,64,128]{3,2,1,0:T(8,128)(2,1)}), bf16[8,4,64,128]{3,2,1,0:T(8,128)(2,1)S(1)}, u32[]{:S(2)}, u32[]{:S(2)}) %all-to-all-start.2) | async-done | bytes 524320 | tf_op jit(solution)/shard_map/all_to_all | solution.py:320
  140.2 1.4 collective-permute-start.14
  141.5 2.7 %collective-permute-done.8.refs_1_ = bf16[8,192,128]{2,1,0:T(8,128)(2,1)S(1)} collective-permute-done((bf16[8,192,128]{2,1,0:T(8,128)(2,1)S(1)}, bf16[8,192,128]{2,1,0:T(8,128)(2,1)S(1)}, u32[]{:S(2)}, u32[]{:S(2)}) %collective-permute-start.8) | collective-permute-done | bytes 393248 | tf_op jit(solution)/shard_map/ppermute | solution.py:29
  144.9 1.3 collective-permute-done.12.refs_5_
  146.3 2.0 %in_terms.1 = (f32[7,128,128]{2,1,0:T(8,128)S(1)}, bf16[7,128,128]{2,1,0:T(8,128)(2,1)S(1)}, bf16[7,128,128]{2,1,0:T(8,128)(2,1)S(1)}, bf16[7,128,128]{2,1,0:T(8,128)(2,1)S(1)}) custom-call(s32[4]{0:T(128)S(1)} %copy-done.4, s32[4,7]{1,0:T(4,128)S(1)} %bitcast.22, bf16[256,896]{1,0:T(8,128)(2,1)S(1)} %copy-done.2, ...), custom_call_target="tpu_custom_call" | custom-call | flops 500000000 | bytes 8388608 | tf_op jit(solution)/shard_map/in_terms/pallas_call | solution.py:263
  148.3 1.4 collective-permute-start.19
  149.7 2.6 %collective-permute-start.20 = (bf16[7,128,128]{2,1,0:T(8,128)(2,1)S(1)}, bf16[7,128,128]{2,1,0:T(8,128)(2,1)S(1)}, u32[]{:S(2)}, u32[]{:S(2)}) collective-permute-start(bf16[7,128,128]{2,1,0:T(8,128)(2,1)S(1)} %get-tuple-element.28), channel_id=1, source_target_pairs={{0,2},{1,3},{2,0},{3,1},{4,6},{5,7},{6,4},{7,5},{8,10},{9,11},{10,... | collective-permute-start | bytes 688136 | tf_op jit(solution)/shard_map/ppermute | solution.py:33
  153.4 3.1 %collective-permute-done.19 = bf16[7,128,128]{2,1,0:T(8,128)(2,1)S(1)} collective-permute-done((bf16[7,128,128]{2,1,0:T(8,128)(2,1)S(1)}, bf16[7,128,128]{2,1,0:T(8,128)(2,1)S(1)}, u32[]{:S(2)}, u32[]{:S(2)}) %collective-permute-start.19) | collective-permute-done | bytes 229408 | tf_op jit(solution)/shard_map/ppermute | solution.py:33
  156.5 6.0 %collective-permute-done.20 = bf16[7,128,128]{2,1,0:T(8,128)(2,1)S(1)} collective-permute-done((bf16[7,128,128]{2,1,0:T(8,128)(2,1)S(1)}, bf16[7,128,128]{2,1,0:T(8,128)(2,1)S(1)}, u32[]{:S(2)}, u32[]{:S(2)}) %collective-permute-start.20) | collective-permute-done | bytes 229408 | tf_op jit(solution)/shard_map/ppermute | solution.py:33
  (60 shorter events, 13.3 us)
Async XLA Ops:
  7.2 60.9 %all-gather.3.cloned.1.call-start = ((), (), s32[]{:S(2)}) async-start(), calls=%async_computation.5 | async-start | bytes 2359296 | tf_op jit(solution)/shard_map/all_gather | solution.py:299
  8.1 6.3 %collective-permute-start.1 = (bf16[128,256]{0,1:T(8,128)(2,1)S(1)}, bf16[128,256]{0,1:T(8,128)(2,1)S(1)}, u32[]{:S(2)}, u32[]{:S(2)}) collective-permute-start(bf16[128,256]{0,1:T(8,128)(2,1)S(1)} %get-tuple-element.32), channel_id=1, source_target_pairs={{0,128},{4,132},{8,136},{12,140},{16,144},{20,148},{24,152},{28,15... | collective-permute-start | bytes 196616 | tf_op jit(solution)/shard_map/ppermute | solution.py:29
  11.8 5.0 %collective-permute-start = (bf16[128,256]{0,1:T(8,128)(2,1)S(1)}, bf16[128,256]{0,1:T(8,128)(2,1)S(1)}, u32[]{:S(2)}, u32[]{:S(2)}) collective-permute-start(bf16[128,256]{0,1:T(8,128)(2,1)S(1)} %get-tuple-element.32), channel_id=1, source_target_pairs={{0,64},{4,68},{8,72},{12,76},{16,80},{20,84},{24,88},{28,92},{32,9... | collective-permute-start | bytes 196616 | tf_op jit(solution)/shard_map/ppermute | solution.py:29
  12.1 4.7 %collective-permute-start.2 = (bf16[128,256]{0,1:T(8,128)(2,1)S(1)}, bf16[128,256]{0,1:T(8,128)(2,1)S(1)}, u32[]{:S(2)}, u32[]{:S(2)}) collective-permute-start(bf16[128,256]{0,1:T(8,128)(2,1)S(1)} %get-tuple-element.32), channel_id=1, source_target_pairs={{0,192},{4,196},{8,200},{12,204},{16,208},{20,212},{24,216},{28,22... | collective-permute-start | bytes 196616 | tf_op jit(solution)/shard_map/ppermute | solution.py:29
  18.4 16.7 %copy-start.3 = (s32[4]{0:T(128)S(1)}, s32[4]{0:T(128)}, u32[]{:S(2)}) copy-start(s32[4]{0:T(128)} %pad_add_fusion.place) | copy-start | bytes 52
  29.7 5.4 %collective-permute-start.3 = (bf16[32,256,128]{2,1,0:T(8,128)(2,1)}, bf16[32,256,128]{2,1,0:T(8,128)(2,1)S(1)}, u32[]{:S(2)}, u32[]{:S(2)}) collective-permute-start(bf16[32,256,128]{2,1,0:T(8,128)(2,1)} %get-tuple-element.17), channel_id=1, source_target_pairs={{0,4},{4,0},{8,12},{12,8},{16,20},{20,16},{24,28},{28,24},{32,36},... | collective-permute-start | bytes 6291464 | tf_op jit(solution)/shard_map/ppermute | solution.py:29
  35.1 2.2 %copy-start = (f32[32,256,128]{2,1,0:T(8,128)S(1)}, f32[32,256,128]{2,1,0:T(8,128)}, u32[]{:S(2)}) copy-start(f32[32,256,128]{2,1,0:T(8,128)} %get-tuple-element.16) | copy-start | bytes 12582916
  38.7 15.1 %collective-permute-start.4 = (bf16[8,256,128]{2,1,0:T(8,128)(2,1)S(1)}, bf16[8,256,128]{2,1,0:T(8,128)(2,1)S(1)}, u32[]{:S(2)}, u32[]{:S(2)}) collective-permute-start(bf16[8,256,128]{2,1,0:T(8,128)(2,1)S(1)} %get-tuple-element.19), channel_id=1, source_target_pairs={{0,64},{4,68},{8,72},{12,76},{16,80},{20,84},{24,88},{28,92},{32,9... | collective-permute-start | bytes 1572872 | tf_op jit(solution)/shard_map/ppermute | solution.py:29
  39.5 26.3 %collective-permute-start.5 = (bf16[8,256,128]{2,1,0:T(8,128)(2,1)S(1)}, bf16[8,256,128]{2,1,0:T(8,128)(2,1)S(1)}, u32[]{:S(2)}, u32[]{:S(2)}) collective-permute-start(bf16[8,256,128]{2,1,0:T(8,128)(2,1)S(1)} %get-tuple-element.20), channel_id=1, source_target_pairs={{0,128},{4,132},{8,136},{12,140},{16,144},{20,148},{24,152},{28,15... | collective-permute-start | bytes 1572872 | tf_op jit(solution)/shard_map/ppermute | solution.py:29
  42.9 22.9 %collective-permute-start.6 = (bf16[8,256,128]{2,1,0:T(8,128)(2,1)S(1)}, bf16[8,256,128]{2,1,0:T(8,128)(2,1)S(1)}, u32[]{:S(2)}, u32[]{:S(2)}) collective-permute-start(bf16[8,256,128]{2,1,0:T(8,128)(2,1)S(1)} %get-tuple-element.21), channel_id=1, source_target_pairs={{0,192},{4,196},{8,200},{12,204},{16,208},{20,212},{24,216},{28,22... | collective-permute-start | bytes 1572872 | tf_op jit(solution)/shard_map/ppermute | solution.py:29
  68.0 9.5 %collective-permute-start.7 = (bf16[32,128,256]{2,1,0:T(8,128)(2,1)}, bf16[32,128,256]{2,1,0:T(8,128)(2,1)S(1)}, u32[]{:S(2)}, u32[]{:S(2)}) collective-permute-start(bf16[32,128,256]{2,1,0:T(8,128)(2,1)} %after.3.own_ref), channel_id=1, source_target_pairs={{0,4},{4,0},{8,12},{12,8},{16,20},{20,16},{24,28},{28,24},{32,36},... | collective-permute-start | bytes 6291464 | tf_op jit(solution)/shard_map/ppermute | solution.py:29
  69.2 26.3 %all-to-all-start = ((bf16[8,256,128]{2,1,0:T(8,128)(2,1)}), bf16[8,256,128]{2,1,0:T(8,128)(2,1)S(1)}, u32[]{:S(2)}, u32[]{:S(2)}) async-start(bf16[8,256,128]{2,1,0:T(8,128)(2,1)} %get-tuple-element.25), calls=%async_computation | async-start | bytes 1048576 | tf_op jit(solution)/shard_map/all_to_all | solution.py:305
  77.4 85.9 %reduce-scatter.2.cloned.1.call-start = ((), (), s32[]{:S(2)}) async-start(), calls=%async_computation.4 | async-start | bytes 6881280 | tf_op jit(solution)/shard_map/reduce_scatter | solution.py:313
  98.0 48.3 %copy-start.2 = (bf16[256,896]{1,0:T(8,128)(2,1)S(1)}, bf16[256,896]{1,0:T(8,128)(2,1)}, u32[]{:S(2)}) copy-start(bf16[256,896]{1,0:T(8,128)(2,1)} %enc_ref.1) | copy-start | bytes 1376260
  98.0 48.3 %copy-start.4 = (s32[4]{0:T(128)S(1)}, s32[4]{0:T(128)}, u32[]{:S(2)}) copy-start(s32[4]{0:T(128)} %pad_add_fusion.place) | copy-start | bytes 52
  98.0 48.3 %copy-start.5 = (s32[7,4]{0,1:T(4,128)S(1)}, s32[7,4]{0,1:T(4,128)}, u32[]{:S(2)}) copy-start(s32[7,4]{0,1:T(4,128)} %param.11) | copy-start | bytes 340
  98.8 18.5 %all-to-all-start.1 = ((bf16[8,192,128]{2,1,0:T(8,128)(2,1)}), bf16[8,192,128]{2,1,0:T(8,128)(2,1)S(1)}, u32[]{:S(2)}, u32[]{:S(2)}) async-start(bf16[8,192,128]{2,1,0:T(8,128)(2,1)} %broadcast_in_dim.16), calls=%async_computation.2 | async-start | bytes 786432 | tf_op jit(solution)/shard_map/all_to_all | solution.py:317
  102.3 2.8 %collective-permute-start.17 = (bf16[64,128]{1,0:T(8,128)(2,1)S(1)}, bf16[64,128]{1,0:T(8,128)(2,1)S(1)}, u32[]{:S(2)}, u32[]{:S(2)}) collective-permute-start(bf16[64,128]{1,0:T(8,128)(2,1)S(1)} %fusion.7), channel_id=1, source_target_pairs={{0,192},{4,196},{8,200},{12,204},{16,208},{20,212},{24,216},{28,22... | collective-permute-start | bytes 49160 | tf_op jit(solution)/shard_map/ppermute | solution.py:29
  104.3 4.1 %collective-permute-start.16 = (bf16[64,128]{1,0:T(8,128)(2,1)S(1)}, bf16[64,128]{1,0:T(8,128)(2,1)S(1)}, u32[]{:S(2)}, u32[]{:S(2)}) collective-permute-start(bf16[64,128]{1,0:T(8,128)(2,1)S(1)} %fusion.7), channel_id=1, source_target_pairs={{0,128},{4,132},{8,136},{12,140},{16,144},{20,148},{24,152},{28,15... | collective-permute-start | bytes 49160 | tf_op jit(solution)/shard_map/ppermute | solution.py:29
  104.3 4.2 %collective-permute-start.15 = (bf16[64,128]{1,0:T(8,128)(2,1)S(1)}, bf16[64,128]{1,0:T(8,128)(2,1)S(1)}, u32[]{:S(2)}, u32[]{:S(2)}) collective-permute-start(bf16[64,128]{1,0:T(8,128)(2,1)S(1)} %fusion.7), channel_id=1, source_target_pairs={{0,64},{4,68},{8,72},{12,76},{16,80},{20,84},{24,88},{28,92},{32,9... | collective-permute-start | bytes 49160 | tf_op jit(solution)/shard_map/ppermute | solution.py:29
  118.3 21.4 %all-to-all-start.2 = ((bf16[8,4,64,128]{3,2,1,0:T(8,128)(2,1)}), bf16[8,4,64,128]{3,2,1,0:T(8,128)(2,1)S(1)}, u32[]{:S(2)}, u32[]{:S(2)}) async-start(bf16[8,4,64,128]{3,2,1,0:T(8,128)(2,1)} %broadcast_in_dim.17), calls=%async_computation.3 | async-start | bytes 1048576 | tf_op jit(solution)/shard_map/all_to_all | solution.py:320
  121.8 18.4 %collective-permute-start.10 = (bf16[8,192,128]{2,1,0:T(8,128)(2,1)S(1)}, bf16[8,192,128]{2,1,0:T(8,128)(2,1)S(1)}, u32[]{:S(2)}, u32[]{:S(2)}) collective-permute-start(bf16[8,192,128]{2,1,0:T(8,128)(2,1)S(1)} %all-to-all-done.1.refs_0_), channel_id=1, source_target_pairs={{0,192},{4,196},{8,200},{12,204},{16,208},{20,212},{24,216},{28,22... | collective-permute-start | bytes 1179656 | tf_op jit(solution)/shard_map/ppermute | solution.py:29
  123.7 17.8 %collective-permute-start.9 = (bf16[8,192,128]{2,1,0:T(8,128)(2,1)S(1)}, bf16[8,192,128]{2,1,0:T(8,128)(2,1)S(1)}, u32[]{:S(2)}, u32[]{:S(2)}) collective-permute-start(bf16[8,192,128]{2,1,0:T(8,128)(2,1)S(1)} %all-to-all-done.1.refs_0_), channel_id=1, source_target_pairs={{0,128},{4,132},{8,136},{12,140},{16,144},{20,148},{24,152},{28,15... | collective-permute-start | bytes 1179656 | tf_op jit(solution)/shard_map/ppermute | solution.py:29
  123.7 20.5 %collective-permute-start.8 = (bf16[8,192,128]{2,1,0:T(8,128)(2,1)S(1)}, bf16[8,192,128]{2,1,0:T(8,128)(2,1)S(1)}, u32[]{:S(2)}, u32[]{:S(2)}) collective-permute-start(bf16[8,192,128]{2,1,0:T(8,128)(2,1)S(1)} %all-to-all-done.1.refs_0_), channel_id=1, source_target_pairs={{0,64},{4,68},{8,72},{12,76},{16,80},{20,84},{24,88},{28,92},{32,9... | collective-permute-start | bytes 1179656 | tf_op jit(solution)/shard_map/ppermute | solution.py:29
  139.6 5.3 %collective-permute-start.18 = (bf16[8,4,64,128]{3,2,1,0:T(8,128)(2,1)S(1)}, bf16[8,4,64,128]{3,2,1,0:T(8,128)(2,1)S(1)}, u32[]{:S(2)}, u32[]{:S(2)}) collective-permute-start(bf16[8,4,64,128]{3,2,1,0:T(8,128)(2,1)S(1)} %all-to-all-done.2.refs_8_), channel_id=1, source_target_pairs={{0,4},{4,0},{8,12},{12,8},{16,20},{20,16},{24,28},{28,24},{32,36},... | collective-permute-start | bytes 1572872 | tf_op jit(solution)/shard_map/ppermute | solution.py:29
  140.1 4.8 %collective-permute-start.11 = (bf16[8,192,128]{2,1,0:T(8,128)(2,1)S(1)}, bf16[8,192,128]{2,1,0:T(8,128)(2,1)S(1)}, u32[]{:S(2)}, u32[]{:S(2)}) collective-permute-start(bf16[8,192,128]{2,1,0:T(8,128)(2,1)S(1)} %all-to-all-done.1.refs_0_), channel_id=1, source_target_pairs={{0,4},{4,0},{8,12},{12,8},{16,20},{20,16},{24,28},{28,24},{32,36},... | collective-permute-start | bytes 1179656 | tf_op jit(solution)/shard_map/ppermute | solution.py:29
  140.2 4.8 %collective-permute-start.14 = (bf16[8,192,128]{2,1,0:T(8,128)(2,1)S(1)}, bf16[8,192,128]{2,1,0:T(8,128)(2,1)S(1)}, u32[]{:S(2)}, u32[]{:S(2)}) collective-permute-start(bf16[8,192,128]{2,1,0:T(8,128)(2,1)S(1)} %collective-permute-done.10.refs_3_), channel_id=1, source_target_pairs={{0,4},{4,0},{8,12},{12,8},{16,20},{20,16},{24,28},{28,24},{32,36},... | collective-permute-start | bytes 1179656 | tf_op jit(solution)/shard_map/ppermute | solution.py:29
  141.5 3.4 %collective-permute-start.13 = (bf16[8,192,128]{2,1,0:T(8,128)(2,1)S(1)}, bf16[8,192,128]{2,1,0:T(8,128)(2,1)S(1)}, u32[]{:S(2)}, u32[]{:S(2)}) collective-permute-start(bf16[8,192,128]{2,1,0:T(8,128)(2,1)S(1)} %collective-permute-done.9.refs_2_), channel_id=1, source_target_pairs={{0,4},{4,0},{8,12},{12,8},{16,20},{20,16},{24,28},{28,24},{32,36},... | collective-permute-start | bytes 1179656 | tf_op jit(solution)/shard_map/ppermute | solution.py:29
  144.2 2.1 %collective-permute-start.12 = (bf16[8,192,128]{2,1,0:T(8,128)(2,1)S(1)}, bf16[8,192,128]{2,1,0:T(8,128)(2,1)S(1)}, u32[]{:S(2)}, u32[]{:S(2)}) collective-permute-start(bf16[8,192,128]{2,1,0:T(8,128)(2,1)S(1)} %collective-permute-done.8.refs_1_), channel_id=1, source_target_pairs={{0,4},{4,0},{8,12},{12,8},{16,20},{20,16},{24,28},{28,24},{32,36},... | collective-permute-start | bytes 1179656 | tf_op jit(solution)/shard_map/ppermute | solution.py:29
  148.3 8.2 %collective-permute-start.19 = (bf16[7,128,128]{2,1,0:T(8,128)(2,1)S(1)}, bf16[7,128,128]{2,1,0:T(8,128)(2,1)S(1)}, u32[]{:S(2)}, u32[]{:S(2)}) collective-permute-start(bf16[7,128,128]{2,1,0:T(8,128)(2,1)S(1)} %get-tuple-element.27), channel_id=1, source_target_pairs={{0,1},{1,2},{2,3},{3,0},{4,5},{5,6},{6,7},{7,4},{8,9},{9,10},{10,1... | collective-permute-start | bytes 688136 | tf_op jit(solution)/shard_map/ppermute | solution.py:33
  149.7 12.9 %collective-permute-start.20 = (bf16[7,128,128]{2,1,0:T(8,128)(2,1)S(1)}, bf16[7,128,128]{2,1,0:T(8,128)(2,1)S(1)}, u32[]{:S(2)}, u32[]{:S(2)}) collective-permute-start(bf16[7,128,128]{2,1,0:T(8,128)(2,1)S(1)} %get-tuple-element.28), channel_id=1, source_target_pairs={{0,2},{1,3},{2,0},{3,1},{4,6},{5,7},{6,4},{7,5},{8,10},{9,11},{10,... | collective-permute-start | bytes 688136 | tf_op jit(solution)/shard_map/ppermute | solution.py:33
  152.3 10.3 %collective-permute-start.21 = (bf16[7,128,128]{2,1,0:T(8,128)(2,1)S(1)}, bf16[7,128,128]{2,1,0:T(8,128)(2,1)S(1)}, u32[]{:S(2)}, u32[]{:S(2)}) collective-permute-start(bf16[7,128,128]{2,1,0:T(8,128)(2,1)S(1)} %get-tuple-element.29), channel_id=1, source_target_pairs={{0,3},{1,0},{2,1},{3,2},{4,7},{5,4},{6,5},{7,6},{8,11},{9,8},{10,9... | collective-permute-start | bytes 688136 | tf_op jit(solution)/shard_map/ppermute | solution.py:33
  (3 other events, 2.8 us)
Sparse Core Ops, SparseCore 0:
  17.9 41.2 all-gather.2
  97.3 55.4 reduce-scatter.1

commit v6 on v5

--- a/solution.py
+++ b/solution.py
@@ -11,7 +11,7 @@
 BS = 128
 STEP_BLOCKS = 28
 OUT_STEP = 28
-FIRST, LAST = 192, 64
+FIRST, LAST = 208, 48
 CORE_STEP = 2
 
 
@@ -44,7 +44,7 @@
     return lax.dot_general(lhs, rhs, ((over[:1], over[1:]), ((), ())), preferred_element_type=F32)
 
 
-def after(value, other):
+def after(value, other, mib=56):
     anywhere = pl.BlockSpec(memory_space=pl.ANY)
     return pl.pallas_call(
         lambda *refs: None,
@@ -107,7 +107,7 @@
             jax.ShapeDtypeStruct((count, rows, BS), BF16),
             jax.ShapeDtypeStruct((count, rows, BS), F32),
         ],
-        compiler_params=params(56),
+        compiler_params=params(44),
         cost_estimate=pl.CostEstimate(flops=3 * 10**9, bytes_accessed=2**24, transcendentals=0),
         name="hidden_sums",
     )(place, contacts, cotangent, weights, before)
@@ -219,7 +219,7 @@
             jax.ShapeDtypeStruct((2 * count, BS, BS), BF16),
             jax.ShapeDtypeStruct((8, BS), F32),
         ],
-        compiler_params=params(56),
+        compiler_params=params(48),
         cost_estimate=pl.CostEstimate(flops=3 * 10**9, bytes_accessed=2**24, transcendentals=0),
         name="out_terms",
     )(place, contacts, cotangent, own, other)

time: 171 us -> 170 us (level)
  starting transfers between devices: 41.3 us -> 50.6 us
  waiting for transfers between devices: 76.2 us -> 71.1 us
  Pallas kernels: 26.8 us -> 22.5 us
    all_to_all x1, waiting for transfers between devices: 15.2 us -> 0.01 us  [per_device(): last_own = lax.all_to_all(copies, 'blk', 0, 0, axis_index_groups=LINES)]
    ppermute x19, starting transfers between devices: 21 us -> 30.3 us  [moved(): return lax.ppermute(value, 'blk', pairs)]
    ppermute x19, waiting for transfers between devices: 36.8 us -> 44.7 us  [moved(): return lax.ppermute(value, 'blk', pairs)]
    pallas_call x1, Pallas kernels: 11.3 us -> 8.39 us  [hidden_sums(): pl.pallas_call(hidden_kernel, grid_spec=pltpu.PrefetchScalarGridSpec(num_...]
    pallas_call x1, Pallas kernels: 10.4 us -> 8.21 us  [out_terms(): pl.pallas_call(out_kernel, grid_spec=pltpu.PrefetchScalarGridSpec(num_sca...]
    unnamed x16 -> x18, local copies, waits for them, and re-layouts: 5.01 us -> 5.25 us
  transfers between devices with their start and end apart: 27 -> 27, of which waited for: 14 -> 15; matrix products, arithmetic and copies ran while one was open for 2% -> 1% of each run, Pallas kernels for 16% -> 13%
where the time goes in v6:
time: 170 us
  waiting for transfers between devices  71.1 us (42%)
  starting transfers between devices  50.6 us (30%)
  Pallas kernels  22.5 us (13%)
  between operations  14.2 us (8%)
  local copies, waits for them, and re-layouts  7.74 us (5%)
  other arithmetic  3.57 us (2%)
    ppermute x19, waiting for transfers between devices, moved(): return lax.ppermute(value, 'blk', pairs)  44.7 us
    ppermute x19, starting transfers between devices, moved(): return lax.ppermute(value, 'blk', pairs)  30.3 us
    all_to_all x1, waiting for transfers between devices, per_device(): along_z = lax.all_to_all(copies, 'blk', 0, 0, axis_index_groups=LINES)  9.62 us
    ppermute x3, waiting for transfers between devices, moved_smp(): return lax.ppermute(value, 'smp', [(i, (i + dy) % NY) for i in range(NY)])  9.23 us
    pallas_call x1, Pallas kernels, hidden_sums(): pl.pallas_call(hidden_kernel, grid_spec=pltpu.PrefetchScalarGridSpec(num_...  8.39 us
    pallas_call x1, Pallas kernels, out_terms(): pl.pallas_call(out_kernel, grid_spec=pltpu.PrefetchScalarGridSpec(num_sca...  8.21 us
    all_to_all x1, starting transfers between devices, per_device(): got = lax.all_to_all(by_z, 'blk', 0, 0, axis_index_groups=LINES)  8.18 us
    all_to_all x1, waiting for transfers between devices, per_device(): got = lax.all_to_all(by_z, 'blk', 0, 0, axis_index_groups=LINES)  7.54 us
  transfers between devices with their start and end apart: 27, of which 15 were waited for; matrix products, arithmetic and copies ran while one was open for 1% of the time, Pallas kernels for 13%

profile of v6, /device:TPU:1, one launch (start us, length us, event | category | flops | bytes accessed | tf_op | source)
XLA Modules:
  0.0 169.7 jit_solution(16555154704720398435)
XLA Ops:
  8.1 3.7 %collective-permute-start.1 = (bf16[128,256]{0,1:T(8,128)(2,1)S(1)}, bf16[128,256]{0,1:T(8,128)(2,1)S(1)}, u32[]{:S(2)}, u32[]{:S(2)}) collective-permute-start(bf16[128,256]{0,1:T(8,128)(2,1)S(1)} %get-tuple-element.32), channel_id=1, source_target_pairs={{0,128},{4,132},{8,136},{12,140},{16,144},{20,148},{24,152},{28,15... | collective-permute-start | bytes 196616 | tf_op jit(solution)/shard_map/ppermute | solution.py:29
  12.1 2.4 %collective-permute-start.2 = (bf16[128,256]{0,1:T(8,128)(2,1)S(1)}, bf16[128,256]{0,1:T(8,128)(2,1)S(1)}, u32[]{:S(2)}, u32[]{:S(2)}) collective-permute-start(bf16[128,256]{0,1:T(8,128)(2,1)S(1)} %get-tuple-element.32), channel_id=1, source_target_pairs={{0,192},{4,196},{8,200},{12,204},{16,208},{20,212},{24,216},{28,22... | collective-permute-start | bytes 196616 | tf_op jit(solution)/shard_map/ppermute | solution.py:29
  14.5 2.4 %collective-permute-done = bf16[128,256]{0,1:T(8,128)(2,1)S(1)} collective-permute-done((bf16[128,256]{0,1:T(8,128)(2,1)S(1)}, bf16[128,256]{0,1:T(8,128)(2,1)S(1)}, u32[]{:S(2)}, u32[]{:S(2)}) %collective-permute-start) | collective-permute-done | bytes 65568 | tf_op jit(solution)/shard_map/ppermute | solution.py:29
  19.5 8.4 %hidden_sums.1 = (bf16[32,256,128]{2,1,0:T(8,128)(2,1)S(1)}, f32[32,256,128]{2,1,0:T(8,128)S(1)}) custom-call(s32[4]{0:T(128)S(1)} %pad_add_fusion.place, s32[2,84]{1,0:T(2,128)S(1)} %bitcast.23, bf16[256,10752]{1,0:T(8,128)(2,1)} %cot_ref.3, bf16[168,128,128]{2,1,0:T(8,128)(2,1)} %weight_ref.1, bf16[4,128,256]{2,1,0:T(8,128)(2,1)S(1)} %copy-done), custom_call_target="tpu_custom_call" | custom-call | flops 3000000000 | bytes 16777216 | tf_op jit(solution)/shard_map/hidden_sums/pallas_call | solution.py:90
  27.9 1.5 collective-permute-start.3
  29.4 3.8 %collective-permute-done.3 = bf16[32,256,128]{2,1,0:T(8,128)(2,1)S(1)} collective-permute-done((bf16[32,256,128]{2,1,0:T(8,128)(2,1)S(1)}, bf16[32,256,128]{2,1,0:T(8,128)(2,1)S(1)}, u32[]{:S(2)}, u32[]{:S(2)}) %collective-permute-start.3) | collective-permute-done | bytes 2097184 | tf_op jit(solution)/shard_map/ppermute | solution.py:29
  33.2 1.4 core_sums.1
  35.3 3.4 %collective-permute-start.5 = (bf16[8,256,128]{2,1,0:T(8,128)(2,1)S(1)}, bf16[8,256,128]{2,1,0:T(8,128)(2,1)S(1)}, u32[]{:S(2)}, u32[]{:S(2)}) collective-permute-start(bf16[8,256,128]{2,1,0:T(8,128)(2,1)S(1)} %get-tuple-element.20), channel_id=1, source_target_pairs={{0,128},{4,132},{8,136},{12,140},{16,144},{20,148},{24,152},{28,15... | collective-permute-start | bytes 1572872 | tf_op jit(solution)/shard_map/ppermute | solution.py:29
  38.8 10.9 %collective-permute-done.4.a_ref = bf16[8,256,128]{2,1,0:T(8,128)(2,1)S(1)} collective-permute-done((bf16[8,256,128]{2,1,0:T(8,128)(2,1)S(1)}, bf16[8,256,128]{2,1,0:T(8,128)(2,1)S(1)}, u32[]{:S(2)}, u32[]{:S(2)}) %collective-permute-start.4) | collective-permute-done | bytes 524320 | tf_op jit(solution)/shard_map/ppermute | solution.py:29
  49.7 12.0 %collective-permute-done.5.b_ref = bf16[8,256,128]{2,1,0:T(8,128)(2,1)S(1)} collective-permute-done((bf16[8,256,128]{2,1,0:T(8,128)(2,1)S(1)}, bf16[8,256,128]{2,1,0:T(8,128)(2,1)S(1)}, u32[]{:S(2)}, u32[]{:S(2)}) %collective-permute-start.5) | collective-permute-done | bytes 524320 | tf_op jit(solution)/shard_map/ppermute | solution.py:29
  61.7 1.6 line_sums.1
  63.9 1.2 collective-permute-start.7
  65.1 8.2 %all-to-all-start = ((bf16[8,256,128]{2,1,0:T(8,128)(2,1)}), bf16[8,256,128]{2,1,0:T(8,128)(2,1)S(1)}, u32[]{:S(2)}, u32[]{:S(2)}) async-start(bf16[8,256,128]{2,1,0:T(8,128)(2,1)} %get-tuple-element.25), calls=%async_computation | async-start | bytes 1048576 | tf_op jit(solution)/shard_map/all_to_all | solution.py:305
  73.4 1.6 copy-done.1
  75.0 8.2 %out_terms.1 = (bf16[168,128,128]{2,1,0:T(8,128)(2,1)}, f32[8,128]{1,0:T(8,128)S(1)}) custom-call(s32[4]{0:T(128)S(1)} %pad_add_fusion.place, s32[2,84]{1,0:T(2,128)S(1)} %bitcast.24, bf16[256,10752]{1,0:T(8,128)(2,1)} %cot_ref.3, bf16[32,128,256]{2,1,0:T(8,128)(2,1)S(1)} %copy-done.1, bf16[32,128,256]{2,1,0:T(8,128)(2,1)S(1)} %collective-permute-done.7.other_ref), custom_call_target="tpu_custom_call" | custom-call | flops 3000000000 | bytes 16777216 | tf_op jit(solution)/shard_map/out_terms/pallas_call | solution.py:199
  83.8 7.5 %all-to-all-done = bf16[8,256,128]{2,1,0:T(8,128)(2,1)S(1)} async-done(((bf16[8,256,128]{2,1,0:T(8,128)(2,1)}), bf16[8,256,128]{2,1,0:T(8,128)(2,1)S(1)}, u32[]{:S(2)}, u32[]{:S(2)}) %all-to-all-start) | async-done | bytes 524320 | tf_op jit(solution)/shard_map/all_to_all | solution.py:305
  91.3 1.1 select_reduce_fusion
  94.7 3.5 %all-to-all-start.1 = ((bf16[8,208,128]{2,1,0:T(8,128)(2,1)}), bf16[8,208,128]{2,1,0:T(8,128)(2,1)S(1)}, u32[]{:S(2)}, u32[]{:S(2)}) async-start(bf16[8,208,128]{2,1,0:T(8,128)(2,1)} %broadcast_in_dim.16), calls=%async_computation.2 | async-start | bytes 851968 | tf_op jit(solution)/shard_map/all_to_all | solution.py:317
  98.2 2.0 %collective-permute-start.17 = (bf16[48,128]{1,0:T(8,128)(2,1)S(1)}, bf16[48,128]{1,0:T(8,128)(2,1)S(1)}, u32[]{:S(2)}, u32[]{:S(2)}) collective-permute-start(bf16[48,128]{1,0:T(8,128)(2,1)S(1)} %fusion.7), channel_id=1, source_target_pairs={{0,192},{4,196},{8,200},{12,204},{16,208},{20,212},{24,216},{28,22... | collective-permute-start | bytes 36872 | tf_op jit(solution)/shard_map/ppermute | solution.py:29
  101.0 3.2 %collective-permute-done.16 = bf16[48,128]{1,0:T(8,128)(2,1)S(1)} collective-permute-done((bf16[48,128]{1,0:T(8,128)(2,1)S(1)}, bf16[48,128]{1,0:T(8,128)(2,1)S(1)}, u32[]{:S(2)}, u32[]{:S(2)}) %collective-permute-start.16) | collective-permute-done | bytes 12320 | tf_op jit(solution)/shard_map/ppermute | solution.py:29
  104.3 9.6 %all-to-all-done.1.refs_0_ = bf16[8,208,128]{2,1,0:T(8,128)(2,1)S(1)} async-done(((bf16[8,208,128]{2,1,0:T(8,128)(2,1)}), bf16[8,208,128]{2,1,0:T(8,128)(2,1)S(1)}, u32[]{:S(2)}, u32[]{:S(2)}) %all-to-all-start.1) | async-done | bytes 426016 | tf_op jit(solution)/shard_map/all_to_all | solution.py:317
  114.7 3.5 %all-to-all-start.2 = ((bf16[8,4,48,128]{3,2,1,0:T(8,128)(2,1)}), bf16[8,4,48,128]{3,2,1,0:T(8,128)(2,1)S(1)}, u32[]{:S(2)}, u32[]{:S(2)}) async-start(bf16[8,4,48,128]{3,2,1,0:T(8,128)(2,1)} %broadcast_in_dim.17), calls=%async_computation.3 | async-start | bytes 786432 | tf_op jit(solution)/shard_map/all_to_all | solution.py:320
  118.2 2.0 %collective-permute-start.10 = (bf16[8,208,128]{2,1,0:T(8,128)(2,1)S(1)}, bf16[8,208,128]{2,1,0:T(8,128)(2,1)S(1)}, u32[]{:S(2)}, u32[]{:S(2)}) collective-permute-start(bf16[8,208,128]{2,1,0:T(8,128)(2,1)S(1)} %all-to-all-done.1.refs_0_), channel_id=1, source_target_pairs={{0,192},{4,196},{8,200},{12,204},{16,208},{20,212},{24,216},{28,22... | collective-permute-start | bytes 1277960 | tf_op jit(solution)/shard_map/ppermute | solution.py:29
  121.9 7.4 %collective-permute-done.10.refs_3_ = bf16[8,208,128]{2,1,0:T(8,128)(2,1)S(1)} collective-permute-done((bf16[8,208,128]{2,1,0:T(8,128)(2,1)S(1)}, bf16[8,208,128]{2,1,0:T(8,128)(2,1)S(1)}, u32[]{:S(2)}, u32[]{:S(2)}) %collective-permute-start.10) | collective-permute-done | bytes 426016 | tf_op jit(solution)/shard_map/ppermute | solution.py:29
  129.3 10.1 %collective-permute-start.14 = (bf16[8,208,128]{2,1,0:T(8,128)(2,1)S(1)}, bf16[8,208,128]{2,1,0:T(8,128)(2,1)S(1)}, u32[]{:S(2)}, u32[]{:S(2)}) collective-permute-start(bf16[8,208,128]{2,1,0:T(8,128)(2,1)S(1)} %collective-permute-done.10.refs_3_), channel_id=1, source_target_pairs={{0,4},{4,0},{8,12},{12,8},{16,20},{20,16},{24,28},{28,24},{32,36},... | collective-permute-start | bytes 1277960 | tf_op jit(solution)/shard_map/ppermute | solution.py:29
  139.4 2.7 %collective-permute-done.8.refs_1_ = bf16[8,208,128]{2,1,0:T(8,128)(2,1)S(1)} collective-permute-done((bf16[8,208,128]{2,1,0:T(8,128)(2,1)S(1)}, bf16[8,208,128]{2,1,0:T(8,128)(2,1)S(1)}, u32[]{:S(2)}, u32[]{:S(2)}) %collective-permute-start.8) | collective-permute-done | bytes 426016 | tf_op jit(solution)/shard_map/ppermute | solution.py:29
  142.7 2.0 %collective-permute-done.18.refs_9_ = bf16[8,4,48,128]{3,2,1,0:T(8,128)(2,1)S(1)} collective-permute-done((bf16[8,4,48,128]{3,2,1,0:T(8,128)(2,1)S(1)}, bf16[8,4,48,128]{3,2,1,0:T(8,128)(2,1)S(1)}, u32[]{:S(2)}, u32[]{:S(2)}) %collective-permute-start.18) | collective-permute-done | bytes 393248 | tf_op jit(solution)/shard_map/ppermute | solution.py:29
  144.8 3.0 %in_terms.1 = (f32[7,128,128]{2,1,0:T(8,128)S(1)}, bf16[7,128,128]{2,1,0:T(8,128)(2,1)S(1)}, bf16[7,128,128]{2,1,0:T(8,128)(2,1)S(1)}, bf16[7,128,128]{2,1,0:T(8,128)(2,1)S(1)}) custom-call(s32[4]{0:T(128)S(1)} %pad_add_fusion.place, s32[4,7]{1,0:T(4,128)S(1)} %bitcast.22, bf16[256,896]{1,0:T(8,128)(2,1)S(1)} %copy-done.3, ...), custom_call_target="tpu_custom_call" | custom-call | flops 500000000 | bytes 8388608 | tf_op jit(solution)/shard_map/in_terms/pallas_call | solution.py:263
  147.8 1.4 collective-permute-start.19
  149.2 2.7 %collective-permute-start.20 = (bf16[7,128,128]{2,1,0:T(8,128)(2,1)S(1)}, bf16[7,128,128]{2,1,0:T(8,128)(2,1)S(1)}, u32[]{:S(2)}, u32[]{:S(2)}) collective-permute-start(bf16[7,128,128]{2,1,0:T(8,128)(2,1)S(1)} %get-tuple-element.28), channel_id=1, source_target_pairs={{0,2},{1,3},{2,0},{3,1},{4,6},{5,7},{6,4},{7,5},{8,10},{9,11},{10,... | collective-permute-start | bytes 688136 | tf_op jit(solution)/shard_map/ppermute | solution.py:33
  152.9 3.3 %collective-permute-done.19 = bf16[7,128,128]{2,1,0:T(8,128)(2,1)S(1)} collective-permute-done((bf16[7,128,128]{2,1,0:T(8,128)(2,1)S(1)}, bf16[7,128,128]{2,1,0:T(8,128)(2,1)S(1)}, u32[]{:S(2)}, u32[]{:S(2)}) %collective-permute-start.19) | collective-permute-done | bytes 229408 | tf_op jit(solution)/shard_map/ppermute | solution.py:33
  156.1 6.0 %collective-permute-done.20 = bf16[7,128,128]{2,1,0:T(8,128)(2,1)S(1)} collective-permute-done((bf16[7,128,128]{2,1,0:T(8,128)(2,1)S(1)}, bf16[7,128,128]{2,1,0:T(8,128)(2,1)S(1)}, u32[]{:S(2)}, u32[]{:S(2)}) %collective-permute-start.20) | collective-permute-done | bytes 229408 | tf_op jit(solution)/shard_map/ppermute | solution.py:33
  (62 shorter events, 14.4 us)
Async XLA Ops:
  7.2 56.7 %all-gather.3.cloned.1.call-start = ((), (), s32[]{:S(2)}) async-start(), calls=%async_computation.5 | async-start | bytes 2359296 | tf_op jit(solution)/shard_map/all_gather | solution.py:299
  8.1 6.3 %collective-permute-start.1 = (bf16[128,256]{0,1:T(8,128)(2,1)S(1)}, bf16[128,256]{0,1:T(8,128)(2,1)S(1)}, u32[]{:S(2)}, u32[]{:S(2)}) collective-permute-start(bf16[128,256]{0,1:T(8,128)(2,1)S(1)} %get-tuple-element.32), channel_id=1, source_target_pairs={{0,128},{4,132},{8,136},{12,140},{16,144},{20,148},{24,152},{28,15... | collective-permute-start | bytes 196616 | tf_op jit(solution)/shard_map/ppermute | solution.py:29
  11.8 5.0 %collective-permute-start = (bf16[128,256]{0,1:T(8,128)(2,1)S(1)}, bf16[128,256]{0,1:T(8,128)(2,1)S(1)}, u32[]{:S(2)}, u32[]{:S(2)}) collective-permute-start(bf16[128,256]{0,1:T(8,128)(2,1)S(1)} %get-tuple-element.32), channel_id=1, source_target_pairs={{0,64},{4,68},{8,72},{12,76},{16,80},{20,84},{24,88},{28,92},{32,9... | collective-permute-start | bytes 196616 | tf_op jit(solution)/shard_map/ppermute | solution.py:29
  12.1 4.7 %collective-permute-start.2 = (bf16[128,256]{0,1:T(8,128)(2,1)S(1)}, bf16[128,256]{0,1:T(8,128)(2,1)S(1)}, u32[]{:S(2)}, u32[]{:S(2)}) collective-permute-start(bf16[128,256]{0,1:T(8,128)(2,1)S(1)} %get-tuple-element.32), channel_id=1, source_target_pairs={{0,192},{4,196},{8,200},{12,204},{16,208},{20,212},{24,216},{28,22... | collective-permute-start | bytes 196616 | tf_op jit(solution)/shard_map/ppermute | solution.py:29
  17.9 1.0 copy-start
  27.9 5.3 %collective-permute-start.3 = (bf16[32,256,128]{2,1,0:T(8,128)(2,1)S(1)}, bf16[32,256,128]{2,1,0:T(8,128)(2,1)S(1)}, u32[]{:S(2)}, u32[]{:S(2)}) collective-permute-start(bf16[32,256,128]{2,1,0:T(8,128)(2,1)S(1)} %get-tuple-element.17), channel_id=1, source_target_pairs={{0,4},{4,0},{8,12},{12,8},{16,20},{20,16},{24,28},{28,24},{32,36},... | collective-permute-start | bytes 6291464 | tf_op jit(solution)/shard_map/ppermute | solution.py:29
  34.6 15.1 %collective-permute-start.4 = (bf16[8,256,128]{2,1,0:T(8,128)(2,1)S(1)}, bf16[8,256,128]{2,1,0:T(8,128)(2,1)S(1)}, u32[]{:S(2)}, u32[]{:S(2)}) collective-permute-start(bf16[8,256,128]{2,1,0:T(8,128)(2,1)S(1)} %get-tuple-element.19), channel_id=1, source_target_pairs={{0,64},{4,68},{8,72},{12,76},{16,80},{20,84},{24,88},{28,92},{32,9... | collective-permute-start | bytes 1572872 | tf_op jit(solution)/shard_map/ppermute | solution.py:29
  35.3 26.3 %collective-permute-start.5 = (bf16[8,256,128]{2,1,0:T(8,128)(2,1)S(1)}, bf16[8,256,128]{2,1,0:T(8,128)(2,1)S(1)}, u32[]{:S(2)}, u32[]{:S(2)}) collective-permute-start(bf16[8,256,128]{2,1,0:T(8,128)(2,1)S(1)} %get-tuple-element.20), channel_id=1, source_target_pairs={{0,128},{4,132},{8,136},{12,140},{16,144},{20,148},{24,152},{28,15... | collective-permute-start | bytes 1572872 | tf_op jit(solution)/shard_map/ppermute | solution.py:29
  38.8 22.9 %collective-permute-start.6 = (bf16[8,256,128]{2,1,0:T(8,128)(2,1)S(1)}, bf16[8,256,128]{2,1,0:T(8,128)(2,1)S(1)}, u32[]{:S(2)}, u32[]{:S(2)}) collective-permute-start(bf16[8,256,128]{2,1,0:T(8,128)(2,1)S(1)} %get-tuple-element.21), channel_id=1, source_target_pairs={{0,192},{4,196},{8,200},{12,204},{16,208},{20,212},{24,216},{28,22... | collective-permute-start | bytes 1572872 | tf_op jit(solution)/shard_map/ppermute | solution.py:29
  63.9 9.5 %copy-start.7 = (s32[84,2]{0,1:T(2,128)S(1)}, s32[84,2]{0,1:T(2,128)}, u32[]{:S(2)}) copy-start(s32[84,2]{0,1:T(2,128)} %param.10) | copy-start | bytes 2020
  63.9 9.4 %collective-permute-start.7 = (bf16[32,128,256]{2,1,0:T(8,128)(2,1)}, bf16[32,128,256]{2,1,0:T(8,128)(2,1)S(1)}, u32[]{:S(2)}, u32[]{:S(2)}) collective-permute-start(bf16[32,128,256]{2,1,0:T(8,128)(2,1)} %after.3.own_ref), channel_id=1, source_target_pairs={{0,4},{4,0},{8,12},{12,8},{16,20},{20,16},{24,28},{28,24},{32,36},... | collective-permute-start | bytes 6291464 | tf_op jit(solution)/shard_map/ppermute | solution.py:29
  65.1 26.2 %all-to-all-start = ((bf16[8,256,128]{2,1,0:T(8,128)(2,1)}), bf16[8,256,128]{2,1,0:T(8,128)(2,1)S(1)}, u32[]{:S(2)}, u32[]{:S(2)}) async-start(bf16[8,256,128]{2,1,0:T(8,128)(2,1)} %get-tuple-element.25), calls=%async_computation | async-start | bytes 1048576 | tf_op jit(solution)/shard_map/all_to_all | solution.py:305
  73.3 89.6 %reduce-scatter.2.cloned.1.call-start = ((), (), s32[]{:S(2)}) async-start(), calls=%async_computation.4 | async-start | bytes 6881280 | tf_op jit(solution)/shard_map/reduce_scatter | solution.py:313
  73.4 1.6 copy-start.1
  93.9 51.0 %copy-start.3 = (bf16[256,896]{1,0:T(8,128)(2,1)S(1)}, bf16[256,896]{1,0:T(8,128)(2,1)}, u32[]{:S(2)}) copy-start(bf16[256,896]{1,0:T(8,128)(2,1)} %enc_ref.1) | copy-start | bytes 1376260
  93.9 51.0 %copy-start.5 = (s32[7,4]{0,1:T(4,128)S(1)}, s32[7,4]{0,1:T(4,128)}, u32[]{:S(2)}) copy-start(s32[7,4]{0,1:T(4,128)} %param.11) | copy-start | bytes 340
  94.7 19.2 %all-to-all-start.1 = ((bf16[8,208,128]{2,1,0:T(8,128)(2,1)}), bf16[8,208,128]{2,1,0:T(8,128)(2,1)S(1)}, u32[]{:S(2)}, u32[]{:S(2)}) async-start(bf16[8,208,128]{2,1,0:T(8,128)(2,1)} %broadcast_in_dim.16), calls=%async_computation.2 | async-start | bytes 851968 | tf_op jit(solution)/shard_map/all_to_all | solution.py:317
  98.2 2.8 %collective-permute-start.17 = (bf16[48,128]{1,0:T(8,128)(2,1)S(1)}, bf16[48,128]{1,0:T(8,128)(2,1)S(1)}, u32[]{:S(2)}, u32[]{:S(2)}) collective-permute-start(bf16[48,128]{1,0:T(8,128)(2,1)S(1)} %fusion.7), channel_id=1, source_target_pairs={{0,192},{4,196},{8,200},{12,204},{16,208},{20,212},{24,216},{28,22... | collective-permute-start | bytes 36872 | tf_op jit(solution)/shard_map/ppermute | solution.py:29
  100.2 4.1 %collective-permute-start.16 = (bf16[48,128]{1,0:T(8,128)(2,1)S(1)}, bf16[48,128]{1,0:T(8,128)(2,1)S(1)}, u32[]{:S(2)}, u32[]{:S(2)}) collective-permute-start(bf16[48,128]{1,0:T(8,128)(2,1)S(1)} %fusion.7), channel_id=1, source_target_pairs={{0,128},{4,132},{8,136},{12,140},{16,144},{20,148},{24,152},{28,15... | collective-permute-start | bytes 36872 | tf_op jit(solution)/shard_map/ppermute | solution.py:29
  100.2 4.2 %collective-permute-start.15 = (bf16[48,128]{1,0:T(8,128)(2,1)S(1)}, bf16[48,128]{1,0:T(8,128)(2,1)S(1)}, u32[]{:S(2)}, u32[]{:S(2)}) collective-permute-start(bf16[48,128]{1,0:T(8,128)(2,1)S(1)} %fusion.7), channel_id=1, source_target_pairs={{0,64},{4,68},{8,72},{12,76},{16,80},{20,84},{24,88},{28,92},{32,9... | collective-permute-start | bytes 36872 | tf_op jit(solution)/shard_map/ppermute | solution.py:29
  114.7 28.0 %all-to-all-start.2 = ((bf16[8,4,48,128]{3,2,1,0:T(8,128)(2,1)}), bf16[8,4,48,128]{3,2,1,0:T(8,128)(2,1)S(1)}, u32[]{:S(2)}, u32[]{:S(2)}) async-start(bf16[8,4,48,128]{3,2,1,0:T(8,128)(2,1)} %broadcast_in_dim.17), calls=%async_computation.3 | async-start | bytes 786432 | tf_op jit(solution)/shard_map/all_to_all | solution.py:320
  118.2 11.1 %collective-permute-start.10 = (bf16[8,208,128]{2,1,0:T(8,128)(2,1)S(1)}, bf16[8,208,128]{2,1,0:T(8,128)(2,1)S(1)}, u32[]{:S(2)}, u32[]{:S(2)}) collective-permute-start(bf16[8,208,128]{2,1,0:T(8,128)(2,1)S(1)} %all-to-all-done.1.refs_0_), channel_id=1, source_target_pairs={{0,192},{4,196},{8,200},{12,204},{16,208},{20,212},{24,216},{28,22... | collective-permute-start | bytes 1277960 | tf_op jit(solution)/shard_map/ppermute | solution.py:29
  120.2 19.2 %collective-permute-start.9 = (bf16[8,208,128]{2,1,0:T(8,128)(2,1)S(1)}, bf16[8,208,128]{2,1,0:T(8,128)(2,1)S(1)}, u32[]{:S(2)}, u32[]{:S(2)}) collective-permute-start(bf16[8,208,128]{2,1,0:T(8,128)(2,1)S(1)} %all-to-all-done.1.refs_0_), channel_id=1, source_target_pairs={{0,128},{4,132},{8,136},{12,140},{16,144},{20,148},{24,152},{28,15... | collective-permute-start | bytes 1277960 | tf_op jit(solution)/shard_map/ppermute | solution.py:29
  120.2 21.9 %collective-permute-start.8 = (bf16[8,208,128]{2,1,0:T(8,128)(2,1)S(1)}, bf16[8,208,128]{2,1,0:T(8,128)(2,1)S(1)}, u32[]{:S(2)}, u32[]{:S(2)}) collective-permute-start(bf16[8,208,128]{2,1,0:T(8,128)(2,1)S(1)} %all-to-all-done.1.refs_0_), channel_id=1, source_target_pairs={{0,64},{4,68},{8,72},{12,76},{16,80},{20,84},{24,88},{28,92},{32,9... | collective-permute-start | bytes 1277960 | tf_op jit(solution)/shard_map/ppermute | solution.py:29
  120.8 23.9 %collective-permute-start.11 = (bf16[8,208,128]{2,1,0:T(8,128)(2,1)S(1)}, bf16[8,208,128]{2,1,0:T(8,128)(2,1)S(1)}, u32[]{:S(2)}, u32[]{:S(2)}) collective-permute-start(bf16[8,208,128]{2,1,0:T(8,128)(2,1)S(1)} %all-to-all-done.1.refs_0_), channel_id=1, source_target_pairs={{0,4},{4,0},{8,12},{12,8},{16,20},{20,16},{24,28},{28,24},{32,36},... | collective-permute-start | bytes 1277960 | tf_op jit(solution)/shard_map/ppermute | solution.py:29
  129.3 15.4 %collective-permute-start.14 = (bf16[8,208,128]{2,1,0:T(8,128)(2,1)S(1)}, bf16[8,208,128]{2,1,0:T(8,128)(2,1)S(1)}, u32[]{:S(2)}, u32[]{:S(2)}) collective-permute-start(bf16[8,208,128]{2,1,0:T(8,128)(2,1)S(1)} %collective-permute-done.10.refs_3_), channel_id=1, source_target_pairs={{0,4},{4,0},{8,12},{12,8},{16,20},{20,16},{24,28},{28,24},{32,36},... | collective-permute-start | bytes 1277960 | tf_op jit(solution)/shard_map/ppermute | solution.py:29
  139.4 5.3 %collective-permute-start.13 = (bf16[8,208,128]{2,1,0:T(8,128)(2,1)S(1)}, bf16[8,208,128]{2,1,0:T(8,128)(2,1)}, u32[]{:S(2)}, u32[]{:S(2)}) collective-permute-start(bf16[8,208,128]{2,1,0:T(8,128)(2,1)S(1)} %collective-permute-done.9.refs_2_), channel_id=1, source_target_pairs={{0,4},{4,0},{8,12},{12,8},{16,20},{20,16},{24,28},{28,24},{32,36},... | collective-permute-start | bytes 1277960 | tf_op jit(solution)/shard_map/ppermute | solution.py:29
  142.0 2.8 %collective-permute-start.12 = (bf16[8,208,128]{2,1,0:T(8,128)(2,1)S(1)}, bf16[8,208,128]{2,1,0:T(8,128)(2,1)}, u32[]{:S(2)}, u32[]{:S(2)}) collective-permute-start(bf16[8,208,128]{2,1,0:T(8,128)(2,1)S(1)} %collective-permute-done.8.refs_1_), channel_id=1, source_target_pairs={{0,4},{4,0},{8,12},{12,8},{16,20},{20,16},{24,28},{28,24},{32,36},... | collective-permute-start | bytes 1277960 | tf_op jit(solution)/shard_map/ppermute | solution.py:29
  142.7 2.0 %collective-permute-start.18 = (bf16[8,4,48,128]{3,2,1,0:T(8,128)(2,1)S(1)}, bf16[8,4,48,128]{3,2,1,0:T(8,128)(2,1)S(1)}, u32[]{:S(2)}, u32[]{:S(2)}) collective-permute-start(bf16[8,4,48,128]{3,2,1,0:T(8,128)(2,1)S(1)} %all-to-all-done.2.refs_8_), channel_id=1, source_target_pairs={{0,4},{4,0},{8,12},{12,8},{16,20},{20,16},{24,28},{28,24},{32,36},... | collective-permute-start | bytes 1179656 | tf_op jit(solution)/shard_map/ppermute | solution.py:29
  147.8 8.3 %collective-permute-start.19 = (bf16[7,128,128]{2,1,0:T(8,128)(2,1)S(1)}, bf16[7,128,128]{2,1,0:T(8,128)(2,1)S(1)}, u32[]{:S(2)}, u32[]{:S(2)}) collective-permute-start(bf16[7,128,128]{2,1,0:T(8,128)(2,1)S(1)} %get-tuple-element.27), channel_id=1, source_target_pairs={{0,1},{1,2},{2,3},{3,0},{4,5},{5,6},{6,7},{7,4},{8,9},{9,10},{10,1... | collective-permute-start | bytes 688136 | tf_op jit(solution)/shard_map/ppermute | solution.py:33
  149.2 12.9 %collective-permute-start.20 = (bf16[7,128,128]{2,1,0:T(8,128)(2,1)S(1)}, bf16[7,128,128]{2,1,0:T(8,128)(2,1)S(1)}, u32[]{:S(2)}, u32[]{:S(2)}) collective-permute-start(bf16[7,128,128]{2,1,0:T(8,128)(2,1)S(1)} %get-tuple-element.28), channel_id=1, source_target_pairs={{0,2},{1,3},{2,0},{3,1},{4,6},{5,7},{6,4},{7,5},{8,10},{9,11},{10,... | collective-permute-start | bytes 688136 | tf_op jit(solution)/shard_map/ppermute | solution.py:33
  151.8 10.3 %collective-permute-start.21 = (bf16[7,128,128]{2,1,0:T(8,128)(2,1)S(1)}, bf16[7,128,128]{2,1,0:T(8,128)(2,1)S(1)}, u32[]{:S(2)}, u32[]{:S(2)}) collective-permute-start(bf16[7,128,128]{2,1,0:T(8,128)(2,1)S(1)} %get-tuple-element.29), channel_id=1, source_target_pairs={{0,3},{1,0},{2,1},{3,2},{4,7},{5,4},{6,5},{7,6},{8,11},{9,8},{10,9... | collective-permute-start | bytes 688136 | tf_op jit(solution)/shard_map/ppermute | solution.py:33
  (4 other events, 2.7 us)
Sparse Core Ops, SparseCore 0:
  17.9 41.2 all-gather.2
  93.2 55.4 reduce-scatter.1

commit v7 on v6

--- a/solution.py
+++ b/solution.py
@@ -11,7 +11,7 @@
 BS = 128
 STEP_BLOCKS = 28
 OUT_STEP = 28
-FIRST, LAST = 208, 48
+FIRST, LAST = 176, 80
 CORE_STEP = 2
 
 
@@ -295,10 +295,11 @@
     pre = hidden_pre.astype(F32)
 
     activation = jax.nn.silu(pre).astype(BF16).T
-    along_x = jnp.stack([activation] + [moved(activation, dx=d) for d in range(1, NX)])
+    arrived = [moved(activation, dx=d) for d in range(1, NX)]
+    along_x = jnp.stack([activation] + arrived)
     act_own = lax.all_gather(along_x, "blk", axis_index_groups=LINES)
     act_own = act_own.reshape(NZ * NX, BS, -1)
-    send, keep = hidden_sums(place, out_index, cotangent, out_weights, along_x)
+    send, keep = hidden_sums(place, out_index, cotangent, out_weights, arrived[0])
 
     by_x = core_sums(place, keep, moved(send, dc=1))
     by_z, own_z = line_sums(place, by_x[0], *[moved(by_x[d], dx=d) for d in range(1, NX)])
@@ -310,7 +311,7 @@
     slope = silu_slope(pre)
     first = (grad_act[:FIRST] * slope[:FIRST]).astype(BF16)
     last = (grad_act[FIRST:] * slope[FIRST:]).astype(BF16)
-    out_grad = lax.psum_scatter(after(terms, first), "smp", scatter_dimension=0, tiled=True)
+    out_grad = lax.psum_scatter(after(terms, last), "smp", scatter_dimension=0, tiled=True)
 
     last_x = jnp.stack([last] + [moved(last, dx=d) for d in range(1, NX)])
     copies = jnp.broadcast_to(first, (NZ, *first.shape))

time: 170 us -> 165 us (0.971)
  starting transfers between devices: 50.6 us -> 40.3 us
  waiting for transfers between devices: 71.1 us -> 78.3 us
    all_to_all x1, waiting for transfers between devices: 0.01 us -> 18 us  [per_device(): last_own = lax.all_to_all(copies, 'blk', 0, 0, axis_index_groups=LINES)]
    ppermute x19, starting transfers between devices: 30.3 us -> 20 us  [moved(): return lax.ppermute(value, 'blk', pairs)]
    ppermute x19, waiting for transfers between devices: 44.7 us -> 35.3 us  [moved(): return lax.ppermute(value, 'blk', pairs)]
    unnamed x18 -> x16, local copies, waits for them, and re-layouts: 5.25 us -> 3.51 us
  transfers between devices with their start and end apart: 27 -> 27, of which waited for: 15 -> 15; matrix products, arithmetic and copies ran while one was open for 1% -> 2% of each run, Pallas kernels for 13% -> 13%
where the time goes in v7:
time: 165 us; the launch traced here: 164 us
  waiting for transfers between devices  78.3 us (47%)
  starting transfers between devices  40.3 us (24%)
  Pallas kernels  21.6 us (13%)
  between operations  14.3 us (9%)
  local copies, waits for them, and re-layouts  6.18 us (4%)
  other arithmetic  3.55 us (2%)
    ppermute x19, waiting for transfers between devices, moved(): return lax.ppermute(value, 'blk', pairs)  35.3 us
    ppermute x19, starting transfers between devices, moved(): return lax.ppermute(value, 'blk', pairs)  20 us
    all_to_all x1, waiting for transfers between devices, per_device(): last_own = lax.all_to_all(copies, 'blk', 0, 0, axis_index_groups=LINES)  18 us
    ppermute x3, waiting for transfers between devices, moved_smp(): return lax.ppermute(value, 'smp', [(i, (i + dy) % NY) for i in range(NY)])  9.2 us
    pallas_call x1, Pallas kernels, hidden_sums(): pl.pallas_call(hidden_kernel, grid_spec=pltpu.PrefetchScalarGridSpec(num_...  8.39 us
    all_to_all x1, waiting for transfers between devices, per_device(): along_z = lax.all_to_all(copies, 'blk', 0, 0, axis_index_groups=LINES)  8.23 us
    pallas_call x1, Pallas kernels, out_terms(): pl.pallas_call(out_kernel, grid_spec=pltpu.PrefetchScalarGridSpec(num_sca...  8.22 us
    all_to_all x1, starting transfers between devices, per_device(): got = lax.all_to_all(by_z, 'blk', 0, 0, axis_index_groups=LINES)  8.19 us
  transfers between devices with their start and end apart: 27, of which 15 were waited for; matrix products, arithmetic and copies ran while one was open for 2% of the time, Pallas kernels for 13%

profile of v7, /device:TPU:1, one launch (start us, length us, event | category | flops | bytes accessed | tf_op | source)
XLA Modules:
  0.0 164.3 jit_solution(15210431292753765352)
XLA Ops:
  8.1 3.7 %collective-permute-start.1 = (bf16[128,256]{0,1:T(8,128)(2,1)S(1)}, bf16[128,256]{0,1:T(8,128)(2,1)S(1)}, u32[]{:S(2)}, u32[]{:S(2)}) collective-permute-start(bf16[128,256]{0,1:T(8,128)(2,1)S(1)} %get-tuple-element.32), channel_id=1, source_target_pairs={{0,128},{4,132},{8,136},{12,140},{16,144},{20,148},{24,152},{28,15... | collective-permute-start | bytes 196616 | tf_op jit(solution)/shard_map/ppermute | solution.py:29
  12.1 2.4 %collective-permute-start.2 = (bf16[128,256]{0,1:T(8,128)(2,1)S(1)}, bf16[128,256]{0,1:T(8,128)(2,1)S(1)}, u32[]{:S(2)}, u32[]{:S(2)}) collective-permute-start(bf16[128,256]{0,1:T(8,128)(2,1)S(1)} %get-tuple-element.32), channel_id=1, source_target_pairs={{0,192},{4,196},{8,200},{12,204},{16,208},{20,212},{24,216},{28,22... | collective-permute-start | bytes 196616 | tf_op jit(solution)/shard_map/ppermute | solution.py:29
  14.5 2.4 %collective-permute-done = bf16[128,256]{0,1:T(8,128)(2,1)S(1)} collective-permute-done((bf16[128,256]{0,1:T(8,128)(2,1)S(1)}, bf16[128,256]{0,1:T(8,128)(2,1)S(1)}, u32[]{:S(2)}, u32[]{:S(2)}) %collective-permute-start) | collective-permute-done | bytes 65568 | tf_op jit(solution)/shard_map/ppermute | solution.py:29
  18.7 8.4 %hidden_sums.1 = (bf16[32,256,128]{2,1,0:T(8,128)(2,1)S(1)}, f32[32,256,128]{2,1,0:T(8,128)S(1)}) custom-call(s32[4]{0:T(128)S(1)} %pad_add_fusion.place, s32[2,84]{1,0:T(2,128)S(1)} %bitcast.23, bf16[256,10752]{1,0:T(8,128)(2,1)} %cot_ref.3, bf16[168,128,128]{2,1,0:T(8,128)(2,1)} %weight_ref.1, bf16[128,256]{1,0:T(8,128)(2,1)S(1)} %copy.14.before_ref), custom_call_target="tpu_custom_call" | custom-call | flops 3000000000 | bytes 16777216 | tf_op jit(solution)/shard_map/hidden_sums/pallas_call | solution.py:90
  27.0 1.5 collective-permute-start.3
  28.5 3.8 %collective-permute-done.3 = bf16[32,256,128]{2,1,0:T(8,128)(2,1)S(1)} collective-permute-done((bf16[32,256,128]{2,1,0:T(8,128)(2,1)S(1)}, bf16[32,256,128]{2,1,0:T(8,128)(2,1)S(1)}, u32[]{:S(2)}, u32[]{:S(2)}) %collective-permute-start.3) | collective-permute-done | bytes 2097184 | tf_op jit(solution)/shard_map/ppermute | solution.py:29
  32.3 1.4 core_sums.1
  34.5 3.4 %collective-permute-start.5 = (bf16[8,256,128]{2,1,0:T(8,128)(2,1)S(1)}, bf16[8,256,128]{2,1,0:T(8,128)(2,1)S(1)}, u32[]{:S(2)}, u32[]{:S(2)}) collective-permute-start(bf16[8,256,128]{2,1,0:T(8,128)(2,1)S(1)} %get-tuple-element.20), channel_id=1, source_target_pairs={{0,128},{4,132},{8,136},{12,140},{16,144},{20,148},{24,152},{28,15... | collective-permute-start | bytes 1572872 | tf_op jit(solution)/shard_map/ppermute | solution.py:29
  37.9 10.8 %collective-permute-done.4.a_ref = bf16[8,256,128]{2,1,0:T(8,128)(2,1)S(1)} collective-permute-done((bf16[8,256,128]{2,1,0:T(8,128)(2,1)S(1)}, bf16[8,256,128]{2,1,0:T(8,128)(2,1)S(1)}, u32[]{:S(2)}, u32[]{:S(2)}) %collective-permute-start.4) | collective-permute-done | bytes 524320 | tf_op jit(solution)/shard_map/ppermute | solution.py:29
  48.7 12.1 %collective-permute-done.5.b_ref = bf16[8,256,128]{2,1,0:T(8,128)(2,1)S(1)} collective-permute-done((bf16[8,256,128]{2,1,0:T(8,128)(2,1)S(1)}, bf16[8,256,128]{2,1,0:T(8,128)(2,1)S(1)}, u32[]{:S(2)}, u32[]{:S(2)}) %collective-permute-start.5) | collective-permute-done | bytes 524320 | tf_op jit(solution)/shard_map/ppermute | solution.py:29
  60.8 1.6 line_sums.1
  63.1 1.2 collective-permute-start.7
  64.3 8.2 %all-to-all-start = ((bf16[8,256,128]{2,1,0:T(8,128)(2,1)}), bf16[8,256,128]{2,1,0:T(8,128)(2,1)S(1)}, u32[]{:S(2)}, u32[]{:S(2)}) async-start(bf16[8,256,128]{2,1,0:T(8,128)(2,1)} %get-tuple-element.25), calls=%async_computation | async-start | bytes 1048576 | tf_op jit(solution)/shard_map/all_to_all | solution.py:306
  72.5 1.6 copy-done
  74.1 8.2 %out_terms.1 = (bf16[168,128,128]{2,1,0:T(8,128)(2,1)}, f32[8,128]{1,0:T(8,128)S(1)}) custom-call(s32[4]{0:T(128)S(1)} %pad_add_fusion.place, s32[2,84]{1,0:T(2,128)S(1)} %bitcast.24, bf16[256,10752]{1,0:T(8,128)(2,1)} %cot_ref.3, bf16[32,128,256]{2,1,0:T(8,128)(2,1)S(1)} %copy-done, bf16[32,128,256]{2,1,0:T(8,128)(2,1)S(1)} %collective-permute-done.7.other_ref), custom_call_target="tpu_custom_call" | custom-call | flops 3000000000 | bytes 16777216 | tf_op jit(solution)/shard_map/out_terms/pallas_call | solution.py:199
  82.9 7.5 %all-to-all-done = bf16[8,256,128]{2,1,0:T(8,128)(2,1)S(1)} async-done(((bf16[8,256,128]{2,1,0:T(8,128)(2,1)}), bf16[8,256,128]{2,1,0:T(8,128)(2,1)S(1)}, u32[]{:S(2)}, u32[]{:S(2)}) %all-to-all-start) | async-done | bytes 524320 | tf_op jit(solution)/shard_map/all_to_all | solution.py:306
  90.5 1.1 select_reduce_fusion
  93.1 3.4 %all-to-all-start.1 = ((bf16[8,176,128]{2,1,0:T(8,128)(2,1)}), bf16[8,176,128]{2,1,0:T(8,128)(2,1)S(1)}, u32[]{:S(2)}, u32[]{:S(2)}) async-start(bf16[8,176,128]{2,1,0:T(8,128)(2,1)} %broadcast_in_dim.16), calls=%async_computation.2 | async-start | bytes 720896 | tf_op jit(solution)/shard_map/all_to_all | solution.py:318
  96.5 2.0 %collective-permute-start.17 = (bf16[80,128]{1,0:T(8,128)(2,1)S(1)}, bf16[80,128]{1,0:T(8,128)(2,1)S(1)}, u32[]{:S(2)}, u32[]{:S(2)}) collective-permute-start(bf16[80,128]{1,0:T(8,128)(2,1)S(1)} %copy-done.7), channel_id=1, source_target_pairs={{0,192},{4,196},{8,200},{12,204},{16,208},{20,212},{24,216},{28,22... | collective-permute-start | bytes 61448 | tf_op jit(solution)/shard_map/ppermute | solution.py:29
  99.4 3.2 %collective-permute-done.16 = bf16[80,128]{1,0:T(8,128)(2,1)S(1)} collective-permute-done((bf16[80,128]{1,0:T(8,128)(2,1)S(1)}, bf16[80,128]{1,0:T(8,128)(2,1)S(1)}, u32[]{:S(2)}, u32[]{:S(2)}) %collective-permute-start.16) | collective-permute-done | bytes 20512 | tf_op jit(solution)/shard_map/ppermute | solution.py:29
  102.6 8.2 %all-to-all-done.1.refs_0_ = bf16[8,176,128]{2,1,0:T(8,128)(2,1)S(1)} async-done(((bf16[8,176,128]{2,1,0:T(8,128)(2,1)}), bf16[8,176,128]{2,1,0:T(8,128)(2,1)S(1)}, u32[]{:S(2)}, u32[]{:S(2)}) %all-to-all-start.1) | async-done | bytes 360480 | tf_op jit(solution)/shard_map/all_to_all | solution.py:318
  110.9 0.9 broadcast_in_dim.17
  111.8 3.5 %all-to-all-start.2 = ((bf16[8,4,80,128]{3,2,1,0:T(8,128)(2,1)}), bf16[8,4,80,128]{3,2,1,0:T(8,128)(2,1)S(1)}, u32[]{:S(2)}, u32[]{:S(2)}) async-start(bf16[8,4,80,128]{3,2,1,0:T(8,128)(2,1)} %broadcast_in_dim.17), calls=%async_computation.3 | async-start | bytes 1310720 | tf_op jit(solution)/shard_map/all_to_all | solution.py:321
  115.3 2.0 %collective-permute-start.10 = (bf16[8,176,128]{2,1,0:T(8,128)(2,1)S(1)}, bf16[8,176,128]{2,1,0:T(8,128)(2,1)S(1)}, u32[]{:S(2)}, u32[]{:S(2)}) collective-permute-start(bf16[8,176,128]{2,1,0:T(8,128)(2,1)S(1)} %all-to-all-done.1.refs_0_), channel_id=1, source_target_pairs={{0,192},{4,196},{8,200},{12,204},{16,208},{20,212},{24,216},{28,22... | collective-permute-start | bytes 1081352 | tf_op jit(solution)/shard_map/ppermute | solution.py:29
  118.0 18.0 %all-to-all-done.2.refs_8_ = bf16[8,4,80,128]{3,2,1,0:T(8,128)(2,1)S(1)} async-done(((bf16[8,4,80,128]{3,2,1,0:T(8,128)(2,1)}), bf16[8,4,80,128]{3,2,1,0:T(8,128)(2,1)S(1)}, u32[]{:S(2)}, u32[]{:S(2)}) %all-to-all-start.2) | async-done | bytes 655392 | tf_op jit(solution)/shard_map/all_to_all | solution.py:321
  137.5 1.2 collective-permute-done.11.refs_4_
  140.3 2.0 %in_terms.1 = (f32[7,128,128]{2,1,0:T(8,128)S(1)}, bf16[7,128,128]{2,1,0:T(8,128)(2,1)S(1)}, bf16[7,128,128]{2,1,0:T(8,128)(2,1)S(1)}, bf16[7,128,128]{2,1,0:T(8,128)(2,1)S(1)}) custom-call(s32[4]{0:T(128)S(1)} %pad_add_fusion.place, s32[4,7]{1,0:T(4,128)S(1)} %bitcast.22, bf16[256,896]{1,0:T(8,128)(2,1)S(1)} %copy-done.2, ...), custom_call_target="tpu_custom_call" | custom-call | flops 500000000 | bytes 8388608 | tf_op jit(solution)/shard_map/in_terms/pallas_call | solution.py:263
  142.4 1.4 collective-permute-start.19
  143.7 2.6 %collective-permute-start.20 = (bf16[7,128,128]{2,1,0:T(8,128)(2,1)S(1)}, bf16[7,128,128]{2,1,0:T(8,128)(2,1)S(1)}, u32[]{:S(2)}, u32[]{:S(2)}) collective-permute-start(bf16[7,128,128]{2,1,0:T(8,128)(2,1)S(1)} %get-tuple-element.28), channel_id=1, source_target_pairs={{0,2},{1,3},{2,0},{3,1},{4,6},{5,7},{6,4},{7,5},{8,10},{9,11},{10,... | collective-permute-start | bytes 688136 | tf_op jit(solution)/shard_map/ppermute | solution.py:33
  146.3 1.1 collective-permute-start.21
  147.4 3.3 %collective-permute-done.19 = bf16[7,128,128]{2,1,0:T(8,128)(2,1)S(1)} collective-permute-done((bf16[7,128,128]{2,1,0:T(8,128)(2,1)S(1)}, bf16[7,128,128]{2,1,0:T(8,128)(2,1)S(1)}, u32[]{:S(2)}, u32[]{:S(2)}) %collective-permute-start.19) | collective-permute-done | bytes 229408 | tf_op jit(solution)/shard_map/ppermute | solution.py:33
  150.7 5.9 %collective-permute-done.20 = bf16[7,128,128]{2,1,0:T(8,128)(2,1)S(1)} collective-permute-done((bf16[7,128,128]{2,1,0:T(8,128)(2,1)S(1)}, bf16[7,128,128]{2,1,0:T(8,128)(2,1)S(1)}, u32[]{:S(2)}, u32[]{:S(2)}) %collective-permute-start.20) | collective-permute-done | bytes 229408 | tf_op jit(solution)/shard_map/ppermute | solution.py:33
  (61 shorter events, 12.0 us)
Async XLA Ops:
  7.2 55.9 %all-gather.3.cloned.1.call-start = ((), (), s32[]{:S(2)}) async-start(), calls=%async_computation.5 | async-start | bytes 2359296 | tf_op jit(solution)/shard_map/all_gather | solution.py:300
  8.1 6.3 %collective-permute-start.1 = (bf16[128,256]{0,1:T(8,128)(2,1)S(1)}, bf16[128,256]{0,1:T(8,128)(2,1)S(1)}, u32[]{:S(2)}, u32[]{:S(2)}) collective-permute-start(bf16[128,256]{0,1:T(8,128)(2,1)S(1)} %get-tuple-element.32), channel_id=1, source_target_pairs={{0,128},{4,132},{8,136},{12,140},{16,144},{20,148},{24,152},{28,15... | collective-permute-start | bytes 196616 | tf_op jit(solution)/shard_map/ppermute | solution.py:29
  11.8 5.0 %collective-permute-start = (bf16[128,256]{0,1:T(8,128)(2,1)S(1)}, bf16[128,256]{0,1:T(8,128)(2,1)S(1)}, u32[]{:S(2)}, u32[]{:S(2)}) collective-permute-start(bf16[128,256]{0,1:T(8,128)(2,1)S(1)} %get-tuple-element.32), channel_id=1, source_target_pairs={{0,64},{4,68},{8,72},{12,76},{16,80},{20,84},{24,88},{28,92},{32,9... | collective-permute-start | bytes 196616 | tf_op jit(solution)/shard_map/ppermute | solution.py:29
  12.1 4.7 %collective-permute-start.2 = (bf16[128,256]{0,1:T(8,128)(2,1)S(1)}, bf16[128,256]{0,1:T(8,128)(2,1)S(1)}, u32[]{:S(2)}, u32[]{:S(2)}) collective-permute-start(bf16[128,256]{0,1:T(8,128)(2,1)S(1)} %get-tuple-element.32), channel_id=1, source_target_pairs={{0,192},{4,196},{8,200},{12,204},{16,208},{20,212},{24,216},{28,22... | collective-permute-start | bytes 196616 | tf_op jit(solution)/shard_map/ppermute | solution.py:29
  27.0 5.3 %collective-permute-start.3 = (bf16[32,256,128]{2,1,0:T(8,128)(2,1)S(1)}, bf16[32,256,128]{2,1,0:T(8,128)(2,1)S(1)}, u32[]{:S(2)}, u32[]{:S(2)}) collective-permute-start(bf16[32,256,128]{2,1,0:T(8,128)(2,1)S(1)} %get-tuple-element.17), channel_id=1, source_target_pairs={{0,4},{4,0},{8,12},{12,8},{16,20},{20,16},{24,28},{28,24},{32,36},... | collective-permute-start | bytes 6291464 | tf_op jit(solution)/shard_map/ppermute | solution.py:29
  33.7 15.0 %collective-permute-start.4 = (bf16[8,256,128]{2,1,0:T(8,128)(2,1)S(1)}, bf16[8,256,128]{2,1,0:T(8,128)(2,1)S(1)}, u32[]{:S(2)}, u32[]{:S(2)}) collective-permute-start(bf16[8,256,128]{2,1,0:T(8,128)(2,1)S(1)} %get-tuple-element.19), channel_id=1, source_target_pairs={{0,64},{4,68},{8,72},{12,76},{16,80},{20,84},{24,88},{28,92},{32,9... | collective-permute-start | bytes 1572872 | tf_op jit(solution)/shard_map/ppermute | solution.py:29
  34.5 26.3 %collective-permute-start.5 = (bf16[8,256,128]{2,1,0:T(8,128)(2,1)S(1)}, bf16[8,256,128]{2,1,0:T(8,128)(2,1)S(1)}, u32[]{:S(2)}, u32[]{:S(2)}) collective-permute-start(bf16[8,256,128]{2,1,0:T(8,128)(2,1)S(1)} %get-tuple-element.20), channel_id=1, source_target_pairs={{0,128},{4,132},{8,136},{12,140},{16,144},{20,148},{24,152},{28,15... | collective-permute-start | bytes 1572872 | tf_op jit(solution)/shard_map/ppermute | solution.py:29
  37.9 22.9 %collective-permute-start.6 = (bf16[8,256,128]{2,1,0:T(8,128)(2,1)S(1)}, bf16[8,256,128]{2,1,0:T(8,128)(2,1)S(1)}, u32[]{:S(2)}, u32[]{:S(2)}) collective-permute-start(bf16[8,256,128]{2,1,0:T(8,128)(2,1)S(1)} %get-tuple-element.21), channel_id=1, source_target_pairs={{0,192},{4,196},{8,200},{12,204},{16,208},{20,212},{24,216},{28,22... | collective-permute-start | bytes 1572872 | tf_op jit(solution)/shard_map/ppermute | solution.py:29
  63.1 9.5 %copy-start.6 = (s32[84,2]{0,1:T(2,128)S(1)}, s32[84,2]{0,1:T(2,128)}, u32[]{:S(2)}) copy-start(s32[84,2]{0,1:T(2,128)} %param.10) | copy-start | bytes 2020
  63.1 9.5 %collective-permute-start.7 = (bf16[32,128,256]{2,1,0:T(8,128)(2,1)}, bf16[32,128,256]{2,1,0:T(8,128)(2,1)S(1)}, u32[]{:S(2)}, u32[]{:S(2)}) collective-permute-start(bf16[32,128,256]{2,1,0:T(8,128)(2,1)} %after.3.own_ref), channel_id=1, source_target_pairs={{0,4},{4,0},{8,12},{12,8},{16,20},{20,16},{24,28},{28,24},{32,36},... | collective-permute-start | bytes 6291464 | tf_op jit(solution)/shard_map/ppermute | solution.py:29
  64.3 26.2 %all-to-all-start = ((bf16[8,256,128]{2,1,0:T(8,128)(2,1)}), bf16[8,256,128]{2,1,0:T(8,128)(2,1)S(1)}, u32[]{:S(2)}, u32[]{:S(2)}) async-start(bf16[8,256,128]{2,1,0:T(8,128)(2,1)} %get-tuple-element.25), calls=%async_computation | async-start | bytes 1048576 | tf_op jit(solution)/shard_map/all_to_all | solution.py:306
  72.5 85.0 %reduce-scatter.2.cloned.1.call-start = ((), (), s32[]{:S(2)}) async-start(), calls=%async_computation.4 | async-start | bytes 6881280 | tf_op jit(solution)/shard_map/reduce_scatter | solution.py:314
  72.5 1.6 copy-start
  92.2 4.3 %copy-start.7 = (bf16[80,128]{1,0:T(8,128)(2,1)S(1)}, bf16[80,128]{1,0:T(8,128)(2,1)}, u32[]{:S(2)}) copy-start(bf16[80,128]{1,0:T(8,128)(2,1)} %fusion.7.refs_1_) | copy-start | bytes 61444
  92.2 48.1 %copy-start.2 = (bf16[256,896]{1,0:T(8,128)(2,1)S(1)}, bf16[256,896]{1,0:T(8,128)(2,1)}, u32[]{:S(2)}) copy-start(bf16[256,896]{1,0:T(8,128)(2,1)} %enc_ref.1) | copy-start | bytes 1376260
  92.2 48.1 %copy-start.4 = (s32[7,4]{0,1:T(4,128)S(1)}, s32[7,4]{0,1:T(4,128)}, u32[]{:S(2)}) copy-start(s32[7,4]{0,1:T(4,128)} %param.11) | copy-start | bytes 340
  93.1 17.8 %all-to-all-start.1 = ((bf16[8,176,128]{2,1,0:T(8,128)(2,1)}), bf16[8,176,128]{2,1,0:T(8,128)(2,1)S(1)}, u32[]{:S(2)}, u32[]{:S(2)}) async-start(bf16[8,176,128]{2,1,0:T(8,128)(2,1)} %broadcast_in_dim.16), calls=%async_computation.2 | async-start | bytes 720896 | tf_op jit(solution)/shard_map/all_to_all | solution.py:318
  96.5 2.9 %collective-permute-start.17 = (bf16[80,128]{1,0:T(8,128)(2,1)S(1)}, bf16[80,128]{1,0:T(8,128)(2,1)S(1)}, u32[]{:S(2)}, u32[]{:S(2)}) collective-permute-start(bf16[80,128]{1,0:T(8,128)(2,1)S(1)} %copy-done.7), channel_id=1, source_target_pairs={{0,192},{4,196},{8,200},{12,204},{16,208},{20,212},{24,216},{28,22... | collective-permute-start | bytes 61448 | tf_op jit(solution)/shard_map/ppermute | solution.py:29
  98.5 4.1 %collective-permute-start.16 = (bf16[80,128]{1,0:T(8,128)(2,1)S(1)}, bf16[80,128]{1,0:T(8,128)(2,1)S(1)}, u32[]{:S(2)}, u32[]{:S(2)}) collective-permute-start(bf16[80,128]{1,0:T(8,128)(2,1)S(1)} %copy-done.7), channel_id=1, source_target_pairs={{0,128},{4,132},{8,136},{12,140},{16,144},{20,148},{24,152},{28,15... | collective-permute-start | bytes 61448 | tf_op jit(solution)/shard_map/ppermute | solution.py:29
  98.5 4.1 %collective-permute-start.15 = (bf16[80,128]{1,0:T(8,128)(2,1)S(1)}, bf16[80,128]{1,0:T(8,128)(2,1)S(1)}, u32[]{:S(2)}, u32[]{:S(2)}) collective-permute-start(bf16[80,128]{1,0:T(8,128)(2,1)S(1)} %copy-done.7), channel_id=1, source_target_pairs={{0,64},{4,68},{8,72},{12,76},{16,80},{20,84},{24,88},{28,92},{32,9... | collective-permute-start | bytes 61448 | tf_op jit(solution)/shard_map/ppermute | solution.py:29
  111.8 24.2 %all-to-all-start.2 = ((bf16[8,4,80,128]{3,2,1,0:T(8,128)(2,1)}), bf16[8,4,80,128]{3,2,1,0:T(8,128)(2,1)S(1)}, u32[]{:S(2)}, u32[]{:S(2)}) async-start(bf16[8,4,80,128]{3,2,1,0:T(8,128)(2,1)} %broadcast_in_dim.17), calls=%async_computation.3 | async-start | bytes 1310720 | tf_op jit(solution)/shard_map/all_to_all | solution.py:321
  115.3 21.2 %collective-permute-start.10 = (bf16[8,176,128]{2,1,0:T(8,128)(2,1)S(1)}, bf16[8,176,128]{2,1,0:T(8,128)(2,1)S(1)}, u32[]{:S(2)}, u32[]{:S(2)}) collective-permute-start(bf16[8,176,128]{2,1,0:T(8,128)(2,1)S(1)} %all-to-all-done.1.refs_0_), channel_id=1, source_target_pairs={{0,192},{4,196},{8,200},{12,204},{16,208},{20,212},{24,216},{28,22... | collective-permute-start | bytes 1081352 | tf_op jit(solution)/shard_map/ppermute | solution.py:29
  117.3 19.7 %collective-permute-start.9 = (bf16[8,176,128]{2,1,0:T(8,128)(2,1)S(1)}, bf16[8,176,128]{2,1,0:T(8,128)(2,1)S(1)}, u32[]{:S(2)}, u32[]{:S(2)}) collective-permute-start(bf16[8,176,128]{2,1,0:T(8,128)(2,1)S(1)} %all-to-all-done.1.refs_0_), channel_id=1, source_target_pairs={{0,128},{4,132},{8,136},{12,140},{16,144},{20,148},{24,152},{28,15... | collective-permute-start | bytes 1081352 | tf_op jit(solution)/shard_map/ppermute | solution.py:29
  117.3 19.8 %collective-permute-start.8 = (bf16[8,176,128]{2,1,0:T(8,128)(2,1)S(1)}, bf16[8,176,128]{2,1,0:T(8,128)(2,1)S(1)}, u32[]{:S(2)}, u32[]{:S(2)}) collective-permute-start(bf16[8,176,128]{2,1,0:T(8,128)(2,1)S(1)} %all-to-all-done.1.refs_0_), channel_id=1, source_target_pairs={{0,64},{4,68},{8,72},{12,76},{16,80},{20,84},{24,88},{28,92},{32,9... | collective-permute-start | bytes 1081352 | tf_op jit(solution)/shard_map/ppermute | solution.py:29
  136.0 4.3 %collective-permute-start.18 = (bf16[8,4,80,128]{3,2,1,0:T(8,128)(2,1)S(1)}, bf16[8,4,80,128]{3,2,1,0:T(8,128)(2,1)S(1)}, u32[]{:S(2)}, u32[]{:S(2)}) collective-permute-start(bf16[8,4,80,128]{3,2,1,0:T(8,128)(2,1)S(1)} %all-to-all-done.2.refs_8_), channel_id=1, source_target_pairs={{0,4},{4,0},{8,12},{12,8},{16,20},{20,16},{24,28},{28,24},{32,36},... | collective-permute-start | bytes 1966088 | tf_op jit(solution)/shard_map/ppermute | solution.py:29
  136.5 2.2 %collective-permute-start.11 = (bf16[8,176,128]{2,1,0:T(8,128)(2,1)S(1)}, bf16[8,176,128]{2,1,0:T(8,128)(2,1)S(1)}, u32[]{:S(2)}, u32[]{:S(2)}) collective-permute-start(bf16[8,176,128]{2,1,0:T(8,128)(2,1)S(1)} %all-to-all-done.1.refs_0_), channel_id=1, source_target_pairs={{0,4},{4,0},{8,12},{12,8},{16,20},{20,16},{24,28},{28,24},{32,36},... | collective-permute-start | bytes 1081352 | tf_op jit(solution)/shard_map/ppermute | solution.py:29
  136.5 2.7 %collective-permute-start.14 = (bf16[8,176,128]{2,1,0:T(8,128)(2,1)S(1)}, bf16[8,176,128]{2,1,0:T(8,128)(2,1)S(1)}, u32[]{:S(2)}, u32[]{:S(2)}) collective-permute-start(bf16[8,176,128]{2,1,0:T(8,128)(2,1)S(1)} %collective-permute-done.10.refs_3_), channel_id=1, source_target_pairs={{0,4},{4,0},{8,12},{12,8},{16,20},{20,16},{24,28},{28,24},{32,36},... | collective-permute-start | bytes 1081352 | tf_op jit(solution)/shard_map/ppermute | solution.py:29
  137.0 2.8 %collective-permute-start.13 = (bf16[8,176,128]{2,1,0:T(8,128)(2,1)S(1)}, bf16[8,176,128]{2,1,0:T(8,128)(2,1)S(1)}, u32[]{:S(2)}, u32[]{:S(2)}) collective-permute-start(bf16[8,176,128]{2,1,0:T(8,128)(2,1)S(1)} %collective-permute-done.9.refs_2_), channel_id=1, source_target_pairs={{0,4},{4,0},{8,12},{12,8},{16,20},{20,16},{24,28},{28,24},{32,36},... | collective-permute-start | bytes 1081352 | tf_op jit(solution)/shard_map/ppermute | solution.py:29
  137.1 3.2 %collective-permute-start.12 = (bf16[8,176,128]{2,1,0:T(8,128)(2,1)S(1)}, bf16[8,176,128]{2,1,0:T(8,128)(2,1)S(1)}, u32[]{:S(2)}, u32[]{:S(2)}) collective-permute-start(bf16[8,176,128]{2,1,0:T(8,128)(2,1)S(1)} %collective-permute-done.8.refs_1_), channel_id=1, source_target_pairs={{0,4},{4,0},{8,12},{12,8},{16,20},{20,16},{24,28},{28,24},{32,36},... | collective-permute-start | bytes 1081352 | tf_op jit(solution)/shard_map/ppermute | solution.py:29
  142.4 8.3 %collective-permute-start.19 = (bf16[7,128,128]{2,1,0:T(8,128)(2,1)S(1)}, bf16[7,128,128]{2,1,0:T(8,128)(2,1)S(1)}, u32[]{:S(2)}, u32[]{:S(2)}) collective-permute-start(bf16[7,128,128]{2,1,0:T(8,128)(2,1)S(1)} %get-tuple-element.27), channel_id=1, source_target_pairs={{0,1},{1,2},{2,3},{3,0},{4,5},{5,6},{6,7},{7,4},{8,9},{9,10},{10,1... | collective-permute-start | bytes 688136 | tf_op jit(solution)/shard_map/ppermute | solution.py:33
  143.7 12.9 %collective-permute-start.20 = (bf16[7,128,128]{2,1,0:T(8,128)(2,1)S(1)}, bf16[7,128,128]{2,1,0:T(8,128)(2,1)S(1)}, u32[]{:S(2)}, u32[]{:S(2)}) collective-permute-start(bf16[7,128,128]{2,1,0:T(8,128)(2,1)S(1)} %get-tuple-element.28), channel_id=1, source_target_pairs={{0,2},{1,3},{2,0},{3,1},{4,6},{5,7},{6,4},{7,5},{8,10},{9,11},{10,... | collective-permute-start | bytes 688136 | tf_op jit(solution)/shard_map/ppermute | solution.py:33
  146.3 10.3 %collective-permute-start.21 = (bf16[7,128,128]{2,1,0:T(8,128)(2,1)S(1)}, bf16[7,128,128]{2,1,0:T(8,128)(2,1)S(1)}, u32[]{:S(2)}, u32[]{:S(2)}) collective-permute-start(bf16[7,128,128]{2,1,0:T(8,128)(2,1)S(1)} %get-tuple-element.29), channel_id=1, source_target_pairs={{0,3},{1,0},{2,1},{3,2},{4,7},{5,4},{6,5},{7,6},{8,11},{9,8},{10,9... | collective-permute-start | bytes 688136 | tf_op jit(solution)/shard_map/ppermute | solution.py:33
  (3 other events, 1.9 us)
Sparse Core Ops, SparseCore 0:
  17.9 41.2 all-gather.2
  92.3 55.4 reduce-scatter.1

commit v8 on v7

--- a/solution.py
+++ b/solution.py
@@ -322,7 +322,8 @@
     parts = own + [moved(part, dc=1) for part in own] + [last_own, moved(last_own, dc=1)]
 
     mine, *away = in_terms(place, in_index, encodings, parts)
-    in_grad = sum((moved_smp(a, d + 1).astype(F32) for d, a in enumerate(away)), mine).astype(BF16)
+    came = [moved_smp(away[d - 1], d) for d in (2, 1, 3)]
+    in_grad = sum((part.astype(F32) for part in came), mine).astype(BF16)
     return (out_grad, in_grad)
 
 

time: 165 us -> 165 us (level)
  no operation moved by 1% of the time
where the time goes in v8:
time: 165 us; the launch traced here: 164 us
  waiting for transfers between devices  77.6 us (47%)
  starting transfers between devices  40.9 us (25%)
  Pallas kernels  21.6 us (13%)
  between operations  14.3 us (9%)
  local copies, waits for them, and re-layouts  6.18 us (4%)
  other arithmetic  3.55 us (2%)
    ppermute x19, waiting for transfers between devices, moved(): return lax.ppermute(value, 'blk', pairs)  35.3 us
    ppermute x19, starting transfers between devices, moved(): return lax.ppermute(value, 'blk', pairs)  20 us
    all_to_all x1, waiting for transfers between devices, per_device(): last_own = lax.all_to_all(copies, 'blk', 0, 0, axis_index_groups=LINES)  18 us
    ppermute x3, waiting for transfers between devices, moved_smp(): return lax.ppermute(value, 'smp', [(i, (i + dy) % NY) for i in range(NY)])  8.44 us
    pallas_call x1, Pallas kernels, hidden_sums(): pl.pallas_call(hidden_kernel, grid_spec=pltpu.PrefetchScalarGridSpec(num_...  8.39 us
    all_to_all x1, waiting for transfers between devices, per_device(): along_z = lax.all_to_all(copies, 'blk', 0, 0, axis_index_groups=LINES)  8.23 us
    pallas_call x1, Pallas kernels, out_terms(): pl.pallas_call(out_kernel, grid_spec=pltpu.PrefetchScalarGridSpec(num_sca...  8.22 us
    all_to_all x1, starting transfers between devices, per_device(): got = lax.all_to_all(by_z, 'blk', 0, 0, axis_index_groups=LINES)  8.19 us
  transfers between devices with their start and end apart: 27, of which 15 were waited for; matrix products, arithmetic and copies ran while one was open for 2% of the time, Pallas kernels for 13%

profile of v8, /device:TPU:1, one launch (start us, length us, event | category | flops | bytes accessed | tf_op | source)
XLA Modules:
  0.0 164.1 jit_solution(3034513590662555686)
XLA Ops:
  7.2 0.9 fusion.5
  8.1 3.7 %collective-permute-start.1 = (bf16[128,256]{0,1:T(8,128)(2,1)S(1)}, bf16[128,256]{0,1:T(8,128)(2,1)S(1)}, u32[]{:S(2)}, u32[]{:S(2)}) collective-permute-start(bf16[128,256]{0,1:T(8,128)(2,1)S(1)} %get-tuple-element.32), channel_id=1, source_target_pairs={{0,128},{4,132},{8,136},{12,140},{16,144},{20,148},{24,152},{28,15... | collective-permute-start | bytes 196616 | tf_op jit(solution)/shard_map/ppermute | solution.py:29
  12.1 2.4 %collective-permute-start.2 = (bf16[128,256]{0,1:T(8,128)(2,1)S(1)}, bf16[128,256]{0,1:T(8,128)(2,1)S(1)}, u32[]{:S(2)}, u32[]{:S(2)}) collective-permute-start(bf16[128,256]{0,1:T(8,128)(2,1)S(1)} %get-tuple-element.32), channel_id=1, source_target_pairs={{0,192},{4,196},{8,200},{12,204},{16,208},{20,212},{24,216},{28,22... | collective-permute-start | bytes 196616 | tf_op jit(solution)/shard_map/ppermute | solution.py:29
  14.5 2.4 %collective-permute-done = bf16[128,256]{0,1:T(8,128)(2,1)S(1)} collective-permute-done((bf16[128,256]{0,1:T(8,128)(2,1)S(1)}, bf16[128,256]{0,1:T(8,128)(2,1)S(1)}, u32[]{:S(2)}, u32[]{:S(2)}) %collective-permute-start) | collective-permute-done | bytes 65568 | tf_op jit(solution)/shard_map/ppermute | solution.py:29
  18.7 8.4 %hidden_sums.1 = (bf16[32,256,128]{2,1,0:T(8,128)(2,1)S(1)}, f32[32,256,128]{2,1,0:T(8,128)S(1)}) custom-call(s32[4]{0:T(128)S(1)} %pad_add_fusion.place, s32[2,84]{1,0:T(2,128)S(1)} %bitcast.23, bf16[256,10752]{1,0:T(8,128)(2,1)} %cot_ref.3, bf16[168,128,128]{2,1,0:T(8,128)(2,1)} %weight_ref.1, bf16[128,256]{1,0:T(8,128)(2,1)S(1)} %copy.14.before_ref), custom_call_target="tpu_custom_call" | custom-call | flops 3000000000 | bytes 16777216 | tf_op jit(solution)/shard_map/hidden_sums/pallas_call | solution.py:90
  27.0 1.5 collective-permute-start.3
  28.5 3.8 %collective-permute-done.3 = bf16[32,256,128]{2,1,0:T(8,128)(2,1)S(1)} collective-permute-done((bf16[32,256,128]{2,1,0:T(8,128)(2,1)S(1)}, bf16[32,256,128]{2,1,0:T(8,128)(2,1)S(1)}, u32[]{:S(2)}, u32[]{:S(2)}) %collective-permute-start.3) | collective-permute-done | bytes 2097184 | tf_op jit(solution)/shard_map/ppermute | solution.py:29
  32.3 1.4 core_sums.1
  34.5 3.4 %collective-permute-start.5 = (bf16[8,256,128]{2,1,0:T(8,128)(2,1)S(1)}, bf16[8,256,128]{2,1,0:T(8,128)(2,1)S(1)}, u32[]{:S(2)}, u32[]{:S(2)}) collective-permute-start(bf16[8,256,128]{2,1,0:T(8,128)(2,1)S(1)} %get-tuple-element.20), channel_id=1, source_target_pairs={{0,128},{4,132},{8,136},{12,140},{16,144},{20,148},{24,152},{28,15... | collective-permute-start | bytes 1572872 | tf_op jit(solution)/shard_map/ppermute | solution.py:29
  37.9 10.8 %collective-permute-done.4.a_ref = bf16[8,256,128]{2,1,0:T(8,128)(2,1)S(1)} collective-permute-done((bf16[8,256,128]{2,1,0:T(8,128)(2,1)S(1)}, bf16[8,256,128]{2,1,0:T(8,128)(2,1)S(1)}, u32[]{:S(2)}, u32[]{:S(2)}) %collective-permute-start.4) | collective-permute-done | bytes 524320 | tf_op jit(solution)/shard_map/ppermute | solution.py:29
  48.7 12.1 %collective-permute-done.5.b_ref = bf16[8,256,128]{2,1,0:T(8,128)(2,1)S(1)} collective-permute-done((bf16[8,256,128]{2,1,0:T(8,128)(2,1)S(1)}, bf16[8,256,128]{2,1,0:T(8,128)(2,1)S(1)}, u32[]{:S(2)}, u32[]{:S(2)}) %collective-permute-start.5) | collective-permute-done | bytes 524320 | tf_op jit(solution)/shard_map/ppermute | solution.py:29
  60.8 1.6 line_sums.1
  63.1 1.2 collective-permute-start.7
  64.3 8.2 %all-to-all-start = ((bf16[8,256,128]{2,1,0:T(8,128)(2,1)}), bf16[8,256,128]{2,1,0:T(8,128)(2,1)S(1)}, u32[]{:S(2)}, u32[]{:S(2)}) async-start(bf16[8,256,128]{2,1,0:T(8,128)(2,1)} %get-tuple-element.25), calls=%async_computation | async-start | bytes 1048576 | tf_op jit(solution)/shard_map/all_to_all | solution.py:306
  72.5 1.6 copy-done
  74.1 8.2 %out_terms.1 = (bf16[168,128,128]{2,1,0:T(8,128)(2,1)}, f32[8,128]{1,0:T(8,128)S(1)}) custom-call(s32[4]{0:T(128)S(1)} %pad_add_fusion.place, s32[2,84]{1,0:T(2,128)S(1)} %bitcast.24, bf16[256,10752]{1,0:T(8,128)(2,1)} %cot_ref.3, bf16[32,128,256]{2,1,0:T(8,128)(2,1)S(1)} %copy-done, bf16[32,128,256]{2,1,0:T(8,128)(2,1)S(1)} %collective-permute-done.7.other_ref), custom_call_target="tpu_custom_call" | custom-call | flops 3000000000 | bytes 16777216 | tf_op jit(solution)/shard_map/out_terms/pallas_call | solution.py:199
  82.9 7.5 %all-to-all-done = bf16[8,256,128]{2,1,0:T(8,128)(2,1)S(1)} async-done(((bf16[8,256,128]{2,1,0:T(8,128)(2,1)}), bf16[8,256,128]{2,1,0:T(8,128)(2,1)S(1)}, u32[]{:S(2)}, u32[]{:S(2)}) %all-to-all-start) | async-done | bytes 524320 | tf_op jit(solution)/shard_map/all_to_all | solution.py:306
  90.5 1.1 select_reduce_fusion
  93.1 3.4 %all-to-all-start.1 = ((bf16[8,176,128]{2,1,0:T(8,128)(2,1)}), bf16[8,176,128]{2,1,0:T(8,128)(2,1)S(1)}, u32[]{:S(2)}, u32[]{:S(2)}) async-start(bf16[8,176,128]{2,1,0:T(8,128)(2,1)} %broadcast_in_dim.16), calls=%async_computation.2 | async-start | bytes 720896 | tf_op jit(solution)/shard_map/all_to_all | solution.py:318
  96.5 2.0 %collective-permute-start.17 = (bf16[80,128]{1,0:T(8,128)(2,1)S(1)}, bf16[80,128]{1,0:T(8,128)(2,1)S(1)}, u32[]{:S(2)}, u32[]{:S(2)}) collective-permute-start(bf16[80,128]{1,0:T(8,128)(2,1)S(1)} %copy-done.7), channel_id=1, source_target_pairs={{0,192},{4,196},{8,200},{12,204},{16,208},{20,212},{24,216},{28,22... | collective-permute-start | bytes 61448 | tf_op jit(solution)/shard_map/ppermute | solution.py:29
  99.4 3.2 %collective-permute-done.16 = bf16[80,128]{1,0:T(8,128)(2,1)S(1)} collective-permute-done((bf16[80,128]{1,0:T(8,128)(2,1)S(1)}, bf16[80,128]{1,0:T(8,128)(2,1)S(1)}, u32[]{:S(2)}, u32[]{:S(2)}) %collective-permute-start.16) | collective-permute-done | bytes 20512 | tf_op jit(solution)/shard_map/ppermute | solution.py:29
  102.6 8.2 %all-to-all-done.1.refs_0_ = bf16[8,176,128]{2,1,0:T(8,128)(2,1)S(1)} async-done(((bf16[8,176,128]{2,1,0:T(8,128)(2,1)}), bf16[8,176,128]{2,1,0:T(8,128)(2,1)S(1)}, u32[]{:S(2)}, u32[]{:S(2)}) %all-to-all-start.1) | async-done | bytes 360480 | tf_op jit(solution)/shard_map/all_to_all | solution.py:318
  110.9 0.9 broadcast_in_dim.17
  111.8 3.5 %all-to-all-start.2 = ((bf16[8,4,80,128]{3,2,1,0:T(8,128)(2,1)}), bf16[8,4,80,128]{3,2,1,0:T(8,128)(2,1)S(1)}, u32[]{:S(2)}, u32[]{:S(2)}) async-start(bf16[8,4,80,128]{3,2,1,0:T(8,128)(2,1)} %broadcast_in_dim.17), calls=%async_computation.3 | async-start | bytes 1310720 | tf_op jit(solution)/shard_map/all_to_all | solution.py:321
  115.3 2.0 %collective-permute-start.10 = (bf16[8,176,128]{2,1,0:T(8,128)(2,1)S(1)}, bf16[8,176,128]{2,1,0:T(8,128)(2,1)S(1)}, u32[]{:S(2)}, u32[]{:S(2)}) collective-permute-start(bf16[8,176,128]{2,1,0:T(8,128)(2,1)S(1)} %all-to-all-done.1.refs_0_), channel_id=1, source_target_pairs={{0,192},{4,196},{8,200},{12,204},{16,208},{20,212},{24,216},{28,22... | collective-permute-start | bytes 1081352 | tf_op jit(solution)/shard_map/ppermute | solution.py:29
  118.0 18.0 %all-to-all-done.2.refs_8_ = bf16[8,4,80,128]{3,2,1,0:T(8,128)(2,1)S(1)} async-done(((bf16[8,4,80,128]{3,2,1,0:T(8,128)(2,1)}), bf16[8,4,80,128]{3,2,1,0:T(8,128)(2,1)S(1)}, u32[]{:S(2)}, u32[]{:S(2)}) %all-to-all-start.2) | async-done | bytes 655392 | tf_op jit(solution)/shard_map/all_to_all | solution.py:321
  137.5 1.2 collective-permute-done.11.refs_4_
  140.3 2.0 %in_terms.1 = (f32[7,128,128]{2,1,0:T(8,128)S(1)}, bf16[7,128,128]{2,1,0:T(8,128)(2,1)S(1)}, bf16[7,128,128]{2,1,0:T(8,128)(2,1)S(1)}, bf16[7,128,128]{2,1,0:T(8,128)(2,1)S(1)}) custom-call(s32[4]{0:T(128)S(1)} %pad_add_fusion.place, s32[4,7]{1,0:T(4,128)S(1)} %bitcast.22, bf16[256,896]{1,0:T(8,128)(2,1)S(1)} %copy-done.2, ...), custom_call_target="tpu_custom_call" | custom-call | flops 500000000 | bytes 8388608 | tf_op jit(solution)/shard_map/in_terms/pallas_call | solution.py:263
  142.4 3.0 %collective-permute-start.19 = (bf16[7,128,128]{2,1,0:T(8,128)(2,1)S(1)}, bf16[7,128,128]{2,1,0:T(8,128)(2,1)S(1)}, u32[]{:S(2)}, u32[]{:S(2)}) collective-permute-start(bf16[7,128,128]{2,1,0:T(8,128)(2,1)S(1)} %get-tuple-element.27), channel_id=1, source_target_pairs={{0,2},{1,3},{2,0},{3,1},{4,6},{5,7},{6,4},{7,5},{8,10},{9,11},{10,... | collective-permute-start | bytes 688136 | tf_op jit(solution)/shard_map/ppermute | solution.py:33
  145.8 2.3 %collective-permute-start.21 = (bf16[7,128,128]{2,1,0:T(8,128)(2,1)S(1)}, bf16[7,128,128]{2,1,0:T(8,128)(2,1)S(1)}, u32[]{:S(2)}, u32[]{:S(2)}) collective-permute-start(bf16[7,128,128]{2,1,0:T(8,128)(2,1)S(1)} %get-tuple-element.29), channel_id=1, source_target_pairs={{0,3},{1,0},{2,1},{3,2},{4,7},{5,4},{6,5},{7,6},{8,11},{9,8},{10,9... | collective-permute-start | bytes 688136 | tf_op jit(solution)/shard_map/ppermute | solution.py:33
  148.0 2.9 %collective-permute-done.19 = bf16[7,128,128]{2,1,0:T(8,128)(2,1)S(1)} collective-permute-done((bf16[7,128,128]{2,1,0:T(8,128)(2,1)S(1)}, bf16[7,128,128]{2,1,0:T(8,128)(2,1)S(1)}, u32[]{:S(2)}, u32[]{:S(2)}) %collective-permute-start.19) | collective-permute-done | bytes 229408 | tf_op jit(solution)/shard_map/ppermute | solution.py:33
  150.9 5.5 %collective-permute-done.20 = bf16[7,128,128]{2,1,0:T(8,128)(2,1)S(1)} collective-permute-done((bf16[7,128,128]{2,1,0:T(8,128)(2,1)S(1)}, bf16[7,128,128]{2,1,0:T(8,128)(2,1)S(1)}, u32[]{:S(2)}, u32[]{:S(2)}) %collective-permute-start.20) | collective-permute-done | bytes 229408 | tf_op jit(solution)/shard_map/ppermute | solution.py:33
  (61 shorter events, 11.5 us)
Async XLA Ops:
  7.2 55.9 %all-gather.3.cloned.1.call-start = ((), (), s32[]{:S(2)}) async-start(), calls=%async_computation.5 | async-start | bytes 2359296 | tf_op jit(solution)/shard_map/all_gather | solution.py:300
  8.1 6.3 %collective-permute-start.1 = (bf16[128,256]{0,1:T(8,128)(2,1)S(1)}, bf16[128,256]{0,1:T(8,128)(2,1)S(1)}, u32[]{:S(2)}, u32[]{:S(2)}) collective-permute-start(bf16[128,256]{0,1:T(8,128)(2,1)S(1)} %get-tuple-element.32), channel_id=1, source_target_pairs={{0,128},{4,132},{8,136},{12,140},{16,144},{20,148},{24,152},{28,15... | collective-permute-start | bytes 196616 | tf_op jit(solution)/shard_map/ppermute | solution.py:29
  11.8 5.0 %collective-permute-start = (bf16[128,256]{0,1:T(8,128)(2,1)S(1)}, bf16[128,256]{0,1:T(8,128)(2,1)S(1)}, u32[]{:S(2)}, u32[]{:S(2)}) collective-permute-start(bf16[128,256]{0,1:T(8,128)(2,1)S(1)} %get-tuple-element.32), channel_id=1, source_target_pairs={{0,64},{4,68},{8,72},{12,76},{16,80},{20,84},{24,88},{28,92},{32,9... | collective-permute-start | bytes 196616 | tf_op jit(solution)/shard_map/ppermute | solution.py:29
  12.1 4.7 %collective-permute-start.2 = (bf16[128,256]{0,1:T(8,128)(2,1)S(1)}, bf16[128,256]{0,1:T(8,128)(2,1)S(1)}, u32[]{:S(2)}, u32[]{:S(2)}) collective-permute-start(bf16[128,256]{0,1:T(8,128)(2,1)S(1)} %get-tuple-element.32), channel_id=1, source_target_pairs={{0,192},{4,196},{8,200},{12,204},{16,208},{20,212},{24,216},{28,22... | collective-permute-start | bytes 196616 | tf_op jit(solution)/shard_map/ppermute | solution.py:29
  27.0 5.3 %collective-permute-start.3 = (bf16[32,256,128]{2,1,0:T(8,128)(2,1)S(1)}, bf16[32,256,128]{2,1,0:T(8,128)(2,1)S(1)}, u32[]{:S(2)}, u32[]{:S(2)}) collective-permute-start(bf16[32,256,128]{2,1,0:T(8,128)(2,1)S(1)} %get-tuple-element.17), channel_id=1, source_target_pairs={{0,4},{4,0},{8,12},{12,8},{16,20},{20,16},{24,28},{28,24},{32,36},... | collective-permute-start | bytes 6291464 | tf_op jit(solution)/shard_map/ppermute | solution.py:29
  33.7 15.0 %collective-permute-start.4 = (bf16[8,256,128]{2,1,0:T(8,128)(2,1)S(1)}, bf16[8,256,128]{2,1,0:T(8,128)(2,1)S(1)}, u32[]{:S(2)}, u32[]{:S(2)}) collective-permute-start(bf16[8,256,128]{2,1,0:T(8,128)(2,1)S(1)} %get-tuple-element.19), channel_id=1, source_target_pairs={{0,64},{4,68},{8,72},{12,76},{16,80},{20,84},{24,88},{28,92},{32,9... | collective-permute-start | bytes 1572872 | tf_op jit(solution)/shard_map/ppermute | solution.py:29
  34.5 26.3 %collective-permute-start.5 = (bf16[8,256,128]{2,1,0:T(8,128)(2,1)S(1)}, bf16[8,256,128]{2,1,0:T(8,128)(2,1)S(1)}, u32[]{:S(2)}, u32[]{:S(2)}) collective-permute-start(bf16[8,256,128]{2,1,0:T(8,128)(2,1)S(1)} %get-tuple-element.20), channel_id=1, source_target_pairs={{0,128},{4,132},{8,136},{12,140},{16,144},{20,148},{24,152},{28,15... | collective-permute-start | bytes 1572872 | tf_op jit(solution)/shard_map/ppermute | solution.py:29
  37.9 22.9 %collective-permute-start.6 = (bf16[8,256,128]{2,1,0:T(8,128)(2,1)S(1)}, bf16[8,256,128]{2,1,0:T(8,128)(2,1)S(1)}, u32[]{:S(2)}, u32[]{:S(2)}) collective-permute-start(bf16[8,256,128]{2,1,0:T(8,128)(2,1)S(1)} %get-tuple-element.21), channel_id=1, source_target_pairs={{0,192},{4,196},{8,200},{12,204},{16,208},{20,212},{24,216},{28,22... | collective-permute-start | bytes 1572872 | tf_op jit(solution)/shard_map/ppermute | solution.py:29
  63.1 9.5 %copy-start.6 = (s32[84,2]{0,1:T(2,128)S(1)}, s32[84,2]{0,1:T(2,128)}, u32[]{:S(2)}) copy-start(s32[84,2]{0,1:T(2,128)} %param.10) | copy-start | bytes 2020
  63.1 9.5 %collective-permute-start.7 = (bf16[32,128,256]{2,1,0:T(8,128)(2,1)}, bf16[32,128,256]{2,1,0:T(8,128)(2,1)S(1)}, u32[]{:S(2)}, u32[]{:S(2)}) collective-permute-start(bf16[32,128,256]{2,1,0:T(8,128)(2,1)} %after.3.own_ref), channel_id=1, source_target_pairs={{0,4},{4,0},{8,12},{12,8},{16,20},{20,16},{24,28},{28,24},{32,36},... | collective-permute-start | bytes 6291464 | tf_op jit(solution)/shard_map/ppermute | solution.py:29
  64.3 26.2 %all-to-all-start = ((bf16[8,256,128]{2,1,0:T(8,128)(2,1)}), bf16[8,256,128]{2,1,0:T(8,128)(2,1)S(1)}, u32[]{:S(2)}, u32[]{:S(2)}) async-start(bf16[8,256,128]{2,1,0:T(8,128)(2,1)} %get-tuple-element.25), calls=%async_computation | async-start | bytes 1048576 | tf_op jit(solution)/shard_map/all_to_all | solution.py:306
  72.5 84.8 %reduce-scatter.2.cloned.1.call-start = ((), (), s32[]{:S(2)}) async-start(), calls=%async_computation.4 | async-start | bytes 6881280 | tf_op jit(solution)/shard_map/reduce_scatter | solution.py:314
  72.5 1.6 copy-start
  92.2 4.3 %copy-start.7 = (bf16[80,128]{1,0:T(8,128)(2,1)S(1)}, bf16[80,128]{1,0:T(8,128)(2,1)}, u32[]{:S(2)}) copy-start(bf16[80,128]{1,0:T(8,128)(2,1)} %fusion.7.refs_1_) | copy-start | bytes 61444
  92.2 48.1 %copy-start.2 = (bf16[256,896]{1,0:T(8,128)(2,1)S(1)}, bf16[256,896]{1,0:T(8,128)(2,1)}, u32[]{:S(2)}) copy-start(bf16[256,896]{1,0:T(8,128)(2,1)} %enc_ref.1) | copy-start | bytes 1376260
  92.2 48.1 %copy-start.4 = (s32[7,4]{0,1:T(4,128)S(1)}, s32[7,4]{0,1:T(4,128)}, u32[]{:S(2)}) copy-start(s32[7,4]{0,1:T(4,128)} %param.11) | copy-start | bytes 340
  93.1 17.8 %all-to-all-start.1 = ((bf16[8,176,128]{2,1,0:T(8,128)(2,1)}), bf16[8,176,128]{2,1,0:T(8,128)(2,1)S(1)}, u32[]{:S(2)}, u32[]{:S(2)}) async-start(bf16[8,176,128]{2,1,0:T(8,128)(2,1)} %broadcast_in_dim.16), calls=%async_computation.2 | async-start | bytes 720896 | tf_op jit(solution)/shard_map/all_to_all | solution.py:318
  96.5 2.9 %collective-permute-start.17 = (bf16[80,128]{1,0:T(8,128)(2,1)S(1)}, bf16[80,128]{1,0:T(8,128)(2,1)S(1)}, u32[]{:S(2)}, u32[]{:S(2)}) collective-permute-start(bf16[80,128]{1,0:T(8,128)(2,1)S(1)} %copy-done.7), channel_id=1, source_target_pairs={{0,192},{4,196},{8,200},{12,204},{16,208},{20,212},{24,216},{28,22... | collective-permute-start | bytes 61448 | tf_op jit(solution)/shard_map/ppermute | solution.py:29
  98.5 4.1 %collective-permute-start.16 = (bf16[80,128]{1,0:T(8,128)(2,1)S(1)}, bf16[80,128]{1,0:T(8,128)(2,1)S(1)}, u32[]{:S(2)}, u32[]{:S(2)}) collective-permute-start(bf16[80,128]{1,0:T(8,128)(2,1)S(1)} %copy-done.7), channel_id=1, source_target_pairs={{0,128},{4,132},{8,136},{12,140},{16,144},{20,148},{24,152},{28,15... | collective-permute-start | bytes 61448 | tf_op jit(solution)/shard_map/ppermute | solution.py:29
  98.5 4.1 %collective-permute-start.15 = (bf16[80,128]{1,0:T(8,128)(2,1)S(1)}, bf16[80,128]{1,0:T(8,128)(2,1)S(1)}, u32[]{:S(2)}, u32[]{:S(2)}) collective-permute-start(bf16[80,128]{1,0:T(8,128)(2,1)S(1)} %copy-done.7), channel_id=1, source_target_pairs={{0,64},{4,68},{8,72},{12,76},{16,80},{20,84},{24,88},{28,92},{32,9... | collective-permute-start | bytes 61448 | tf_op jit(solution)/shard_map/ppermute | solution.py:29
  111.8 24.2 %all-to-all-start.2 = ((bf16[8,4,80,128]{3,2,1,0:T(8,128)(2,1)}), bf16[8,4,80,128]{3,2,1,0:T(8,128)(2,1)S(1)}, u32[]{:S(2)}, u32[]{:S(2)}) async-start(bf16[8,4,80,128]{3,2,1,0:T(8,128)(2,1)} %broadcast_in_dim.17), calls=%async_computation.3 | async-start | bytes 1310720 | tf_op jit(solution)/shard_map/all_to_all | solution.py:321
  115.3 21.2 %collective-permute-start.10 = (bf16[8,176,128]{2,1,0:T(8,128)(2,1)S(1)}, bf16[8,176,128]{2,1,0:T(8,128)(2,1)S(1)}, u32[]{:S(2)}, u32[]{:S(2)}) collective-permute-start(bf16[8,176,128]{2,1,0:T(8,128)(2,1)S(1)} %all-to-all-done.1.refs_0_), channel_id=1, source_target_pairs={{0,192},{4,196},{8,200},{12,204},{16,208},{20,212},{24,216},{28,22... | collective-permute-start | bytes 1081352 | tf_op jit(solution)/shard_map/ppermute | solution.py:29
  117.3 19.7 %collective-permute-start.9 = (bf16[8,176,128]{2,1,0:T(8,128)(2,1)S(1)}, bf16[8,176,128]{2,1,0:T(8,128)(2,1)S(1)}, u32[]{:S(2)}, u32[]{:S(2)}) collective-permute-start(bf16[8,176,128]{2,1,0:T(8,128)(2,1)S(1)} %all-to-all-done.1.refs_0_), channel_id=1, source_target_pairs={{0,128},{4,132},{8,136},{12,140},{16,144},{20,148},{24,152},{28,15... | collective-permute-start | bytes 1081352 | tf_op jit(solution)/shard_map/ppermute | solution.py:29
  117.3 19.8 %collective-permute-start.8 = (bf16[8,176,128]{2,1,0:T(8,128)(2,1)S(1)}, bf16[8,176,128]{2,1,0:T(8,128)(2,1)S(1)}, u32[]{:S(2)}, u32[]{:S(2)}) collective-permute-start(bf16[8,176,128]{2,1,0:T(8,128)(2,1)S(1)} %all-to-all-done.1.refs_0_), channel_id=1, source_target_pairs={{0,64},{4,68},{8,72},{12,76},{16,80},{20,84},{24,88},{28,92},{32,9... | collective-permute-start | bytes 1081352 | tf_op jit(solution)/shard_map/ppermute | solution.py:29
  136.0 4.3 %collective-permute-start.18 = (bf16[8,4,80,128]{3,2,1,0:T(8,128)(2,1)S(1)}, bf16[8,4,80,128]{3,2,1,0:T(8,128)(2,1)S(1)}, u32[]{:S(2)}, u32[]{:S(2)}) collective-permute-start(bf16[8,4,80,128]{3,2,1,0:T(8,128)(2,1)S(1)} %all-to-all-done.2.refs_8_), channel_id=1, source_target_pairs={{0,4},{4,0},{8,12},{12,8},{16,20},{20,16},{24,28},{28,24},{32,36},... | collective-permute-start | bytes 1966088 | tf_op jit(solution)/shard_map/ppermute | solution.py:29
  136.5 2.2 %collective-permute-start.11 = (bf16[8,176,128]{2,1,0:T(8,128)(2,1)S(1)}, bf16[8,176,128]{2,1,0:T(8,128)(2,1)S(1)}, u32[]{:S(2)}, u32[]{:S(2)}) collective-permute-start(bf16[8,176,128]{2,1,0:T(8,128)(2,1)S(1)} %all-to-all-done.1.refs_0_), channel_id=1, source_target_pairs={{0,4},{4,0},{8,12},{12,8},{16,20},{20,16},{24,28},{28,24},{32,36},... | collective-permute-start | bytes 1081352 | tf_op jit(solution)/shard_map/ppermute | solution.py:29
  136.5 2.7 %collective-permute-start.14 = (bf16[8,176,128]{2,1,0:T(8,128)(2,1)S(1)}, bf16[8,176,128]{2,1,0:T(8,128)(2,1)S(1)}, u32[]{:S(2)}, u32[]{:S(2)}) collective-permute-start(bf16[8,176,128]{2,1,0:T(8,128)(2,1)S(1)} %collective-permute-done.10.refs_3_), channel_id=1, source_target_pairs={{0,4},{4,0},{8,12},{12,8},{16,20},{20,16},{24,28},{28,24},{32,36},... | collective-permute-start | bytes 1081352 | tf_op jit(solution)/shard_map/ppermute | solution.py:29
  137.0 2.8 %collective-permute-start.13 = (bf16[8,176,128]{2,1,0:T(8,128)(2,1)S(1)}, bf16[8,176,128]{2,1,0:T(8,128)(2,1)S(1)}, u32[]{:S(2)}, u32[]{:S(2)}) collective-permute-start(bf16[8,176,128]{2,1,0:T(8,128)(2,1)S(1)} %collective-permute-done.9.refs_2_), channel_id=1, source_target_pairs={{0,4},{4,0},{8,12},{12,8},{16,20},{20,16},{24,28},{28,24},{32,36},... | collective-permute-start | bytes 1081352 | tf_op jit(solution)/shard_map/ppermute | solution.py:29
  137.1 3.2 %collective-permute-start.12 = (bf16[8,176,128]{2,1,0:T(8,128)(2,1)S(1)}, bf16[8,176,128]{2,1,0:T(8,128)(2,1)S(1)}, u32[]{:S(2)}, u32[]{:S(2)}) collective-permute-start(bf16[8,176,128]{2,1,0:T(8,128)(2,1)S(1)} %collective-permute-done.8.refs_1_), channel_id=1, source_target_pairs={{0,4},{4,0},{8,12},{12,8},{16,20},{20,16},{24,28},{28,24},{32,36},... | collective-permute-start | bytes 1081352 | tf_op jit(solution)/shard_map/ppermute | solution.py:29
  142.4 8.6 %collective-permute-start.19 = (bf16[7,128,128]{2,1,0:T(8,128)(2,1)S(1)}, bf16[7,128,128]{2,1,0:T(8,128)(2,1)S(1)}, u32[]{:S(2)}, u32[]{:S(2)}) collective-permute-start(bf16[7,128,128]{2,1,0:T(8,128)(2,1)S(1)} %get-tuple-element.27), channel_id=1, source_target_pairs={{0,2},{1,3},{2,0},{3,1},{4,6},{5,7},{6,4},{7,5},{8,10},{9,11},{10,... | collective-permute-start | bytes 688136 | tf_op jit(solution)/shard_map/ppermute | solution.py:33
  145.3 11.1 %collective-permute-start.20 = (bf16[7,128,128]{2,1,0:T(8,128)(2,1)S(1)}, bf16[7,128,128]{2,1,0:T(8,128)(2,1)S(1)}, u32[]{:S(2)}, u32[]{:S(2)}) collective-permute-start(bf16[7,128,128]{2,1,0:T(8,128)(2,1)S(1)} %get-tuple-element.28), channel_id=1, source_target_pairs={{0,1},{1,2},{2,3},{3,0},{4,5},{5,6},{6,7},{7,4},{8,9},{9,10},{10,1... | collective-permute-start | bytes 688136 | tf_op jit(solution)/shard_map/ppermute | solution.py:33
  145.8 10.7 %collective-permute-start.21 = (bf16[7,128,128]{2,1,0:T(8,128)(2,1)S(1)}, bf16[7,128,128]{2,1,0:T(8,128)(2,1)S(1)}, u32[]{:S(2)}, u32[]{:S(2)}) collective-permute-start(bf16[7,128,128]{2,1,0:T(8,128)(2,1)S(1)} %get-tuple-element.29), channel_id=1, source_target_pairs={{0,3},{1,0},{2,1},{3,2},{4,7},{5,4},{6,5},{7,6},{8,11},{9,8},{10,9... | collective-permute-start | bytes 688136 | tf_op jit(solution)/shard_map/ppermute | solution.py:33
  (3 other events, 1.9 us)
Sparse Core Ops, SparseCore 0:
  17.9 41.2 all-gather.2
  92.3 55.4 reduce-scatter.1

commit v9 on v8

--- a/solution.py
+++ b/solution.py
@@ -11,7 +11,7 @@
 BS = 128
 STEP_BLOCKS = 28
 OUT_STEP = 28
-FIRST, LAST = 176, 80
+FIRST, LAST = 160, 96
 CORE_STEP = 2
 
 

time: 165 us -> 186 us (1.13)
  starting transfers between devices: 40.9 us -> 56.1 us
  waiting for transfers between devices: 77.6 us -> 83.3 us
    ppermute x19, starting transfers between devices: 20 us -> 35 us  [moved(): return lax.ppermute(value, 'blk', pairs)]
    all_to_all x1, waiting for transfers between devices: 18 us -> 22.1 us  [per_device(): last_own = lax.all_to_all(copies, 'blk', 0, 0, axis_index_groups=LINES)]
  transfers between devices with their start and end apart: 27 -> 27, of which waited for: 15 -> 13; matrix products, arithmetic and copies ran while one was open for 2% -> 2% of each run, Pallas kernels for 13% -> 12%
where the time goes in v9:
time: 186 us
  waiting for transfers between devices  83.3 us (45%)
  starting transfers between devices  56.1 us (30%)
  Pallas kernels  21.6 us (12%)
  between operations  14.2 us (8%)
  local copies, waits for them, and re-layouts  6.96 us (4%)
  other arithmetic  3.56 us (2%)
    ppermute x19, waiting for transfers between devices, moved(): return lax.ppermute(value, 'blk', pairs)  36.3 us
    ppermute x19, starting transfers between devices, moved(): return lax.ppermute(value, 'blk', pairs)  35 us
    all_to_all x1, waiting for transfers between devices, per_device(): last_own = lax.all_to_all(copies, 'blk', 0, 0, axis_index_groups=LINES)  22.1 us
    all_to_all x1, waiting for transfers between devices, per_device(): along_z = lax.all_to_all(copies, 'blk', 0, 0, axis_index_groups=LINES)  9.01 us
    pallas_call x1, Pallas kernels, hidden_sums(): pl.pallas_call(hidden_kernel, grid_spec=pltpu.PrefetchScalarGridSpec(num_...  8.39 us
    ppermute x3, waiting for transfers between devices, moved_smp(): return lax.ppermute(value, 'smp', [(i, (i + dy) % NY) for i in range(NY)])  8.35 us
    pallas_call x1, Pallas kernels, out_terms(): pl.pallas_call(out_kernel, grid_spec=pltpu.PrefetchScalarGridSpec(num_sca...  8.22 us
    all_to_all x1, starting transfers between devices, per_device(): got = lax.all_to_all(by_z, 'blk', 0, 0, axis_index_groups=LINES)  8.19 us
  transfers between devices with their start and end apart: 27, of which 13 were waited for; matrix products, arithmetic and copies ran while one was open for 2% of the time, Pallas kernels for 12%

profile of v9, /device:TPU:1, one launch (start us, length us, event | category | flops | bytes accessed | tf_op | source)
XLA Modules:
  0.0 185.8 jit_solution(10411045934026228754)
XLA Ops:
  8.1 3.7 %collective-permute-start.1 = (bf16[128,256]{0,1:T(8,128)(2,1)S(1)}, bf16[128,256]{0,1:T(8,128)(2,1)S(1)}, u32[]{:S(2)}, u32[]{:S(2)}) collective-permute-start(bf16[128,256]{0,1:T(8,128)(2,1)S(1)} %get-tuple-element.32), channel_id=1, source_target_pairs={{0,128},{4,132},{8,136},{12,140},{16,144},{20,148},{24,152},{28,15... | collective-permute-start | bytes 196616 | tf_op jit(solution)/shard_map/ppermute | solution.py:29
  12.1 2.4 %collective-permute-start.2 = (bf16[128,256]{0,1:T(8,128)(2,1)S(1)}, bf16[128,256]{0,1:T(8,128)(2,1)S(1)}, u32[]{:S(2)}, u32[]{:S(2)}) collective-permute-start(bf16[128,256]{0,1:T(8,128)(2,1)S(1)} %get-tuple-element.32), channel_id=1, source_target_pairs={{0,192},{4,196},{8,200},{12,204},{16,208},{20,212},{24,216},{28,22... | collective-permute-start | bytes 196616 | tf_op jit(solution)/shard_map/ppermute | solution.py:29
  14.5 2.4 %collective-permute-done = bf16[128,256]{0,1:T(8,128)(2,1)S(1)} collective-permute-done((bf16[128,256]{0,1:T(8,128)(2,1)S(1)}, bf16[128,256]{0,1:T(8,128)(2,1)S(1)}, u32[]{:S(2)}, u32[]{:S(2)}) %collective-permute-start) | collective-permute-done | bytes 65568 | tf_op jit(solution)/shard_map/ppermute | solution.py:29
  18.7 8.4 %hidden_sums.1 = (bf16[32,256,128]{2,1,0:T(8,128)(2,1)S(1)}, f32[32,256,128]{2,1,0:T(8,128)S(1)}) custom-call(s32[4]{0:T(128)S(1)} %pad_add_fusion.place, s32[2,84]{1,0:T(2,128)S(1)} %bitcast.23, bf16[256,10752]{1,0:T(8,128)(2,1)} %cot_ref.3, bf16[168,128,128]{2,1,0:T(8,128)(2,1)} %weight_ref.1, bf16[128,256]{1,0:T(8,128)(2,1)S(1)} %copy.14.before_ref), custom_call_target="tpu_custom_call" | custom-call | flops 3000000000 | bytes 16777216 | tf_op jit(solution)/shard_map/hidden_sums/pallas_call | solution.py:90
  27.0 1.5 collective-permute-start.3
  28.5 3.8 %collective-permute-done.3 = bf16[32,256,128]{2,1,0:T(8,128)(2,1)S(1)} collective-permute-done((bf16[32,256,128]{2,1,0:T(8,128)(2,1)S(1)}, bf16[32,256,128]{2,1,0:T(8,128)(2,1)S(1)}, u32[]{:S(2)}, u32[]{:S(2)}) %collective-permute-start.3) | collective-permute-done | bytes 2097184 | tf_op jit(solution)/shard_map/ppermute | solution.py:29
  32.3 1.4 core_sums.1
  34.5 3.4 %collective-permute-start.5 = (bf16[8,256,128]{2,1,0:T(8,128)(2,1)S(1)}, bf16[8,256,128]{2,1,0:T(8,128)(2,1)S(1)}, u32[]{:S(2)}, u32[]{:S(2)}) collective-permute-start(bf16[8,256,128]{2,1,0:T(8,128)(2,1)S(1)} %get-tuple-element.20), channel_id=1, source_target_pairs={{0,128},{4,132},{8,136},{12,140},{16,144},{20,148},{24,152},{28,15... | collective-permute-start | bytes 1572872 | tf_op jit(solution)/shard_map/ppermute | solution.py:29
  37.9 10.8 %collective-permute-done.4.a_ref = bf16[8,256,128]{2,1,0:T(8,128)(2,1)S(1)} collective-permute-done((bf16[8,256,128]{2,1,0:T(8,128)(2,1)S(1)}, bf16[8,256,128]{2,1,0:T(8,128)(2,1)S(1)}, u32[]{:S(2)}, u32[]{:S(2)}) %collective-permute-start.4) | collective-permute-done | bytes 524320 | tf_op jit(solution)/shard_map/ppermute | solution.py:29
  48.7 12.1 %collective-permute-done.5.b_ref = bf16[8,256,128]{2,1,0:T(8,128)(2,1)S(1)} collective-permute-done((bf16[8,256,128]{2,1,0:T(8,128)(2,1)S(1)}, bf16[8,256,128]{2,1,0:T(8,128)(2,1)S(1)}, u32[]{:S(2)}, u32[]{:S(2)}) %collective-permute-start.5) | collective-permute-done | bytes 524320 | tf_op jit(solution)/shard_map/ppermute | solution.py:29
  60.8 1.6 line_sums.1
  64.3 8.2 %all-to-all-start = ((bf16[8,256,128]{2,1,0:T(8,128)(2,1)}), bf16[8,256,128]{2,1,0:T(8,128)(2,1)S(1)}, u32[]{:S(2)}, u32[]{:S(2)}) async-start(bf16[8,256,128]{2,1,0:T(8,128)(2,1)} %get-tuple-element.25), calls=%async_computation | async-start | bytes 1048576 | tf_op jit(solution)/shard_map/all_to_all | solution.py:306
  72.5 1.6 copy-done
  74.1 8.2 %out_terms.1 = (bf16[168,128,128]{2,1,0:T(8,128)(2,1)}, f32[8,128]{1,0:T(8,128)S(1)}) custom-call(s32[4]{0:T(128)S(1)} %pad_add_fusion.place, s32[2,84]{1,0:T(2,128)S(1)} %bitcast.24, bf16[256,10752]{1,0:T(8,128)(2,1)} %cot_ref.3, bf16[32,128,256]{2,1,0:T(8,128)(2,1)S(1)} %copy-done, bf16[32,128,256]{2,1,0:T(8,128)(2,1)S(1)} %collective-permute-done.7.other_ref), custom_call_target="tpu_custom_call" | custom-call | flops 3000000000 | bytes 16777216 | tf_op jit(solution)/shard_map/out_terms/pallas_call | solution.py:199
  82.9 7.5 %all-to-all-done = bf16[8,256,128]{2,1,0:T(8,128)(2,1)S(1)} async-done(((bf16[8,256,128]{2,1,0:T(8,128)(2,1)}), bf16[8,256,128]{2,1,0:T(8,128)(2,1)S(1)}, u32[]{:S(2)}, u32[]{:S(2)}) %all-to-all-start) | async-done | bytes 524320 | tf_op jit(solution)/shard_map/all_to_all | solution.py:306
  92.9 1.9 %collective-permute-start.17 = (bf16[96,128]{1,0:T(8,128)(2,1)S(1)}, bf16[96,128]{1,0:T(8,128)(2,1)S(1)}, u32[]{:S(2)}, u32[]{:S(2)}) collective-permute-start(bf16[96,128]{1,0:T(8,128)(2,1)S(1)} %copy-done.7), channel_id=1, source_target_pairs={{0,192},{4,196},{8,200},{12,204},{16,208},{20,212},{24,216},{28,22... | collective-permute-start | bytes 73736 | tf_op jit(solution)/shard_map/ppermute | solution.py:29
  95.8 3.2 %collective-permute-done.16 = bf16[96,128]{1,0:T(8,128)(2,1)S(1)} collective-permute-done((bf16[96,128]{1,0:T(8,128)(2,1)S(1)}, bf16[96,128]{1,0:T(8,128)(2,1)S(1)}, u32[]{:S(2)}, u32[]{:S(2)}) %collective-permute-start.16) | collective-permute-done | bytes 24608 | tf_op jit(solution)/shard_map/ppermute | solution.py:29
  100.0 3.7 %all-to-all-start.2 = ((bf16[8,4,96,128]{3,2,1,0:T(8,128)(2,1)}), bf16[8,4,96,128]{3,2,1,0:T(8,128)(2,1)S(1)}, u32[]{:S(2)}, u32[]{:S(2)}) async-start(bf16[8,4,96,128]{3,2,1,0:T(8,128)(2,1)} %broadcast_in_dim.17), calls=%async_computation.3 | async-start | bytes 1572864 | tf_op jit(solution)/shard_map/all_to_all | solution.py:321
  103.8 22.1 %all-to-all-done.2.refs_8_ = bf16[8,4,96,128]{3,2,1,0:T(8,128)(2,1)S(1)} async-done(((bf16[8,4,96,128]{3,2,1,0:T(8,128)(2,1)}), bf16[8,4,96,128]{3,2,1,0:T(8,128)(2,1)S(1)}, u32[]{:S(2)}, u32[]{:S(2)}) %all-to-all-start.2) | async-done | bytes 786464 | tf_op jit(solution)/shard_map/all_to_all | solution.py:321
  126.6 3.4 %all-to-all-start.1 = ((bf16[8,160,128]{2,1,0:T(8,128)(2,1)}), bf16[8,160,128]{2,1,0:T(8,128)(2,1)S(1)}, u32[]{:S(2)}, u32[]{:S(2)}) async-start(bf16[8,160,128]{2,1,0:T(8,128)(2,1)} %broadcast_in_dim.16), calls=%async_computation.2 | async-start | bytes 655360 | tf_op jit(solution)/shard_map/all_to_all | solution.py:318
  130.1 2.0 %collective-permute-start.18 = (bf16[8,4,96,128]{3,2,1,0:T(8,128)(2,1)S(1)}, bf16[8,4,96,128]{3,2,1,0:T(8,128)(2,1)S(1)}, u32[]{:S(2)}, u32[]{:S(2)}) collective-permute-start(bf16[8,4,96,128]{3,2,1,0:T(8,128)(2,1)S(1)} %all-to-all-done.2.refs_8_), channel_id=1, source_target_pairs={{0,4},{4,0},{8,12},{12,8},{16,20},{20,16},{24,28},{28,24},{32,36},... | collective-permute-start | bytes 2359304 | tf_op jit(solution)/shard_map/ppermute | solution.py:29
  132.1 9.0 %all-to-all-done.1.refs_0_ = bf16[8,160,128]{2,1,0:T(8,128)(2,1)S(1)} async-done(((bf16[8,160,128]{2,1,0:T(8,128)(2,1)}), bf16[8,160,128]{2,1,0:T(8,128)(2,1)S(1)}, u32[]{:S(2)}, u32[]{:S(2)}) %all-to-all-start.1) | async-done | bytes 327712 | tf_op jit(solution)/shard_map/all_to_all | solution.py:318
  142.8 4.2 %collective-permute-start.11 = (bf16[8,160,128]{2,1,0:T(8,128)(2,1)S(1)}, bf16[8,160,128]{2,1,0:T(8,128)(2,1)S(1)}, u32[]{:S(2)}, u32[]{:S(2)}) collective-permute-start(bf16[8,160,128]{2,1,0:T(8,128)(2,1)S(1)} %all-to-all-done.1.refs_0_), channel_id=1, source_target_pairs={{0,4},{4,0},{8,12},{12,8},{16,20},{20,16},{24,28},{28,24},{32,36},... | collective-permute-start | bytes 983048 | tf_op jit(solution)/shard_map/ppermute | solution.py:29
  147.0 7.7 %collective-permute-start.14 = (bf16[8,160,128]{2,1,0:T(8,128)(2,1)S(1)}, bf16[8,160,128]{2,1,0:T(8,128)(2,1)S(1)}, u32[]{:S(2)}, u32[]{:S(2)}) collective-permute-start(bf16[8,160,128]{2,1,0:T(8,128)(2,1)S(1)} %collective-permute-done.10.refs_3_), channel_id=1, source_target_pairs={{0,4},{4,0},{8,12},{12,8},{16,20},{20,16},{24,28},{28,24},{32,36},... | collective-permute-start | bytes 983048 | tf_op jit(solution)/shard_map/ppermute | solution.py:29
  154.7 2.7 %collective-permute-start.13 = (bf16[8,160,128]{2,1,0:T(8,128)(2,1)S(1)}, bf16[8,160,128]{2,1,0:T(8,128)(2,1)S(1)}, u32[]{:S(2)}, u32[]{:S(2)}) collective-permute-start(bf16[8,160,128]{2,1,0:T(8,128)(2,1)S(1)} %collective-permute-done.9.refs_2_), channel_id=1, source_target_pairs={{0,4},{4,0},{8,12},{12,8},{16,20},{20,16},{24,28},{28,24},{32,36},... | collective-permute-start | bytes 983048 | tf_op jit(solution)/shard_map/ppermute | solution.py:29
  157.4 2.4 %collective-permute-done.8.refs_1_ = bf16[8,160,128]{2,1,0:T(8,128)(2,1)S(1)} collective-permute-done((bf16[8,160,128]{2,1,0:T(8,128)(2,1)S(1)}, bf16[8,160,128]{2,1,0:T(8,128)(2,1)S(1)}, u32[]{:S(2)}, u32[]{:S(2)}) %collective-permute-start.8) | collective-permute-done | bytes 327712 | tf_op jit(solution)/shard_map/ppermute | solution.py:29
  160.8 1.2 collective-permute-done.12.refs_5_
  162.1 2.0 %in_terms.1 = (f32[7,128,128]{2,1,0:T(8,128)S(1)}, bf16[7,128,128]{2,1,0:T(8,128)(2,1)S(1)}, bf16[7,128,128]{2,1,0:T(8,128)(2,1)S(1)}, bf16[7,128,128]{2,1,0:T(8,128)(2,1)S(1)}) custom-call(s32[4]{0:T(128)S(1)} %pad_add_fusion.place, s32[4,7]{1,0:T(4,128)S(1)} %bitcast.22, bf16[256,896]{1,0:T(8,128)(2,1)S(1)} %copy-done.2, ...), custom_call_target="tpu_custom_call" | custom-call | flops 500000000 | bytes 8388608 | tf_op jit(solution)/shard_map/in_terms/pallas_call | solution.py:263
  164.1 3.0 %collective-permute-start.19 = (bf16[7,128,128]{2,1,0:T(8,128)(2,1)S(1)}, bf16[7,128,128]{2,1,0:T(8,128)(2,1)S(1)}, u32[]{:S(2)}, u32[]{:S(2)}) collective-permute-start(bf16[7,128,128]{2,1,0:T(8,128)(2,1)S(1)} %get-tuple-element.27), channel_id=1, source_target_pairs={{0,2},{1,3},{2,0},{3,1},{4,6},{5,7},{6,4},{7,5},{8,10},{9,11},{10,... | collective-permute-start | bytes 688136 | tf_op jit(solution)/shard_map/ppermute | solution.py:33
  167.5 2.3 %collective-permute-start.21 = (bf16[7,128,128]{2,1,0:T(8,128)(2,1)S(1)}, bf16[7,128,128]{2,1,0:T(8,128)(2,1)S(1)}, u32[]{:S(2)}, u32[]{:S(2)}) collective-permute-start(bf16[7,128,128]{2,1,0:T(8,128)(2,1)S(1)} %get-tuple-element.29), channel_id=1, source_target_pairs={{0,3},{1,0},{2,1},{3,2},{4,7},{5,4},{6,5},{7,6},{8,11},{9,8},{10,9... | collective-permute-start | bytes 688136 | tf_op jit(solution)/shard_map/ppermute | solution.py:33
  169.8 2.7 %collective-permute-done.19 = bf16[7,128,128]{2,1,0:T(8,128)(2,1)S(1)} collective-permute-done((bf16[7,128,128]{2,1,0:T(8,128)(2,1)S(1)}, bf16[7,128,128]{2,1,0:T(8,128)(2,1)S(1)}, u32[]{:S(2)}, u32[]{:S(2)}) %collective-permute-start.19) | collective-permute-done | bytes 229408 | tf_op jit(solution)/shard_map/ppermute | solution.py:33
  172.5 5.6 %collective-permute-done.20 = bf16[7,128,128]{2,1,0:T(8,128)(2,1)S(1)} collective-permute-done((bf16[7,128,128]{2,1,0:T(8,128)(2,1)S(1)}, bf16[7,128,128]{2,1,0:T(8,128)(2,1)S(1)}, u32[]{:S(2)}, u32[]{:S(2)}) %collective-permute-start.20) | collective-permute-done | bytes 229408 | tf_op jit(solution)/shard_map/ppermute | solution.py:33
  (61 shorter events, 15.5 us)
Async XLA Ops:
  7.2 55.9 %all-gather.3.cloned.1.call-start = ((), (), s32[]{:S(2)}) async-start(), calls=%async_computation.5 | async-start | bytes 2359296 | tf_op jit(solution)/shard_map/all_gather | solution.py:300
  8.1 6.3 %collective-permute-start.1 = (bf16[128,256]{0,1:T(8,128)(2,1)S(1)}, bf16[128,256]{0,1:T(8,128)(2,1)S(1)}, u32[]{:S(2)}, u32[]{:S(2)}) collective-permute-start(bf16[128,256]{0,1:T(8,128)(2,1)S(1)} %get-tuple-element.32), channel_id=1, source_target_pairs={{0,128},{4,132},{8,136},{12,140},{16,144},{20,148},{24,152},{28,15... | collective-permute-start | bytes 196616 | tf_op jit(solution)/shard_map/ppermute | solution.py:29
  11.8 5.0 %collective-permute-start = (bf16[128,256]{0,1:T(8,128)(2,1)S(1)}, bf16[128,256]{0,1:T(8,128)(2,1)S(1)}, u32[]{:S(2)}, u32[]{:S(2)}) collective-permute-start(bf16[128,256]{0,1:T(8,128)(2,1)S(1)} %get-tuple-element.32), channel_id=1, source_target_pairs={{0,64},{4,68},{8,72},{12,76},{16,80},{20,84},{24,88},{28,92},{32,9... | collective-permute-start | bytes 196616 | tf_op jit(solution)/shard_map/ppermute | solution.py:29
  12.1 4.7 %collective-permute-start.2 = (bf16[128,256]{0,1:T(8,128)(2,1)S(1)}, bf16[128,256]{0,1:T(8,128)(2,1)S(1)}, u32[]{:S(2)}, u32[]{:S(2)}) collective-permute-start(bf16[128,256]{0,1:T(8,128)(2,1)S(1)} %get-tuple-element.32), channel_id=1, source_target_pairs={{0,192},{4,196},{8,200},{12,204},{16,208},{20,212},{24,216},{28,22... | collective-permute-start | bytes 196616 | tf_op jit(solution)/shard_map/ppermute | solution.py:29
  27.0 5.3 %collective-permute-start.3 = (bf16[32,256,128]{2,1,0:T(8,128)(2,1)S(1)}, bf16[32,256,128]{2,1,0:T(8,128)(2,1)S(1)}, u32[]{:S(2)}, u32[]{:S(2)}) collective-permute-start(bf16[32,256,128]{2,1,0:T(8,128)(2,1)S(1)} %get-tuple-element.17), channel_id=1, source_target_pairs={{0,4},{4,0},{8,12},{12,8},{16,20},{20,16},{24,28},{28,24},{32,36},... | collective-permute-start | bytes 6291464 | tf_op jit(solution)/shard_map/ppermute | solution.py:29
  33.7 15.0 %collective-permute-start.4 = (bf16[8,256,128]{2,1,0:T(8,128)(2,1)S(1)}, bf16[8,256,128]{2,1,0:T(8,128)(2,1)S(1)}, u32[]{:S(2)}, u32[]{:S(2)}) collective-permute-start(bf16[8,256,128]{2,1,0:T(8,128)(2,1)S(1)} %get-tuple-element.19), channel_id=1, source_target_pairs={{0,64},{4,68},{8,72},{12,76},{16,80},{20,84},{24,88},{28,92},{32,9... | collective-permute-start | bytes 1572872 | tf_op jit(solution)/shard_map/ppermute | solution.py:29
  34.5 26.3 %collective-permute-start.5 = (bf16[8,256,128]{2,1,0:T(8,128)(2,1)S(1)}, bf16[8,256,128]{2,1,0:T(8,128)(2,1)S(1)}, u32[]{:S(2)}, u32[]{:S(2)}) collective-permute-start(bf16[8,256,128]{2,1,0:T(8,128)(2,1)S(1)} %get-tuple-element.20), channel_id=1, source_target_pairs={{0,128},{4,132},{8,136},{12,140},{16,144},{20,148},{24,152},{28,15... | collective-permute-start | bytes 1572872 | tf_op jit(solution)/shard_map/ppermute | solution.py:29
  37.9 22.9 %collective-permute-start.6 = (bf16[8,256,128]{2,1,0:T(8,128)(2,1)S(1)}, bf16[8,256,128]{2,1,0:T(8,128)(2,1)S(1)}, u32[]{:S(2)}, u32[]{:S(2)}) collective-permute-start(bf16[8,256,128]{2,1,0:T(8,128)(2,1)S(1)} %get-tuple-element.21), channel_id=1, source_target_pairs={{0,192},{4,196},{8,200},{12,204},{16,208},{20,212},{24,216},{28,22... | collective-permute-start | bytes 1572872 | tf_op jit(solution)/shard_map/ppermute | solution.py:29
  63.1 9.5 %copy-start.6 = (s32[84,2]{0,1:T(2,128)S(1)}, s32[84,2]{0,1:T(2,128)}, u32[]{:S(2)}) copy-start(s32[84,2]{0,1:T(2,128)} %param.10) | copy-start | bytes 2020
  63.1 9.5 %collective-permute-start.7 = (bf16[32,128,256]{2,1,0:T(8,128)(2,1)}, bf16[32,128,256]{2,1,0:T(8,128)(2,1)S(1)}, u32[]{:S(2)}, u32[]{:S(2)}) collective-permute-start(bf16[32,128,256]{2,1,0:T(8,128)(2,1)} %after.3.own_ref), channel_id=1, source_target_pairs={{0,4},{4,0},{8,12},{12,8},{16,20},{20,16},{24,28},{28,24},{32,36},... | collective-permute-start | bytes 6291464 | tf_op jit(solution)/shard_map/ppermute | solution.py:29
  64.3 26.2 %all-to-all-start = ((bf16[8,256,128]{2,1,0:T(8,128)(2,1)}), bf16[8,256,128]{2,1,0:T(8,128)(2,1)S(1)}, u32[]{:S(2)}, u32[]{:S(2)}) async-start(bf16[8,256,128]{2,1,0:T(8,128)(2,1)} %get-tuple-element.25), calls=%async_computation | async-start | bytes 1048576 | tf_op jit(solution)/shard_map/all_to_all | solution.py:306
  72.5 106.5 %reduce-scatter.2.cloned.1.call-start = ((), (), s32[]{:S(2)}) async-start(), calls=%async_computation.4 | async-start | bytes 6881280 | tf_op jit(solution)/shard_map/reduce_scatter | solution.py:314
  72.5 1.6 copy-start
  92.2 0.7 copy-start.7
  92.9 69.2 %copy-start.2 = (bf16[256,896]{1,0:T(8,128)(2,1)S(1)}, bf16[256,896]{1,0:T(8,128)(2,1)}, u32[]{:S(2)}) copy-start(bf16[256,896]{1,0:T(8,128)(2,1)} %enc_ref.1) | copy-start | bytes 1376260
  92.9 69.2 %copy-start.4 = (s32[7,4]{0,1:T(4,128)S(1)}, s32[7,4]{0,1:T(4,128)}, u32[]{:S(2)}) copy-start(s32[7,4]{0,1:T(4,128)} %param.11) | copy-start | bytes 340
  92.9 2.8 %collective-permute-start.17 = (bf16[96,128]{1,0:T(8,128)(2,1)S(1)}, bf16[96,128]{1,0:T(8,128)(2,1)S(1)}, u32[]{:S(2)}, u32[]{:S(2)}) collective-permute-start(bf16[96,128]{1,0:T(8,128)(2,1)S(1)} %copy-done.7), channel_id=1, source_target_pairs={{0,192},{4,196},{8,200},{12,204},{16,208},{20,212},{24,216},{28,22... | collective-permute-start | bytes 73736 | tf_op jit(solution)/shard_map/ppermute | solution.py:29
  94.8 4.2 %collective-permute-start.16 = (bf16[96,128]{1,0:T(8,128)(2,1)S(1)}, bf16[96,128]{1,0:T(8,128)(2,1)S(1)}, u32[]{:S(2)}, u32[]{:S(2)}) collective-permute-start(bf16[96,128]{1,0:T(8,128)(2,1)S(1)} %copy-done.7), channel_id=1, source_target_pairs={{0,128},{4,132},{8,136},{12,140},{16,144},{20,148},{24,152},{28,15... | collective-permute-start | bytes 73736 | tf_op jit(solution)/shard_map/ppermute | solution.py:29
  94.8 4.2 %collective-permute-start.15 = (bf16[96,128]{1,0:T(8,128)(2,1)S(1)}, bf16[96,128]{1,0:T(8,128)(2,1)S(1)}, u32[]{:S(2)}, u32[]{:S(2)}) collective-permute-start(bf16[96,128]{1,0:T(8,128)(2,1)S(1)} %copy-done.7), channel_id=1, source_target_pairs={{0,64},{4,68},{8,72},{12,76},{16,80},{20,84},{24,88},{28,92},{32,9... | collective-permute-start | bytes 73736 | tf_op jit(solution)/shard_map/ppermute | solution.py:29
  100.0 25.8 %all-to-all-start.2 = ((bf16[8,4,96,128]{3,2,1,0:T(8,128)(2,1)}), bf16[8,4,96,128]{3,2,1,0:T(8,128)(2,1)S(1)}, u32[]{:S(2)}, u32[]{:S(2)}) async-start(bf16[8,4,96,128]{3,2,1,0:T(8,128)(2,1)} %broadcast_in_dim.17), calls=%async_computation.3 | async-start | bytes 1572864 | tf_op jit(solution)/shard_map/all_to_all | solution.py:321
  126.6 14.4 %all-to-all-start.1 = ((bf16[8,160,128]{2,1,0:T(8,128)(2,1)}), bf16[8,160,128]{2,1,0:T(8,128)(2,1)S(1)}, u32[]{:S(2)}, u32[]{:S(2)}) async-start(bf16[8,160,128]{2,1,0:T(8,128)(2,1)} %broadcast_in_dim.16), calls=%async_computation.2 | async-start | bytes 655360 | tf_op jit(solution)/shard_map/all_to_all | solution.py:318
  130.1 32.0 %collective-permute-start.18 = (bf16[8,4,96,128]{3,2,1,0:T(8,128)(2,1)S(1)}, bf16[8,4,96,128]{3,2,1,0:T(8,128)(2,1)S(1)}, u32[]{:S(2)}, u32[]{:S(2)}) collective-permute-start(bf16[8,4,96,128]{3,2,1,0:T(8,128)(2,1)S(1)} %all-to-all-done.2.refs_8_), channel_id=1, source_target_pairs={{0,4},{4,0},{8,12},{12,8},{16,20},{20,16},{24,28},{28,24},{32,36},... | collective-permute-start | bytes 2359304 | tf_op jit(solution)/shard_map/ppermute | solution.py:29
  141.1 5.9 %collective-permute-start.10 = (bf16[8,160,128]{2,1,0:T(8,128)(2,1)S(1)}, bf16[8,160,128]{2,1,0:T(8,128)(2,1)S(1)}, u32[]{:S(2)}, u32[]{:S(2)}) collective-permute-start(bf16[8,160,128]{2,1,0:T(8,128)(2,1)S(1)} %all-to-all-done.1.refs_0_), channel_id=1, source_target_pairs={{0,192},{4,196},{8,200},{12,204},{16,208},{20,212},{24,216},{28,22... | collective-permute-start | bytes 983048 | tf_op jit(solution)/shard_map/ppermute | solution.py:29
  142.2 12.5 %collective-permute-start.9 = (bf16[8,160,128]{2,1,0:T(8,128)(2,1)S(1)}, bf16[8,160,128]{2,1,0:T(8,128)(2,1)S(1)}, u32[]{:S(2)}, u32[]{:S(2)}) collective-permute-start(bf16[8,160,128]{2,1,0:T(8,128)(2,1)S(1)} %all-to-all-done.1.refs_0_), channel_id=1, source_target_pairs={{0,128},{4,132},{8,136},{12,140},{16,144},{20,148},{24,152},{28,15... | collective-permute-start | bytes 983048 | tf_op jit(solution)/shard_map/ppermute | solution.py:29
  142.6 17.2 %collective-permute-start.8 = (bf16[8,160,128]{2,1,0:T(8,128)(2,1)S(1)}, bf16[8,160,128]{2,1,0:T(8,128)(2,1)S(1)}, u32[]{:S(2)}, u32[]{:S(2)}) collective-permute-start(bf16[8,160,128]{2,1,0:T(8,128)(2,1)S(1)} %all-to-all-done.1.refs_0_), channel_id=1, source_target_pairs={{0,64},{4,68},{8,72},{12,76},{16,80},{20,84},{24,88},{28,92},{32,9... | collective-permute-start | bytes 983048 | tf_op jit(solution)/shard_map/ppermute | solution.py:29
  142.8 18.1 %collective-permute-start.11 = (bf16[8,160,128]{2,1,0:T(8,128)(2,1)S(1)}, bf16[8,160,128]{2,1,0:T(8,128)(2,1)S(1)}, u32[]{:S(2)}, u32[]{:S(2)}) collective-permute-start(bf16[8,160,128]{2,1,0:T(8,128)(2,1)S(1)} %all-to-all-done.1.refs_0_), channel_id=1, source_target_pairs={{0,4},{4,0},{8,12},{12,8},{16,20},{20,16},{24,28},{28,24},{32,36},... | collective-permute-start | bytes 983048 | tf_op jit(solution)/shard_map/ppermute | solution.py:29
  147.0 13.8 %collective-permute-start.14 = (bf16[8,160,128]{2,1,0:T(8,128)(2,1)S(1)}, bf16[8,160,128]{2,1,0:T(8,128)(2,1)S(1)}, u32[]{:S(2)}, u32[]{:S(2)}) collective-permute-start(bf16[8,160,128]{2,1,0:T(8,128)(2,1)S(1)} %collective-permute-done.10.refs_3_), channel_id=1, source_target_pairs={{0,4},{4,0},{8,12},{12,8},{16,20},{20,16},{24,28},{28,24},{32,36},... | collective-permute-start | bytes 983048 | tf_op jit(solution)/shard_map/ppermute | solution.py:29
  154.7 6.1 %collective-permute-start.13 = (bf16[8,160,128]{2,1,0:T(8,128)(2,1)S(1)}, bf16[8,160,128]{2,1,0:T(8,128)(2,1)S(1)}, u32[]{:S(2)}, u32[]{:S(2)}) collective-permute-start(bf16[8,160,128]{2,1,0:T(8,128)(2,1)S(1)} %collective-permute-done.9.refs_2_), channel_id=1, source_target_pairs={{0,4},{4,0},{8,12},{12,8},{16,20},{20,16},{24,28},{28,24},{32,36},... | collective-permute-start | bytes 983048 | tf_op jit(solution)/shard_map/ppermute | solution.py:29
  159.8 2.3 %collective-permute-start.12 = (bf16[8,160,128]{2,1,0:T(8,128)(2,1)S(1)}, bf16[8,160,128]{2,1,0:T(8,128)(2,1)S(1)}, u32[]{:S(2)}, u32[]{:S(2)}) collective-permute-start(bf16[8,160,128]{2,1,0:T(8,128)(2,1)S(1)} %collective-permute-done.8.refs_1_), channel_id=1, source_target_pairs={{0,4},{4,0},{8,12},{12,8},{16,20},{20,16},{24,28},{28,24},{32,36},... | collective-permute-start | bytes 983048 | tf_op jit(solution)/shard_map/ppermute | solution.py:29
  164.1 8.4 %collective-permute-start.19 = (bf16[7,128,128]{2,1,0:T(8,128)(2,1)S(1)}, bf16[7,128,128]{2,1,0:T(8,128)(2,1)S(1)}, u32[]{:S(2)}, u32[]{:S(2)}) collective-permute-start(bf16[7,128,128]{2,1,0:T(8,128)(2,1)S(1)} %get-tuple-element.27), channel_id=1, source_target_pairs={{0,2},{1,3},{2,0},{3,1},{4,6},{5,7},{6,4},{7,5},{8,10},{9,11},{10,... | collective-permute-start | bytes 688136 | tf_op jit(solution)/shard_map/ppermute | solution.py:33
  167.1 11.0 %collective-permute-start.20 = (bf16[7,128,128]{2,1,0:T(8,128)(2,1)S(1)}, bf16[7,128,128]{2,1,0:T(8,128)(2,1)S(1)}, u32[]{:S(2)}, u32[]{:S(2)}) collective-permute-start(bf16[7,128,128]{2,1,0:T(8,128)(2,1)S(1)} %get-tuple-element.28), channel_id=1, source_target_pairs={{0,1},{1,2},{2,3},{3,0},{4,5},{5,6},{6,7},{7,4},{8,9},{9,10},{10,1... | collective-permute-start | bytes 688136 | tf_op jit(solution)/shard_map/ppermute | solution.py:33
  167.5 10.6 %collective-permute-start.21 = (bf16[7,128,128]{2,1,0:T(8,128)(2,1)S(1)}, bf16[7,128,128]{2,1,0:T(8,128)(2,1)S(1)}, u32[]{:S(2)}, u32[]{:S(2)}) collective-permute-start(bf16[7,128,128]{2,1,0:T(8,128)(2,1)S(1)} %get-tuple-element.29), channel_id=1, source_target_pairs={{0,3},{1,0},{2,1},{3,2},{4,7},{5,4},{6,5},{7,6},{8,11},{9,8},{10,9... | collective-permute-start | bytes 688136 | tf_op jit(solution)/shard_map/ppermute | solution.py:33
  (3 other events, 1.9 us)
Sparse Core Ops, SparseCore 0:
  17.9 41.2 all-gather.2
  92.3 55.4 reduce-scatter.1
